TPU v7x, 32 devices: a whole 2x2x4 slice. The times are simulated.
32 devices in a mesh: row: 4 (over z), col: 8 (over y, x, core).
Axes of the slice: x: 2, y: 2, z: 4, core: 2. Of those that a mesh axis runs over, the one named last changes fastest.
Arguments:
- profiles: bfloat16 [50, 16384], P(None, ('col', 'row')), may hold values from -1.1953125 to 1.1953125
- cell_width: bfloat16 [16384], P(('col', 'row')), may hold values from 1 to 3
- basis: bfloat16 [64, 16384], P(None, ('col', 'row')), may hold values from -6 to 6
- block_lists: int32 [4, 8, 2, 128], P('row', 'col'), may hold values from 0 to 31, as said below
- block_counts: int32 [4, 8], P('row', 'col'), may hold values from 8 to 128, as said below
- landmarks: int32 [8], replicated, may hold values from 0 to 127, as said below
Outputs:
- row_scaling: float32 [16384], P('row')
- column_scaling: float32 [16384], P('col')
- ritz_basis: float32 [64, 16384], P(None, ('row', 'col'))
Inputs may be any that keep to these rules, and one draw needn't show every extreme that they name: `block_lists`: in each tile the first block_counts slots name distinct blocks, row block below 32 and column block below 16; every block of the tile whose global row block and global column block differ by at most one is among them; later slots also name blocks of the tile. `block_counts`: A tile whose column cells lie among its own row cells has exactly 128 live slots. `landmarks`: Distinct, increasing, one in each aligned group of 16 consecutive blocks.
All inputs are finite; a program needn't handle non-finite values.
Results may differ from a plain program's by a relative error of at most 0.0057.
Values may be sent and summed in bfloat16 or wider, within the bound.
No kernel may reach another device: no remote copies, remote signals or barrier semaphores. Data moves between devices by JAX's collectives and lax.ppermute only.
A program may use at most 64 MiB of HBM per device.

v0:
```python
import functools

import jax
import jax.numpy as jnp
from jax import lax
from jax.experimental import pallas as pl
from jax.experimental.pallas import tpu as pltpu
from jax.sharding import PartitionSpec as P

BLK = 128
SWEEPS = 3
GROUP = 32
BUILD_GROUP = 16
TILE_GROUP = 16
ROWS, COLUMNS, COUNT = 0, 1, 2
FEAT = 64
PIECES = 16
SCALE = 512.0
LOG2E = 1.4426950408889634
F32 = jnp.float32
BF16 = jnp.bfloat16
MIB = 1 << 20
STRIP_TILES = 8

VMEM_SPEC = pl.BlockSpec(memory_space=pltpu.VMEM)
SMEM_SPEC = pl.BlockSpec(memory_space=pltpu.SMEM)


def split3(x):
    high = x.astype(BF16).astype(F32)
    mid = (x - high).astype(BF16).astype(F32)
    low = (x - high - mid).astype(BF16).astype(F32)
    return high, mid, low


def tree_sum(values):
    values = list(values)
    while len(values) > 1:
        values = [a + b for a, b in zip(values[::2], values[1::2])]
    return values[0]


def call(kernel, outs, ins, scratch=(), limit=24, flops=1 << 24):
    args, specs = [], []
    for kind, array in ins:
        if kind == "smem":
            specs.append(SMEM_SPEC)
        elif kind == "hbm":
            specs.append(pl.BlockSpec(memory_space=pltpu.HBM))
            array = pltpu.with_memory_space_constraint(array, pltpu.HBM)
        else:
            specs.append(VMEM_SPEC)
            if kind == "keep":
                array = pltpu.with_memory_space_constraint(array, pltpu.VMEM)
        args.append(array)
    return pl.pallas_call(
        kernel,
        out_shape=tuple(outs),
        in_specs=specs,
        out_specs=tuple(VMEM_SPEC for _ in outs),
        scratch_shapes=list(scratch),
        compiler_params=pltpu.CompilerParams(vmem_limit_bytes=limit * MIB),
        cost_estimate=pl.CostEstimate(flops=flops, bytes_accessed=1 << 20, transcendentals=0),
    )(*args)


def pack_kernel(prof_hbm, width_hbm, lists_hbm, counts, out_ref, *scratch):
    work, prof_ref, width_ref, lists_ref, sems = scratch
    pairs = [
        (prof_hbm, prof_ref),
        (width_hbm, width_ref),
        (lists_hbm, lists_ref),
    ]
    copies = [pltpu.make_async_copy(a, b, sems.at[i]) for i, (a, b) in enumerate(pairs)]
    for copy in copies:
        copy.start()
    for copy in copies:
        copy.wait()
    pcs = prof_ref.shape[0]
    prof = prof_ref[...].astype(F32)
    norm = jnp.sum(prof * prof, axis=0, keepdims=True)
    high, mid, low = split3(norm)
    work[...] = jnp.zeros_like(work)
    work[0:pcs, :] = prof
    work[pcs : pcs + 1, :] = high
    work[pcs + 1 : pcs + 2, :] = mid
    work[pcs + 2 : pcs + 3, :] = low
    work[pcs + 3 : pcs + 6, :] = jnp.ones((3, prof.shape[1]), F32)
    work[pcs + 6 : pcs + 7, :] = width_ref[...].astype(F32).reshape(1, -1)
    work[pcs + 8 : pcs + 10, 0:BLK] = lists_ref[0, 0].astype(F32)
    work[pcs + 10 : pcs + 11, 0:BLK] = jnp.full((1, BLK), counts[0, 0], jnp.int32).astype(F32)
    out_ref[...] = work[...].astype(BF16)


def places():
    return lax.axis_index("row"), lax.axis_index("col")


def stack_kernel(pcs, *refs):
    packs, (stack, table) = refs[:-2], refs[-2:]
    n = len(packs)
    me_row, _ = places()
    first = FEAT - 16
    for k, pack in enumerate(packs):
        stack[k] = pack[...]
        rows = pack[first:, 0:BLK].astype(F32)
        rows = pltpu.roll(rows, 16 - (pcs + 8 - first), 0)
        table[shifted(me_row, k, n)] = rows[0:8].astype(jnp.int32)


def slot_loop(step, count, size, group):
    def advance(number, carry):
        for i in range(0, group, size):
            step(*[number * group + i + j for j in range(size)])
        return carry

    lax.fori_loop(0, (count + group - 1) // group, advance, 0)


class Tile:
    def __init__(self, table, n_row, k, own, others):
        _, me_col = places()
        self.group = shifted(me_col // 2, k, n_row)
        self.table, self.k = table, k
        slots = own.shape[0]
        self.blocks, self.base = (own, 0) if k == 0 else (others, (k - 1) * slots)
        self.total = table[self.group * 8 + COUNT, 0]

    def row(self, s):
        return self.table[self.group * 8 + ROWS, s]

    def column(self, s):
        return self.table[self.group * 8 + COLUMNS, s]

    def block(self, s):
        return self.blocks[self.base + s]


def shifted(me, k, n):
    return lax.rem(me + (n - k), n)


def ordered_sum(stage, refs, me):
    n = len(refs)
    for k, ref in enumerate(refs):
        stage[shifted(me, k, n)] = ref[...]
    return tree_sum([stage[i] for i in range(n)])


def square(tile, slots):
    a, b, c, d = [tile.block(s) for s in slots]
    return jnp.concatenate(
        [jnp.concatenate([a, b], axis=1), jnp.concatenate([c, d], axis=1)], axis=0
    )


def add_rows(acc, sums, firsts, targets):
    for (row, lane), target in zip(firsts, targets):
        acc[target] += sums[row : row + 8, lane : lane + BLK]


def row_sums(tile, left, acc, row_blocks, spare):
    first = tile.group * row_blocks

    def step(*slots):
        low = [left[0, tile.column(s)] for s in slots[:2]]
        high = [left[1, tile.column(s)] for s in slots[2:]]
        sums = jnp.dot(
            jnp.concatenate(low + high, axis=0),
            square(tile, slots),
            preferred_element_type=F32,
        )
        firsts = [(0, 0), (PIECES, BLK), (2 * PIECES, 0), (3 * PIECES, BLK)]
        targets = [jnp.where(s < tile.total, first + tile.row(s), spare) for s in slots]
        add_rows(acc, sums, firsts, targets)

    slot_loop(step, tile.total, 4, GROUP)


def col_sums(tile, left, acc, row_blocks, spare):
    first = tile.group * row_blocks

    def step(*slots):
        if left is None:
            rows = lax.broadcasted_iota(jnp.int32, (4 * PIECES, 2 * BLK), 0)
            lanes = lax.broadcasted_iota(jnp.int32, (4 * PIECES, 2 * BLK), 1)
            block = rows // PIECES
            pieces = (rows % PIECES == 0) & (block % 2 == lanes // BLK)
            pieces = pieces.astype(F32).astype(BF16)
        else:
            pieces = [left[i % 2, first + tile.row(s)] for i, s in enumerate(slots)]
            pieces = jnp.concatenate(pieces, axis=0)
        sums = lax.dot_general(
            pieces,
            square(tile, slots),
            (((1,), (1,)), ((), ())),
            preferred_element_type=F32,
        )
        firsts = [(0, 0), (PIECES, 0), (2 * PIECES, BLK), (3 * PIECES, BLK)]
        targets = [jnp.where(s < tile.total, tile.column(s), spare) for s in slots]
        add_rows(acc, sums, firsts, targets)

    slot_loop(step, tile.total, 4, GROUP)


def fill_pieces(left, scaling):
    high, mid, low = split3(scaling)
    shape = (PIECES, BLK)
    rows = lax.broadcasted_iota(jnp.int32, shape, 0)
    empty = jnp.zeros(shape, F32).astype(BF16)
    for b in range(scaling.shape[0]):
        value = jnp.where(
            rows == 0,
            jnp.broadcast_to(high[b : b + 1], shape),
            jnp.where(
                rows == 1,
                jnp.broadcast_to(mid[b : b + 1], shape),
                jnp.where(rows == 2, jnp.broadcast_to(low[b : b + 1], shape), 0.0),
            ),
        ).astype(BF16)
        left[0, b] = jnp.concatenate([value, empty], axis=1)
        left[1, b] = jnp.concatenate([empty, value], axis=1)


def build(tile, offset, row_prof, row_inv, col_prof, col_inv):
    def step(s):
        row, column = offset + tile.row(s), tile.column(s)
        distance = jnp.dot(col_prof[column], row_prof[row], preferred_element_type=F32)
        block = jnp.exp2(distance * col_inv[column] * row_inv[row][0:1, :])
        tile.blocks[tile.base + s] = block.astype(BF16)

    slot_loop(step, tile.total, 1, BUILD_GROUP)


def fill_rows(pcs, stacks, row_prof, row_inv, offset):
    me_row, me_col = places()
    n_row = stacks[0].shape[0]
    per = stacks[0].shape[2] // BLK
    for i, stack in enumerate(stacks):
        core = lax.rem(me_col + i, 2)
        for k in range(n_row):
            piece = core * n_row + shifted(me_row, k, n_row)
            for j in range(per):
                block = stack[k, :, j * BLK : (j + 1) * BLK]
                row_prof[offset + piece * per + j] = block
                width = block.astype(F32)[pcs + 6 : pcs + 7, :]
                row_inv[offset + piece * per + j] = jnp.broadcast_to(1.0 / width, (8, BLK))


def own_kernel(
    pcs, table, stack, other, tile, col_prof, col_inv, sums, row_prof, row_inv, acc
):
    n_row = stack.shape[0]
    per = stack.shape[2] // BLK
    me_row, _ = places()
    fill_rows(pcs, [stack, other], row_prof, row_inv, 0)
    rows = lax.broadcasted_iota(jnp.int32, (FEAT, BLK), 0)
    for k in range(n_row):
        piece = shifted(me_row, k, n_row)
        for j in range(per):
            block = stack[k, :, j * BLK : (j + 1) * BLK].astype(F32)
            turned = jnp.where(rows < pcs, -2.0 * block, 0.0)
            turned = jnp.where((rows >= pcs) & (rows < pcs + 3), 1.0, turned)
            turned = jnp.where(
                (rows >= pcs + 3) & (rows < pcs + 6), pltpu.roll(block, 3, 0), turned
            )
            turned = jnp.where(rows == pcs + 7, pltpu.roll(block, 1, 0), turned)
            turned = turned.T
            col_prof[piece * per + j] = turned.astype(BF16)
            col_inv[piece * per + j] = jnp.broadcast_to(
                -LOG2E / turned[:, pcs + 7 : pcs + 8], (BLK, BLK)
            )
    own = Tile(table, n_row, 0, tile, None)
    build(own, 0, row_prof, row_inv, col_prof, col_inv)
    sums[...] = column_totals([own], None, acc, row_prof.shape[0])


def column_totals(tiles, left, acc, row_blocks):
    col_blocks = acc.shape[0] - 1
    acc[...] = jnp.zeros_like(acc)
    for tile in tiles:
        col_sums(tile, left, acc, row_blocks, col_blocks)
    return jnp.sum(acc[0:col_blocks], axis=1)


def row_part(tiles, left, acc, row_blocks, out):
    blocks = acc.shape[0] - 1
    acc[...] = jnp.zeros_like(acc)
    for tile in tiles:
        row_sums(tile, left, acc, row_blocks, blocks)
    out[...] = jnp.sum(acc[0:blocks], axis=1)


def strip_kernel(pcs, n_row, *refs):
    table, own, col_prof, col_inv, own_sums = refs[:5]
    stacks = refs[5 : 5 + 2 * n_row - 2]
    others, out, row_prof, row_inv, left, row_acc, col_acc = refs[-7:]
    row_blocks = row_prof.shape[0] // (n_row - 1)
    tiles = [Tile(table, n_row, k, own, others) for k in range(n_row)]
    for k in range(1, n_row):
        first = (k - 1) * row_blocks
        fill_rows(pcs, stacks[2 * k - 2 : 2 * k], row_prof, row_inv, first)
    for k in range(1, n_row):
        first = (k - 1) * row_blocks
        build(tiles[k], first, row_prof, row_inv, col_prof, col_inv)
    totals = column_totals(tiles[1:], None, col_acc, row_blocks) + own_sums[...]
    fill_pieces(left, SCALE / totals)
    row_part(tiles, left, row_acc, row_blocks, out)


def row_scalings(stage, parts):
    for k, part in enumerate(parts):
        stage[shifted(places()[1] // 2, k, len(parts))] = part[...].astype(F32)
    return SCALE / tree_sum([stage[i] for i in range(len(parts))])


def sweep_kernel(n_row, n_chip, *refs):
    table, own, others = refs[:3]
    parts = refs[3 : 3 + n_chip]
    out, stage, row_left, left, row_acc, col_acc = refs[-6:]
    row_blocks = out.shape[0] // n_row
    tiles = [Tile(table, n_row, k, own, others) for k in range(n_row)]
    fill_pieces(row_left, row_scalings(stage, parts))
    totals = column_totals(tiles, row_left, col_acc, row_blocks)
    fill_pieces(left, SCALE / totals)
    row_part(tiles, left, row_acc, row_blocks, out)


def pieces_of(value):
    return [v.astype(BF16) for v in split3(value)]


def last_kernel(n_row, n_chip, n_land, *refs):
    table, marks, own, others = refs[:4]
    parts, bases = refs[4 : 4 + n_chip], refs[4 + n_chip : 4 + n_chip + n_row]
    keep, away, both, scaling_out, stage, row_left, col_acc, scaled, acc = refs[-9:]
    cols = bases[0].shape[0]
    per = bases[0].shape[1] // BLK
    blocks = 2 * n_chip * per
    me_row, me_col = places()
    tiles = [Tile(table, n_row, k, own, others) for k in range(n_row)]
    fill_pieces(row_left, row_scalings(stage, parts))
    scaling = SCALE / column_totals(tiles, row_left, col_acc, blocks)
    scaling_out[...] = scaling
    for k in range(n_row):
        piece = shifted(me_row, k, n_row)
        for j in range(per):
            block = bases[k][:, j * BLK : (j + 1) * BLK].astype(F32)
            b = piece * per + j
            scaled[b, 0:cols] = (block * scaling_out[pl.ds(b, 1), :]).astype(BF16)
    high, mid, low = split3(scaling)
    shape = (PIECES, BLK)
    rows = lax.broadcasted_iota(jnp.int32, shape, 0)
    for b in range(scaling.shape[0]):
        value = jnp.where(
            rows == 0,
            jnp.broadcast_to(high[b : b + 1], shape),
            jnp.where(
                rows == 1,
                jnp.broadcast_to(mid[b : b + 1], shape),
                jnp.where(rows == 2, jnp.broadcast_to(low[b : b + 1], shape), 0.0),
            ),
        )
        scaled[b, cols : cols + PIECES] = value.astype(BF16)
    acc[...] = jnp.zeros_like(acc)
    for k in range(n_row):
        tile = tiles[k]

        def step(s, tile=tile):
            target = jnp.where(s < tile.total, tile.row(s), blocks)
            sums = jnp.dot(scaled[tile.column(s)], tile.block(s), preferred_element_type=F32)
            acc[target] += sums[0 : cols + 8]

        slot_loop(step, jnp.where(tile.group == me_row, tile.total, 0), 1, BUILD_GROUP)
    core = lax.rem(me_col, 2)
    for q in range(n_chip):
        mine = (2 * q + core) * per
        other = (2 * q + 1 - core) * per
        for j in range(per):
            keep[q, j] = acc[mine + j, 0:cols]
            away[q, j] = acc[other + j, 0:cols].astype(BF16)
    part = jnp.sum(acc[0:blocks, cols : cols + 8], axis=1)
    for i, value in enumerate(pieces_of(part)):
        both[i * blocks : (i + 1) * blocks] = value
    for i in range(n_land):
        first = 3 * blocks + i * cols
        both[first : first + cols] = acc[marks[me_row * n_land + i] - me_row * blocks, 0:cols].astype(BF16)


def three(ref, blocks):
    value = ref[0 : 3 * blocks].astype(F32)
    return (value[2 * blocks :] + value[blocks : 2 * blocks]) + value[0:blocks]


def pair_kernel(keep, away, both, both_in, both_out, *outs):
    n_chip, per, cols = keep.shape[:3]
    blocks = 2 * n_chip * per
    chip = places()[1] // 2
    parts = pieces_of(three(both, blocks) + three(both_in, blocks))
    for i, value in enumerate(parts):
        both_out[i * blocks : (i + 1) * blocks] = value
    lands = both[3 * blocks :].astype(F32) + both_in[3 * blocks :].astype(F32)
    both_out[3 * blocks :] = lands.astype(BF16)
    for k, out in enumerate(outs):
        to = lax.rem(chip + k, n_chip)
        for j in range(per):
            value = keep[to, j] + away[to, j].astype(F32)
            out[j * cols : (j + 1) * cols] = value.astype(BF16)


def gram_kernel(n_land, cols, per, *refs):
    marks = refs[0]
    gram, scaling_out, own, inverse, stage, land_stage = refs[-6:]
    parts = refs[1:-6]
    n = len(parts)
    me_row, me_col = places()
    blocks = scaling_out.shape[0]
    for k, part in enumerate(parts):
        place = shifted(me_col // 2, k, n)
        stage[place] = three(part, blocks)
        land_stage[place] = part[3 * blocks :]
    inverse[...] = 1.0 / tree_sum([stage[i] for i in range(n)])
    scaling_out[...] = SCALE * inverse[...]
    for j in range(per):
        own[j : j + 1, :] = inverse[pl.ds(me_col * per + j, 1), :]
    total = None
    for i in range(n_land):
        summed = tree_sum(
            [land_stage[k, i * cols : (i + 1) * cols].astype(F32) for k in range(n)]
        )
        block = marks[me_row * n_land + i] - me_row * blocks
        projected = summed * inverse[pl.ds(block, 1), :]
        product = lax.dot_general(
            projected,
            projected,
            (((1,), (1,)), ((), ())),
            precision=lax.Precision.HIGHEST,
            preferred_element_type=F32,
        )
        total = product if total is None else total + product
    gram[...] = total


WIDE = 4


def eliminate(gram):
    cols = gram.shape[0]
    rows = lax.broadcasted_iota(jnp.int32, (cols, 2 * cols), 0)
    lanes = lax.broadcasted_iota(jnp.int32, (cols, 2 * cols), 1)
    unit = (rows[:, :cols] == lanes[:, :cols]).astype(F32)
    work = jnp.concatenate([gram, unit], axis=1)
    for first in range(0, cols, WIDE):
        tops = [work[first + i : first + i + 1, :] for i in range(WIDE)]
        sides = [
            jnp.broadcast_to(work[:, first + i : first + i + 1], work.shape)
            for i in range(WIDE)
        ]
        change = None
        for i in range(WIDE):
            pivot = first + i
            unit_top = tops[i] / sides[i][pivot : pivot + 1, :]
            for m in range(i + 1, WIDE):
                factor = sides[i][first + m : first + m + 1, :]
                tops[m] = tops[m] - factor * unit_top
                inner = factor / sides[i][pivot : pivot + 1, :]
                sides[m] = sides[m] - sides[i] * inner
            term = sides[i] * unit_top
            change = term if change is None else change + term
        reduced = work - change
        kept = work
        for i in range(WIDE):
            kept = jnp.where(rows == first + i, tops[i], kept)
        work = jnp.where(rows >= first + WIDE, reduced, kept)
    pivots = jnp.sum(jnp.where(rows == lanes, work, 0.0), axis=1, keepdims=True)
    return (work * lax.rsqrt(pivots))[:, cols:]


def ritz_kernel(n_row, cells, *refs):
    grams, parts = refs[:n_row], refs[n_row:-3]
    own, out, stage = refs[-3:]
    cols = grams[0].shape[0]
    per = out.shape[1] // BLK
    inverse = eliminate(ordered_sum(stage, grams, places()[0]) * (1.0 / cells))
    for j in range(per):
        summed = tree_sum([m[j * cols : (j + 1) * cols].astype(F32) for m in parts])
        projected = summed * own[j : j + 1, :]
        out[:, j * BLK : (j + 1) * BLK] = jnp.dot(
            inverse, projected, precision=lax.Precision.HIGHEST, preferred_element_type=F32
        )


def swap(x, axis, k):
    return lax.ppermute(x, axis, [(i, i ^ k) for i in range(lax.axis_size(axis))])


def shift(x, axis, k):
    n = lax.axis_size(axis)
    return lax.ppermute(x, axis, [(i, (i + k) % n) for i in range(n)])


def shifts(x, axis):
    return [x] + [shift(x, axis, k) for k in range(1, lax.axis_size(axis))]


def chip_shift(x, k):
    n = lax.axis_size("col") // 2
    return lax.ppermute(
        x,
        "col",
        [(2 * q + p, 2 * ((q + k) % n) + p) for q in range(n) for p in range(2)],
    )


def chip_shifts(x):
    return [x] + [chip_shift(x, k) for k in range(1, lax.axis_size("col") // 2)]


def sibling(x):
    return swap(x, "col", 1)


def vec(*arrays):
    return [("vmem", a) for a in arrays]


def strip_body(profiles, cell_width, basis, block_lists, block_counts, landmarks):
    n_row, n_col = lax.axis_size("row"), lax.axis_size("col")
    n_chip = n_col // 2
    pcs, share = profiles.shape
    cols = basis.shape[0]
    per = share // BLK
    row_blocks, col_blocks = n_col * per, n_row * per
    all_rows = n_row * row_blocks
    slots = block_lists.shape[-1]
    n_land = landmarks.shape[0] // n_row

    def shape(*dims, dtype=F32):
        return jax.ShapeDtypeStruct(dims, dtype)

    (packed,) = call(
        pack_kernel,
        [shape(FEAT, share, dtype=BF16)],
        [("hbm", a) for a in (profiles, cell_width, block_lists)] + [("smem", block_counts)],
        [
            pltpu.VMEM((FEAT, share), F32),
            pltpu.VMEM(profiles.shape, BF16),
            pltpu.VMEM(cell_width.shape, BF16),
            pltpu.VMEM(block_lists.shape, jnp.int32),
            pltpu.SemaphoreType.DMA((3,)),
        ],
    )
    stack, table = call(
        functools.partial(stack_kernel, pcs),
        [shape(n_row, FEAT, share, dtype=BF16), shape(n_row, 8, BLK, dtype=jnp.int32)],
        vec(*shifts(packed, "row")),
    )
    table = ("smem", table.reshape(n_row * 8, BLK))
    marks = ("smem", landmarks)
    far = [chip_shift(stack, k) for k in range(1, n_chip)]
    bases = shifts(basis, "row")
    own, col_prof, col_inv, sums = call(
        functools.partial(own_kernel, pcs),
        [
            pltpu.VMEM((slots, BLK, BLK), BF16),
            pltpu.VMEM((col_blocks, BLK, FEAT), BF16),
            pltpu.VMEM((col_blocks, BLK, BLK), F32),
            shape(col_blocks, BLK),
        ],
        [table] + vec(stack, sibling(stack)),
        [
            pltpu.VMEM((row_blocks, FEAT, BLK), BF16),
            pltpu.VMEM((row_blocks, 8, BLK), F32),
            pltpu.VMEM((col_blocks + 1, 8, BLK), F32),
        ],
    )
    far, sums, bases = lax.optimization_barrier((far, sums, bases))
    stacks = [x for pack in far for x in (pack, sibling(pack))]
    far_slots = (n_row - 1) * slots
    others, part = call(
        functools.partial(strip_kernel, pcs, n_row),
        [pltpu.VMEM((far_slots, BLK, BLK), BF16), shape(all_rows, BLK)],
        [table, ("keep", own), ("keep", col_prof), ("keep", col_inv)]
        + vec(sums, *stacks),
        [
            pltpu.VMEM((all_rows - row_blocks, FEAT, BLK), BF16),
            pltpu.VMEM((all_rows - row_blocks, 8, BLK), F32),
            pltpu.VMEM((2, col_blocks, PIECES, 2 * BLK), BF16),
            pltpu.VMEM((all_rows + 1, 8, BLK), F32),
            pltpu.VMEM((col_blocks + 1, 8, BLK), F32),
        ],
    )
    tiles = [("keep", own), ("keep", others)]

    def chip_parts(part):
        return chip_shifts((part + sibling(part)).astype(BF16))

    for _ in range(SWEEPS - 2):
        (part,) = call(
            functools.partial(sweep_kernel, n_row, n_chip),
            [shape(all_rows, BLK)],
            [table] + tiles + vec(*chip_parts(part)),
            [
                pltpu.VMEM((n_chip, all_rows, BLK), F32),
                pltpu.VMEM((2, all_rows, PIECES, 2 * BLK), BF16),
                pltpu.VMEM((2, col_blocks, PIECES, 2 * BLK), BF16),
                pltpu.VMEM((all_rows + 1, 8, BLK), F32),
                pltpu.VMEM((col_blocks + 1, 8, BLK), F32),
            ],
        )
    both_rows = 3 * row_blocks + n_land * cols
    keep, away, both, col_scaling = call(
        functools.partial(last_kernel, n_row, n_chip, n_land),
        [
            shape(n_chip, per, cols, BLK),
            shape(n_chip, per, cols, BLK, dtype=BF16),
            shape(both_rows, BLK, dtype=BF16),
            shape(col_blocks, BLK),
        ],
        [table, marks] + tiles + vec(*chip_parts(part), *bases),
        [
            pltpu.VMEM((n_chip, all_rows, BLK), F32),
            pltpu.VMEM((2, all_rows, PIECES, 2 * BLK), BF16),
            pltpu.VMEM((col_blocks + 1, 8, BLK), F32),
            pltpu.VMEM((col_blocks, cols + PIECES, BLK), BF16),
            pltpu.VMEM((row_blocks + 1, cols + 8, BLK), F32),
        ],
    )
    pairs = call(
        pair_kernel,
        [shape(both_rows, BLK, dtype=BF16)]
        + [shape(per * cols, BLK, dtype=BF16)] * n_chip,
        vec(keep, sibling(away), both, sibling(both)),
    )
    sums = [pairs[0]] + [chip_shift(pairs[0], k) for k in range(1, n_chip)]
    shares = [pairs[1]] + [chip_shift(pairs[1 + k], k) for k in range(1, n_chip)]
    gram, row_scaling, own = call(
        functools.partial(gram_kernel, n_land, cols, per),
        [shape(cols, cols), shape(row_blocks, BLK), shape(per, BLK)],
        [marks] + vec(*sums),
        [
            pltpu.VMEM((row_blocks, BLK), F32),
            pltpu.VMEM((n_chip, row_blocks, BLK), F32),
            pltpu.VMEM((n_chip, n_land * cols, BLK), BF16),
        ],
    )
    (ritz,) = call(
        functools.partial(ritz_kernel, n_row, landmarks.shape[0] * BLK),
        [shape(cols, share)],
        vec(*shifts(gram, "row"), *shares, own),
        [pltpu.VMEM((n_row, cols, cols), F32)],
    )
    return row_scaling.reshape(-1), col_scaling.reshape(-1), ritz


def tile_pack_kernel(prof_ref, width_ref, out_ref, work):
    pcs = prof_ref.shape[0]
    prof = prof_ref[...].astype(F32)
    norm = jnp.sum(prof * prof, axis=0, keepdims=True)
    high, mid, low = split3(norm)
    work[...] = jnp.zeros_like(work)
    work[0:pcs, :] = prof
    work[pcs : pcs + 1, :] = high
    work[pcs + 1 : pcs + 2, :] = mid
    work[pcs + 2 : pcs + 3, :] = low
    work[pcs + 3 : pcs + 6, :] = jnp.ones((3, prof.shape[1]), F32)
    work[pcs + 6 : pcs + 7, :] = width_ref[...].astype(F32)
    out_ref[...] = work[...].astype(BF16)


def tile_square(tile, slots):
    a, b, c, d = [tile[s] for s in slots]
    return jnp.concatenate(
        [jnp.concatenate([a, b], axis=1), jnp.concatenate([c, d], axis=1)], axis=0
    )


def tile_add_rows(acc, lists, target, slots, sums, total, spare, firsts):
    for i, (s, (row, lane)) in enumerate(zip(slots, firsts)):
        place = jnp.where(s < total, lists[0, 0, target, s], spare)
        acc[place] += sums[row : row + 8, lane : lane + BLK]


def tile_row_sums(lists, tile, left, acc, total, spare):
    def step(*slots):
        low = [left[0, lists[0, 0, 1, s]] for s in slots[:2]]
        high = [left[1, lists[0, 0, 1, s]] for s in slots[2:]]
        sums = jnp.dot(
            jnp.concatenate(low + high, axis=0),
            tile_square(tile, slots),
            preferred_element_type=F32,
        )
        firsts = [(0, 0), (PIECES, BLK), (2 * PIECES, 0), (3 * PIECES, BLK)]
        tile_add_rows(acc, lists, 0, slots, sums, total, spare, firsts)

    slot_loop(step, total, 4, 4 * TILE_GROUP)


def tile_col_sums(lists, tile, left, acc, total, spare):
    def step(*slots):
        pieces = [left[i % 2, lists[0, 0, 0, s]] for i, s in enumerate(slots)]
        sums = lax.dot_general(
            jnp.concatenate(pieces, axis=0),
            tile_square(tile, slots),
            (((1,), (1,)), ((), ())),
            preferred_element_type=F32,
        )
        firsts = [(0, 0), (PIECES, 0), (2 * PIECES, BLK), (3 * PIECES, BLK)]
        tile_add_rows(acc, lists, 1, slots, sums, total, spare, firsts)

    slot_loop(step, total, 4, 4 * TILE_GROUP)


def tile_build_kernel(pcs, n_row, n_col, *refs):
    lists, counts = refs[:2]
    col_in = refs[2 : 2 + n_row]
    row_in = refs[2 + n_row : 2 + n_row + n_col]
    tile, part, row_prof, row_inv, col_prof, col_inv, acc, left = refs[2 + n_row + n_col :]
    per = row_in[0].shape[1] // BLK
    col_blocks, row_blocks = n_row * per, n_col * per
    total = counts[0, 0]
    me_row, me_col = places()
    for k, ref in enumerate(row_in):
        core = lax.rem(me_col + k, 2)
        piece = shifted(me_col // 2, k // 2, n_col // 2) * 2 + core
        for j in range(per):
            block = ref[:, j * BLK : (j + 1) * BLK]
            row_prof[piece * per + j] = block
            width = block.astype(F32)[pcs + 6 : pcs + 7, :]
            row_inv[piece * per + j] = jnp.broadcast_to(1.0 / width, (8, BLK))
    rows = lax.broadcasted_iota(jnp.int32, (FEAT, BLK), 0)
    for k, ref in enumerate(col_in):
        piece = shifted(me_row, k, n_row)
        for j in range(per):
            block = ref[0:FEAT, j * BLK : (j + 1) * BLK].astype(F32)
            turned = jnp.where(rows < pcs, -2.0 * block, 0.0)
            turned = jnp.where((rows >= pcs) & (rows < pcs + 3), 1.0, turned)
            turned = jnp.where(
                (rows >= pcs + 3) & (rows < pcs + 6), pltpu.roll(block, 3, 0), turned
            )
            turned = jnp.where(rows == pcs + 7, pltpu.roll(block, 1, 0), turned)
            turned = turned.T
            col_prof[piece * per + j] = turned.astype(BF16)
            col_inv[piece * per + j] = jnp.broadcast_to(
                -LOG2E / turned[:, pcs + 7 : pcs + 8], (BLK, BLK)
            )

    def step(s):
        rb, cb = lists[0, 0, 0, s], lists[0, 0, 1, s]
        distance = jnp.dot(col_prof[cb], row_prof[rb], preferred_element_type=F32)
        block = jnp.exp2(distance * col_inv[cb] * row_inv[rb][0:1, :])
        tile[s] = block.astype(BF16)

    slot_loop(step, total, 1, TILE_GROUP)
    ones = (lax.broadcasted_iota(jnp.int32, (PIECES, BLK), 0) == 0).astype(F32).astype(BF16)
    empty = jnp.zeros_like(ones)
    for b in range(row_blocks):
        left[0, b] = jnp.concatenate([ones, empty], axis=1)
        left[1, b] = jnp.concatenate([empty, ones], axis=1)
    acc[...] = jnp.zeros_like(acc)
    tile_col_sums(lists, tile, left, acc, total, col_blocks)
    part[...] = jnp.sum(acc[0:col_blocks], axis=1)


def tile_pass_kernel(over_rows, n_parts, *refs):
    lists, counts, tile = refs[:3]
    parts = refs[3 : 3 + n_parts]
    out, stage, left, acc = refs[-4:]
    total = counts[0, 0]
    blocks = out.shape[0]
    me_row, me_col = places()
    scaling = SCALE / ordered_sum(stage, parts, me_row if over_rows else me_col // 2)
    fill_pieces(left, scaling)
    acc[...] = jnp.zeros_like(acc)
    (tile_row_sums if over_rows else tile_col_sums)(lists, tile, left, acc, total, blocks)
    out[...] = jnp.sum(acc[0:blocks], axis=1)


def tile_last_kernel(n_row, n_col, n_land, *refs):
    lists, counts, marks, tile = refs[:4]
    parts, bases = refs[4 : 4 + n_row], refs[4 + n_row : 4 + 2 * n_row]
    keep, away, both, scaling_out, stage, scaled, acc = refs[4 + 2 * n_row :]
    cols = bases[0].shape[0]
    per = bases[0].shape[1] // BLK
    blocks = n_col * per
    total = counts[0, 0]
    me_row, me_col = places()
    scaling = SCALE / ordered_sum(stage, parts, me_row)
    scaling_out[...] = scaling
    for k in range(n_row):
        piece = shifted(me_row, k, n_row)
        for j in range(per):
            block = bases[k][:, j * BLK : (j + 1) * BLK].astype(F32)
            b = piece * per + j
            scaled[b, 0:cols] = (block * scaling_out[pl.ds(b, 1), :]).astype(BF16)
    high, mid, low = split3(scaling)
    shape = (PIECES, BLK)
    rows = lax.broadcasted_iota(jnp.int32, shape, 0)
    for b in range(scaling.shape[0]):
        value = jnp.where(
            rows == 0,
            jnp.broadcast_to(high[b : b + 1], shape),
            jnp.where(
                rows == 1,
                jnp.broadcast_to(mid[b : b + 1], shape),
                jnp.where(rows == 2, jnp.broadcast_to(low[b : b + 1], shape), 0.0),
            ),
        )
        scaled[b, cols : cols + PIECES] = value.astype(BF16)
    acc[...] = jnp.zeros_like(acc)

    def step(s):
        target = jnp.where(s < total, lists[0, 0, 0, s], blocks)
        sums = jnp.dot(scaled[lists[0, 0, 1, s]], tile[s], preferred_element_type=F32)
        acc[target] += sums[0 : cols + 8]

    slot_loop(step, total, 1, TILE_GROUP)
    core = lax.rem(me_col, 2)
    for q in range(n_col // 2):
        own = (2 * q + core) * per
        other = (2 * q + 1 - core) * per
        for j in range(per):
            keep[q, j] = acc[own + j, 0:cols]
            away[q, j] = acc[other + j, 0:cols].astype(BF16)
    row_part = jnp.sum(acc[0:blocks, cols : cols + 8], axis=1)
    for i, value in enumerate(pieces_of(row_part)):
        both[i * blocks : (i + 1) * blocks] = value
    for i in range(n_land):
        first = 3 * blocks + i * cols
        both[first : first + cols] = acc[marks[me_row * n_land + i] - me_row * blocks, 0:cols].astype(BF16)


def tile_body(profiles, cell_width, basis, block_lists, block_counts, landmarks):
    n_row, n_col = lax.axis_size("row"), lax.axis_size("col")
    n_chip = n_col // 2
    pcs, share = profiles.shape
    cols = basis.shape[0]
    per = share // BLK
    row_blocks, col_blocks = n_col * per, n_row * per
    slots = block_lists.shape[-1]
    n_land = landmarks.shape[0] // n_row

    def shape(*dims, dtype=F32):
        return jax.ShapeDtypeStruct(dims, dtype)

    (packed,) = call(
        tile_pack_kernel,
        [shape(FEAT, share, dtype=BF16)],
        vec(profiles, cell_width.reshape(1, share)),
        [pltpu.VMEM((FEAT, share), F32)],
    )
    spread = lax.ppermute(
        packed,
        ("row", "col"),
        [((q % n_row) * n_col + q // n_row, q) for q in range(n_row * n_col)],
    )
    row_packs = []
    for pack in chip_shifts(spread):
        row_packs += [pack, sibling(pack)]
    col_packs = shifts(packed, "row")
    bases = shifts(basis, "row")
    lists = [("smem", block_lists), ("smem", block_counts)]
    marks = [("smem", landmarks)]
    tile, part = call(
        functools.partial(tile_build_kernel, pcs, n_row, n_col),
        [pltpu.VMEM((slots, BLK, BLK), BF16), shape(col_blocks, BLK)],
        lists + vec(*col_packs, *row_packs),
        [
            pltpu.VMEM((row_blocks, FEAT, BLK), BF16),
            pltpu.VMEM((row_blocks, 8, BLK), F32),
            pltpu.VMEM((col_blocks, BLK, FEAT), BF16),
            pltpu.VMEM((col_blocks, BLK, BLK), F32),
            pltpu.VMEM((col_blocks + 1, 8, BLK), F32),
            pltpu.VMEM((2, row_blocks, PIECES, 2 * BLK), BF16),
        ],
    )
    for number in range(SWEEPS - 1):
        early = [("hbm", b) for b in bases[1:]] if number == 0 else []
        (part,) = call(
            functools.partial(tile_pass_kernel, True, n_row),
            [shape(row_blocks, BLK)],
            lists + [("keep", tile)] + vec(*shifts(part, "row")) + early,
            [
                pltpu.VMEM((n_row, col_blocks, BLK), F32),
                pltpu.VMEM((2, col_blocks, PIECES, 2 * BLK), BF16),
                pltpu.VMEM((row_blocks + 1, 8, BLK), F32),
            ],
        )
        (part,) = call(
            functools.partial(tile_pass_kernel, False, n_chip),
            [shape(col_blocks, BLK)],
            lists + [("keep", tile)] + vec(*chip_shifts(part + sibling(part))),
            [
                pltpu.VMEM((n_chip, row_blocks, BLK), F32),
                pltpu.VMEM((2, row_blocks, PIECES, 2 * BLK), BF16),
                pltpu.VMEM((col_blocks + 1, 8, BLK), F32),
            ],
        )
    both_rows = 3 * row_blocks + n_land * cols
    keep, away, both, col_scaling = call(
        functools.partial(tile_last_kernel, n_row, n_col, n_land),
        [
            shape(n_chip, per, cols, BLK),
            shape(n_chip, per, cols, BLK, dtype=BF16),
            shape(both_rows, BLK, dtype=BF16),
            shape(col_blocks, BLK),
        ],
        lists + marks + [("keep", tile)] + vec(*shifts(part, "row"), *bases),
        [
            pltpu.VMEM((n_row, col_blocks, BLK), F32),
            pltpu.VMEM((col_blocks, cols + PIECES, BLK), BF16),
            pltpu.VMEM((row_blocks + 1, cols + 8, BLK), F32),
        ],
    )
    pairs = call(
        pair_kernel,
        [shape(both_rows, BLK, dtype=BF16)]
        + [shape(per * cols, BLK, dtype=BF16)] * n_chip,
        vec(keep, sibling(away), both, sibling(both)),
    )
    sums = [pairs[0]] + [chip_shift(pairs[0], k) for k in range(1, n_chip)]
    shares = [pairs[1]] + [chip_shift(pairs[1 + k], k) for k in range(1, n_chip)]
    gram, row_scaling, own = call(
        functools.partial(gram_kernel, n_land, cols, per),
        [shape(cols, cols), shape(row_blocks, BLK), shape(per, BLK)],
        marks + vec(*sums),
        [
            pltpu.VMEM((row_blocks, BLK), F32),
            pltpu.VMEM((n_chip, row_blocks, BLK), F32),
            pltpu.VMEM((n_chip, n_land * cols, BLK), BF16),
        ],
    )
    (ritz,) = call(
        functools.partial(ritz_kernel, n_row, landmarks.shape[0] * BLK),
        [shape(cols, share)],
        vec(*shifts(gram, "row"), *shares, own),
        [pltpu.VMEM((n_row, cols, cols), F32)],
    )
    return row_scaling.reshape(-1), col_scaling.reshape(-1), ritz


def solution(mesh):
    placed = (
        P(None, ("col", "row")),
        P(("col", "row")),
        P(None, ("col", "row")),
        P("row", "col", None, None),
        P("row", "col"),
        P(),
    )
    return jax.shard_map(
        strip_body if mesh.shape["row"] <= STRIP_TILES else tile_body,
        mesh=mesh,
        in_specs=placed,
        out_specs=(P("row"), P("col"), P(None, ("row", "col"))),
        check_vma=False,
    )
```

profile of v0, /device:TPU:0, one launch (start us, length us, event | category | flops | bytes accessed | tf_op | source)
XLA Modules:
  0.0 95.6 jit_solution(9240531203608844439)
XLA Ops:
  2.2 5.1 %collective-permute-start.2 = (bf16[64,512]{1,0:T(8,128)(2,1)S(1)}, bf16[64,512]{1,0:T(8,128)(2,1)S(1)}, u32[]{:S(2)}, u32[]{:S(2)}) collective-permute-start(bf16[64,512]{1,0:T(8,128)(2,1)S(1)} %shard_map.85.refs_0_), channel_id=1, source_target_pairs={{0,24},{8,0},{16,8},{24,16},{1,25},{9,1},{17,9},{25,17},{2,26},{10... | collective-permute-start | bytes 196616 | tf_op jit(solution)/shard_map/ppermute | solution.py:499
  7.3 1.0 %collective-permute-start = (bf16[64,512]{1,0:T(8,128)(2,1)S(1)}, bf16[64,512]{1,0:T(8,128)(2,1)S(1)}, u32[]{:S(2)}, u32[]{:S(2)}) collective-permute-start(bf16[64,512]{1,0:T(8,128)(2,1)S(1)} %shard_map.85.refs_0_), channel_id=1, source_target_pairs={{0,8},{8,16},{16,24},{24,0},{1,9},{9,17},{17,25},{25,1},{2,10},{10... | collective-permute-start | bytes 196616 | tf_op jit(solution)/shard_map/ppermute | solution.py:499
  8.3 1.5 %collective-permute-done.2.refs_3_ = bf16[64,512]{1,0:T(8,128)(2,1)S(1)} collective-permute-done((bf16[64,512]{1,0:T(8,128)(2,1)S(1)}, bf16[64,512]{1,0:T(8,128)(2,1)S(1)}, u32[]{:S(2)}, u32[]{:S(2)}) %collective-permute-start.2) | collective-permute-done | bytes 65568 | tf_op jit(solution)/shard_map/ppermute | solution.py:499
  9.8 4.0 %collective-permute-done.1.refs_2_ = bf16[64,512]{1,0:T(8,128)(2,1)S(1)} collective-permute-done((bf16[64,512]{1,0:T(8,128)(2,1)S(1)}, bf16[64,512]{1,0:T(8,128)(2,1)S(1)}, u32[]{:S(2)}, u32[]{:S(2)}) %collective-permute-start.1) | collective-permute-done | bytes 65568 | tf_op jit(solution)/shard_map/ppermute | solution.py:499
  13.9 2.5 %collective-permute-start.6 = (bf16[4,64,512]{2,1,0:T(8,128)(2,1)S(1)}, bf16[4,64,512]{2,1,0:T(8,128)(2,1)S(1)}, u32[]{:S(2)}, u32[]{:S(2)}) collective-permute-start(bf16[4,64,512]{2,1,0:T(8,128)(2,1)S(1)} %get-tuple-element.32.stack), channel_id=1, source_target_pairs={{0,6},{1,7},{2,0},{3,1},{4,2},{5,3},{6,4},{7,5},{8,14},{9,15},{10,... | collective-permute-start | bytes 786440 | tf_op jit(solution)/shard_map/ppermute | solution.py:508
  17.5 1.8 %collective-permute-start.8 = (bf16[64,512]{1,0:T(8,128)(2,1)}, bf16[64,512]{1,0:T(8,128)(2,1)S(1)}, u32[]{:S(2)}, u32[]{:S(2)}) collective-permute-start(bf16[64,512]{1,0:T(8,128)(2,1)} %refs_8_), channel_id=1, source_target_pairs={{0,16},{8,24},{16,0},{24,8},{1,17},{9,25},{17,1},{25,9},{2,18},{10... | collective-permute-start | bytes 196616 | tf_op jit(solution)/shard_map/ppermute | solution.py:499
  19.2 4.0 %collective-permute-done.8.refs_10_ = bf16[64,512]{1,0:T(8,128)(2,1)S(1)} collective-permute-done((bf16[64,512]{1,0:T(8,128)(2,1)}, bf16[64,512]{1,0:T(8,128)(2,1)S(1)}, u32[]{:S(2)}, u32[]{:S(2)}) %collective-permute-start.8) | collective-permute-done | bytes 65568 | tf_op jit(solution)/shard_map/ppermute | solution.py:499
  23.2 3.8 %collective-permute-start.9 = (bf16[64,512]{1,0:T(8,128)(2,1)}, bf16[64,512]{1,0:T(8,128)(2,1)S(1)}, u32[]{:S(2)}, u32[]{:S(2)}) collective-permute-start(bf16[64,512]{1,0:T(8,128)(2,1)} %refs_8_), channel_id=1, source_target_pairs={{0,24},{8,0},{16,8},{24,16},{1,25},{9,1},{17,9},{25,17},{2,26},{10... | collective-permute-start | bytes 196616 | tf_op jit(solution)/shard_map/ppermute | solution.py:499
  27.0 5.8 %shard_map.87 = (bf16[128,128,128]{2,1,0:T(8,128)(2,1)S(1)}, bf16[16,128,64]{2,1,0:T(8,128)(2,1)S(1)}, f32[16,128,128]{2,1,0:T(8,128)S(1)}, f32[16,128]{1,0:T(8,128)S(1)}) custom-call(s32[32,128]{1,0:T(8,128)S(1)} %bitcast.3, bf16[4,64,512]{2,1,0:T(8,128)(2,1)S(1)} %get-tuple-element.32.stack, bf16[4,64,512]{2,1,0:T(8,128)(2,1)S(1)} %collective-permute-done.3.other), custom_call_target="tpu_custom_call" | custom-call | flops 16777216 | bytes 1048576 | tf_op jit(solution)/shard_map/pallas_call | solution.py:56
  33.5 0.9 collective-permute-done.10.refs_6_
  35.2 6.4 %shard_map.88 = (bf16[384,128,128]{2,1,0:T(8,128)(2,1)S(1)}, f32[128,128]{1,0:T(8,128)S(1)}) custom-call(s32[32,128]{1,0:T(8,128)S(1)} %bitcast.4, bf16[128,128,128]{2,1,0:T(8,128)(2,1)S(1)} %get-tuple-element.33.refs_1_.refs_2_, bf16[16,128,64]{2,1,0:T(8,128)(2,1)S(1)} %get-tuple-element.34.refs_2_, f32[16,128,128]{2,1,0:T(8,128)S(1)} %get-tuple-element.35.refs_3_, ...), custom_call_target="tpu_custom_call" | custom-call | flops 16777216 | bytes 1048576 | tf_op jit(solution)/shard_map/pallas_call | solution.py:56
  43.0 2.6 %collective-permute-start.16 = (bf16[128,128]{1,0:T(8,128)(2,1)S(1)}, bf16[128,128]{1,0:T(8,128)(2,1)S(1)}, u32[]{:S(2)}, u32[]{:S(2)}) collective-permute-start(bf16[128,128]{1,0:T(8,128)(2,1)S(1)} %add_convert_fusion.1.refs_3_), channel_id=1, source_target_pairs={{0,6},{1,7},{2,0},{3,1},{4,2},{5,3},{6,4},{7,5},{8,14},{9,15},{10,... | collective-permute-start | bytes 98312 | tf_op jit(solution)/shard_map/ppermute | solution.py:508
  45.6 1.8 %collective-permute-start.15 = (bf16[128,128]{1,0:T(8,128)(2,1)S(1)}, bf16[128,128]{1,0:T(8,128)(2,1)S(1)}, u32[]{:S(2)}, u32[]{:S(2)}) collective-permute-start(bf16[128,128]{1,0:T(8,128)(2,1)S(1)} %add_convert_fusion.1.refs_3_), channel_id=1, source_target_pairs={{0,4},{1,5},{2,6},{3,7},{4,0},{5,1},{6,2},{7,3},{8,12},{9,13},{10,... | collective-permute-start | bytes 98312 | tf_op jit(solution)/shard_map/ppermute | solution.py:508
  47.8 1.7 %collective-permute-done.15.refs_5_ = bf16[128,128]{1,0:T(8,128)(2,1)S(1)} collective-permute-done((bf16[128,128]{1,0:T(8,128)(2,1)S(1)}, bf16[128,128]{1,0:T(8,128)(2,1)S(1)}, u32[]{:S(2)}, u32[]{:S(2)}) %collective-permute-start.15) | collective-permute-done | bytes 32800 | tf_op jit(solution)/shard_map/ppermute | solution.py:508
  49.5 2.7 %collective-permute-done.14.refs_4_ = bf16[128,128]{1,0:T(8,128)(2,1)S(1)} collective-permute-done((bf16[128,128]{1,0:T(8,128)(2,1)S(1)}, bf16[128,128]{1,0:T(8,128)(2,1)S(1)}, u32[]{:S(2)}, u32[]{:S(2)}) %collective-permute-start.14) | collective-permute-done | bytes 32800 | tf_op jit(solution)/shard_map/ppermute | solution.py:508
  52.2 6.9 %shard_map.89 = f32[128,128]{1,0:T(8,128)S(1)} custom-call(s32[32,128]{1,0:T(8,128)S(1)} %bitcast.5, bf16[128,128,128]{2,1,0:T(8,128)(2,1)S(1)} %get-tuple-element.33.refs_1_.refs_2_, bf16[384,128,128]{2,1,0:T(8,128)(2,1)S(1)} %get-tuple-element.41.refs_2_.refs_3_, bf16[128,128]{1,0:T(8,128)(2,1)S(1)} %add_convert_fusion.1.refs_3_, ...), custom_call_target="tpu_custom_call" | custom-call | flops 16777216 | bytes 1048576 | tf_op jit(solution)/shard_map/pallas_call | solution.py:56
  59.3 1.2 %collective-permute-done.17 = f32[128,128]{1,0:T(8,128)S(1)} collective-permute-done((f32[128,128]{1,0:T(8,128)S(1)}, f32[128,128]{1,0:T(8,128)S(1)}, u32[]{:S(2)}, u32[]{:S(2)}) %collective-permute-start.17) | collective-permute-done | bytes 65568 | tf_op jit(solution)/shard_map/ppermute | solution.py:494
  61.1 1.7 %collective-permute-start.18 = (bf16[128,128]{1,0:T(8,128)(2,1)S(1)}, bf16[128,128]{1,0:T(8,128)(2,1)S(1)}, u32[]{:S(2)}, u32[]{:S(2)}) collective-permute-start(bf16[128,128]{1,0:T(8,128)(2,1)S(1)} %add_convert_fusion.refs_4_), channel_id=1, source_target_pairs={{0,2},{1,3},{2,4},{3,5},{4,6},{5,7},{6,0},{7,1},{8,10},{9,11},{10,... | collective-permute-start | bytes 98312 | tf_op jit(solution)/shard_map/ppermute | solution.py:508
  62.8 1.7 %collective-permute-done.20.refs_7_ = bf16[128,128]{1,0:T(8,128)(2,1)S(1)} collective-permute-done((bf16[128,128]{1,0:T(8,128)(2,1)S(1)}, bf16[128,128]{1,0:T(8,128)(2,1)S(1)}, u32[]{:S(2)}, u32[]{:S(2)}) %collective-permute-start.20) | collective-permute-done | bytes 32800 | tf_op jit(solution)/shard_map/ppermute | solution.py:508
  64.6 1.4 %collective-permute-done.18.refs_5_ = bf16[128,128]{1,0:T(8,128)(2,1)S(1)} collective-permute-done((bf16[128,128]{1,0:T(8,128)(2,1)S(1)}, bf16[128,128]{1,0:T(8,128)(2,1)S(1)}, u32[]{:S(2)}, u32[]{:S(2)}) %collective-permute-start.18) | collective-permute-done | bytes 32800 | tf_op jit(solution)/shard_map/ppermute | solution.py:508
  65.9 8.0 %shard_map.90 = (f32[4,4,64,128]{3,2,1,0:T(8,128)S(1)}, bf16[4,4,64,128]{3,2,1,0:T(8,128)(2,1)S(1)}, bf16[224,128]{1,0:T(8,128)(2,1)S(1)}, f32[16,128]{1,0:T(8,128)}) custom-call(s32[32,128]{1,0:T(8,128)S(1)} %bitcast.6, s32[8]{0:T(128)S(1)} %copy-done.1, bf16[128,128,128]{2,1,0:T(8,128)(2,1)S(1)} %get-tuple-element.33.refs_1_.refs_2_, ...), custom_call_target="tpu_custom_call" | custom-call | flops 16777216 | bytes 1048576 | tf_op jit(solution)/shard_map/pallas_call | solution.py:56
  74.5 1.1 %collective-permute-done.22.both_in = bf16[224,128]{1,0:T(8,128)(2,1)S(1)} collective-permute-done((bf16[224,128]{1,0:T(8,128)(2,1)S(1)}, bf16[224,128]{1,0:T(8,128)(2,1)S(1)}, u32[]{:S(2)}, u32[]{:S(2)}) %collective-permute-start.22) | collective-permute-done | bytes 57376 | tf_op jit(solution)/shard_map/ppermute | solution.py:494
  75.8 2.0 %collective-permute-start.29 = (bf16[256,128]{1,0:T(8,128)(2,1)S(1)}, bf16[256,128]{1,0:T(8,128)(2,1)S(1)}, u32[]{:S(2)}, u32[]{:S(2)}) collective-permute-start(bf16[256,128]{1,0:T(8,128)(2,1)S(1)} %get-tuple-element.55), channel_id=1, source_target_pairs={{0,2},{1,3},{2,4},{3,5},{4,6},{5,7},{6,0},{7,1},{8,10},{9,11},{10,... | collective-permute-start | bytes 196616 | tf_op jit(solution)/shard_map/ppermute | solution.py:508
  77.8 1.5 %collective-permute-start.23 = (bf16[224,128]{1,0:T(8,128)(2,1)S(1)}, bf16[224,128]{1,0:T(8,128)(2,1)S(1)}, u32[]{:S(2)}, u32[]{:S(2)}) collective-permute-start(bf16[224,128]{1,0:T(8,128)(2,1)S(1)} %get-tuple-element.50.refs_1_), channel_id=1, source_target_pairs={{0,2},{1,3},{2,4},{3,5},{4,6},{5,7},{6,0},{7,1},{8,10},{9,11},{10,... | collective-permute-start | bytes 172040 | tf_op jit(solution)/shard_map/ppermute | solution.py:508
  80.4 2.3 %collective-permute-start.31 = (bf16[256,128]{1,0:T(8,128)(2,1)S(1)}, bf16[256,128]{1,0:T(8,128)(2,1)S(1)}, u32[]{:S(2)}, u32[]{:S(2)}) collective-permute-start(bf16[256,128]{1,0:T(8,128)(2,1)S(1)} %get-tuple-element.57), channel_id=1, source_target_pairs={{0,6},{1,7},{2,0},{3,1},{4,2},{5,3},{6,4},{7,5},{8,14},{9,15},{10,... | collective-permute-start | bytes 196616 | tf_op jit(solution)/shard_map/ppermute | solution.py:508
  83.5 1.3 %shard_map.92 = (f32[64,64]{1,0:T(8,128)S(1)}, f32[32,128]{1,0:T(8,128)}, f32[4,128]{1,0:T(4,128)S(1)}) custom-call(s32[8]{0:T(128)S(1)} %copy-done.1, bf16[224,128]{1,0:T(8,128)(2,1)S(1)} %get-tuple-element.50.refs_1_, bf16[224,128]{1,0:T(8,128)(2,1)S(1)} %collective-permute-done.23.refs_2_, bf16[224,128]{1,0:T(8,128)(2,1)S(1)} %collective-permute-done.24.refs_3_, ...), custom_call_target="tpu_custom_call" | custom-call | flops 16777216 | bytes 1048576 | tf_op jit(solution)/shard_map/pallas_call | solution.py:56
  84.8 1.8 %collective-permute-start.28 = (f32[64,64]{1,0:T(8,128)S(1)}, f32[64,64]{1,0:T(8,128)S(1)}, u32[]{:S(2)}, u32[]{:S(2)}) collective-permute-start(f32[64,64]{1,0:T(8,128)S(1)} %get-tuple-element.53.refs_0_), channel_id=1, source_target_pairs={{0,24},{8,0},{16,8},{24,16},{1,25},{9,1},{17,9},{25,17},{2,26},{10... | collective-permute-start | bytes 49160 | tf_op jit(solution)/shard_map/ppermute | solution.py:499
  86.6 0.9 collective-permute-start.26
  87.6 1.2 %collective-permute-done.28.refs_3_ = f32[64,64]{1,0:T(8,128)S(1)} collective-permute-done((f32[64,64]{1,0:T(8,128)S(1)}, f32[64,64]{1,0:T(8,128)S(1)}, u32[]{:S(2)}, u32[]{:S(2)}) %collective-permute-start.28) | collective-permute-done | bytes 16416 | tf_op jit(solution)/shard_map/ppermute | solution.py:499
  88.7 2.7 %collective-permute-done.27.refs_2_ = f32[64,64]{1,0:T(8,128)S(1)} collective-permute-done((f32[64,64]{1,0:T(8,128)S(1)}, f32[64,64]{1,0:T(8,128)S(1)}, u32[]{:S(2)}, u32[]{:S(2)}) %collective-permute-start.27) | collective-permute-done | bytes 16416 | tf_op jit(solution)/shard_map/ppermute | solution.py:499
  91.5 0.9 collective-permute-done.26.refs_1_
  92.4 3.2 %shard_map.93 = f32[64,512]{1,0:T(8,128)} custom-call(f32[64,64]{1,0:T(8,128)S(1)} %get-tuple-element.53.refs_0_, f32[64,64]{1,0:T(8,128)S(1)} %collective-permute-done.26.refs_1_, f32[64,64]{1,0:T(8,128)S(1)} %collective-permute-done.27.refs_2_, f32[64,64]{1,0:T(8,128)S(1)} %collective-permute-done.28.refs_3_, ...), custom_call_target="tpu_custom_call" | custom-call | flops 16777216 | bytes 1048576 | tf_op jit(solution)/shard_map/pallas_call | solution.py:56
  (47 shorter events, 8.6 us)
Async XLA Ops:
  2.2 7.6 %collective-permute-start.2 = (bf16[64,512]{1,0:T(8,128)(2,1)S(1)}, bf16[64,512]{1,0:T(8,128)(2,1)S(1)}, u32[]{:S(2)}, u32[]{:S(2)}) collective-permute-start(bf16[64,512]{1,0:T(8,128)(2,1)S(1)} %shard_map.85.refs_0_), channel_id=1, source_target_pairs={{0,24},{8,0},{16,8},{24,16},{1,25},{9,1},{17,9},{25,17},{2,26},{10... | collective-permute-start | bytes 196616 | tf_op jit(solution)/shard_map/ppermute | solution.py:499
  7.3 6.5 %collective-permute-start.1 = (bf16[64,512]{1,0:T(8,128)(2,1)S(1)}, bf16[64,512]{1,0:T(8,128)(2,1)S(1)}, u32[]{:S(2)}, u32[]{:S(2)}) collective-permute-start(bf16[64,512]{1,0:T(8,128)(2,1)S(1)} %shard_map.85.refs_0_), channel_id=1, source_target_pairs={{0,16},{8,24},{16,0},{24,8},{1,17},{9,25},{17,1},{25,9},{2,18},{10... | collective-permute-start | bytes 196616 | tf_op jit(solution)/shard_map/ppermute | solution.py:499
  7.3 6.5 %collective-permute-start = (bf16[64,512]{1,0:T(8,128)(2,1)S(1)}, bf16[64,512]{1,0:T(8,128)(2,1)S(1)}, u32[]{:S(2)}, u32[]{:S(2)}) collective-permute-start(bf16[64,512]{1,0:T(8,128)(2,1)S(1)} %shard_map.85.refs_0_), channel_id=1, source_target_pairs={{0,8},{8,16},{16,24},{24,0},{1,9},{9,17},{17,25},{25,1},{2,10},{10... | collective-permute-start | bytes 196616 | tf_op jit(solution)/shard_map/ppermute | solution.py:499
  13.8 9.4 %collective-permute-start.3 = (bf16[4,64,512]{2,1,0:T(8,128)(2,1)S(1)}, bf16[4,64,512]{2,1,0:T(8,128)(2,1)S(1)}, u32[]{:S(2)}, u32[]{:S(2)}) collective-permute-start(bf16[4,64,512]{2,1,0:T(8,128)(2,1)S(1)} %get-tuple-element.32.stack), channel_id=1, source_target_pairs={{0,1},{1,0},{2,3},{3,2},{4,5},{5,4},{6,7},{7,6},{8,9},{9,8},{10,11... | collective-permute-start | bytes 786440 | tf_op jit(solution)/shard_map/ppermute | solution.py:494
  13.9 19.0 %collective-permute-start.6 = (bf16[4,64,512]{2,1,0:T(8,128)(2,1)S(1)}, bf16[4,64,512]{2,1,0:T(8,128)(2,1)S(1)}, u32[]{:S(2)}, u32[]{:S(2)}) collective-permute-start(bf16[4,64,512]{2,1,0:T(8,128)(2,1)S(1)} %get-tuple-element.32.stack), channel_id=1, source_target_pairs={{0,6},{1,7},{2,0},{3,1},{4,2},{5,3},{6,4},{7,5},{8,14},{9,15},{10,... | collective-permute-start | bytes 786440 | tf_op jit(solution)/shard_map/ppermute | solution.py:508
  16.4 16.5 %collective-permute-start.5 = (bf16[4,64,512]{2,1,0:T(8,128)(2,1)S(1)}, bf16[4,64,512]{2,1,0:T(8,128)(2,1)S(1)}, u32[]{:S(2)}, u32[]{:S(2)}) collective-permute-start(bf16[4,64,512]{2,1,0:T(8,128)(2,1)S(1)} %get-tuple-element.32.stack), channel_id=1, source_target_pairs={{0,4},{1,5},{2,6},{3,7},{4,0},{5,1},{6,2},{7,3},{8,12},{9,13},{10,... | collective-permute-start | bytes 786440 | tf_op jit(solution)/shard_map/ppermute | solution.py:508
  16.9 16.0 %collective-permute-start.4 = (bf16[4,64,512]{2,1,0:T(8,128)(2,1)S(1)}, bf16[4,64,512]{2,1,0:T(8,128)(2,1)S(1)}, u32[]{:S(2)}, u32[]{:S(2)}) collective-permute-start(bf16[4,64,512]{2,1,0:T(8,128)(2,1)S(1)} %get-tuple-element.32.stack), channel_id=1, source_target_pairs={{0,2},{1,3},{2,4},{3,5},{4,6},{5,7},{6,0},{7,1},{8,10},{9,11},{10,... | collective-permute-start | bytes 786440 | tf_op jit(solution)/shard_map/ppermute | solution.py:508
  17.5 5.7 %collective-permute-start.8 = (bf16[64,512]{1,0:T(8,128)(2,1)}, bf16[64,512]{1,0:T(8,128)(2,1)S(1)}, u32[]{:S(2)}, u32[]{:S(2)}) collective-permute-start(bf16[64,512]{1,0:T(8,128)(2,1)} %refs_8_), channel_id=1, source_target_pairs={{0,16},{8,24},{16,0},{24,8},{1,17},{9,25},{17,1},{25,9},{2,18},{10... | collective-permute-start | bytes 196616 | tf_op jit(solution)/shard_map/ppermute | solution.py:499
  23.2 9.6 %collective-permute-start.7 = (bf16[64,512]{1,0:T(8,128)(2,1)}, bf16[64,512]{1,0:T(8,128)(2,1)S(1)}, u32[]{:S(2)}, u32[]{:S(2)}) collective-permute-start(bf16[64,512]{1,0:T(8,128)(2,1)} %refs_8_), channel_id=1, source_target_pairs={{0,8},{8,16},{16,24},{24,0},{1,9},{9,17},{17,25},{25,1},{2,10},{10... | collective-permute-start | bytes 196616 | tf_op jit(solution)/shard_map/ppermute | solution.py:499
  23.2 9.6 %collective-permute-start.9 = (bf16[64,512]{1,0:T(8,128)(2,1)}, bf16[64,512]{1,0:T(8,128)(2,1)S(1)}, u32[]{:S(2)}, u32[]{:S(2)}) collective-permute-start(bf16[64,512]{1,0:T(8,128)(2,1)} %refs_8_), channel_id=1, source_target_pairs={{0,24},{8,0},{16,8},{24,16},{1,25},{9,1},{17,9},{25,17},{2,26},{10... | collective-permute-start | bytes 196616 | tf_op jit(solution)/shard_map/ppermute | solution.py:499
  32.8 1.6 %collective-permute-start.10 = (bf16[4,64,512]{2,1,0:T(8,128)(2,1)S(1)}, bf16[4,64,512]{2,1,0:T(8,128)(2,1)S(1)}, u32[]{:S(2)}, u32[]{:S(2)}) collective-permute-start(bf16[4,64,512]{2,1,0:T(8,128)(2,1)S(1)} %collective-permute-done.4.refs_5_), channel_id=1, source_target_pairs={{0,1},{1,0},{2,3},{3,2},{4,5},{5,4},{6,7},{7,6},{8,9},{9,8},{10,11... | collective-permute-start | bytes 786440 | tf_op jit(solution)/shard_map/ppermute | solution.py:494
  32.9 1.9 %collective-permute-start.11 = (bf16[4,64,512]{2,1,0:T(8,128)(2,1)S(1)}, bf16[4,64,512]{2,1,0:T(8,128)(2,1)S(1)}, u32[]{:S(2)}, u32[]{:S(2)}) collective-permute-start(bf16[4,64,512]{2,1,0:T(8,128)(2,1)S(1)} %collective-permute-done.5.refs_7_), channel_id=1, source_target_pairs={{0,1},{1,0},{2,3},{3,2},{4,5},{5,4},{6,7},{7,6},{8,9},{9,8},{10,11... | collective-permute-start | bytes 786440 | tf_op jit(solution)/shard_map/ppermute | solution.py:494
  33.4 1.8 %collective-permute-start.12 = (bf16[4,64,512]{2,1,0:T(8,128)(2,1)S(1)}, bf16[4,64,512]{2,1,0:T(8,128)(2,1)S(1)}, u32[]{:S(2)}, u32[]{:S(2)}) collective-permute-start(bf16[4,64,512]{2,1,0:T(8,128)(2,1)S(1)} %collective-permute-done.6.refs_9_), channel_id=1, source_target_pairs={{0,1},{1,0},{2,3},{3,2},{4,5},{5,4},{6,7},{7,6},{8,9},{9,8},{10,11... | collective-permute-start | bytes 786440 | tf_op jit(solution)/shard_map/ppermute | solution.py:494
  41.6 1.4 %collective-permute-start.13 = (f32[128,128]{1,0:T(8,128)S(1)}, f32[128,128]{1,0:T(8,128)S(1)}, u32[]{:S(2)}, u32[]{:S(2)}) collective-permute-start(f32[128,128]{1,0:T(8,128)S(1)} %get-tuple-element.42), channel_id=1, source_target_pairs={{0,1},{1,0},{2,3},{3,2},{4,5},{5,4},{6,7},{7,6},{8,9},{9,8},{10,11... | collective-permute-start | bytes 196616 | tf_op jit(solution)/shard_map/ppermute | solution.py:494
  43.0 4.8 %collective-permute-start.16 = (bf16[128,128]{1,0:T(8,128)(2,1)S(1)}, bf16[128,128]{1,0:T(8,128)(2,1)S(1)}, u32[]{:S(2)}, u32[]{:S(2)}) collective-permute-start(bf16[128,128]{1,0:T(8,128)(2,1)S(1)} %add_convert_fusion.1.refs_3_), channel_id=1, source_target_pairs={{0,6},{1,7},{2,0},{3,1},{4,2},{5,3},{6,4},{7,5},{8,14},{9,15},{10,... | collective-permute-start | bytes 98312 | tf_op jit(solution)/shard_map/ppermute | solution.py:508
  45.6 3.9 %collective-permute-start.15 = (bf16[128,128]{1,0:T(8,128)(2,1)S(1)}, bf16[128,128]{1,0:T(8,128)(2,1)S(1)}, u32[]{:S(2)}, u32[]{:S(2)}) collective-permute-start(bf16[128,128]{1,0:T(8,128)(2,1)S(1)} %add_convert_fusion.1.refs_3_), channel_id=1, source_target_pairs={{0,4},{1,5},{2,6},{3,7},{4,0},{5,1},{6,2},{7,3},{8,12},{9,13},{10,... | collective-permute-start | bytes 98312 | tf_op jit(solution)/shard_map/ppermute | solution.py:508
  47.4 4.8 %collective-permute-start.14 = (bf16[128,128]{1,0:T(8,128)(2,1)S(1)}, bf16[128,128]{1,0:T(8,128)(2,1)S(1)}, u32[]{:S(2)}, u32[]{:S(2)}) collective-permute-start(bf16[128,128]{1,0:T(8,128)(2,1)S(1)} %add_convert_fusion.1.refs_3_), channel_id=1, source_target_pairs={{0,2},{1,3},{2,4},{3,5},{4,6},{5,7},{6,0},{7,1},{8,10},{9,11},{10,... | collective-permute-start | bytes 98312 | tf_op jit(solution)/shard_map/ppermute | solution.py:508
  59.2 1.3 %collective-permute-start.17 = (f32[128,128]{1,0:T(8,128)S(1)}, f32[128,128]{1,0:T(8,128)S(1)}, u32[]{:S(2)}, u32[]{:S(2)}) collective-permute-start(f32[128,128]{1,0:T(8,128)S(1)} %shard_map.89), channel_id=1, source_target_pairs={{0,1},{1,0},{2,3},{3,2},{4,5},{5,4},{6,7},{7,6},{8,9},{9,8},{10,11... | collective-permute-start | bytes 196616 | tf_op jit(solution)/shard_map/ppermute | solution.py:494
  60.5 4.0 %collective-permute-start.20 = (bf16[128,128]{1,0:T(8,128)(2,1)S(1)}, bf16[128,128]{1,0:T(8,128)(2,1)S(1)}, u32[]{:S(2)}, u32[]{:S(2)}) collective-permute-start(bf16[128,128]{1,0:T(8,128)(2,1)S(1)} %add_convert_fusion.refs_4_), channel_id=1, source_target_pairs={{0,6},{1,7},{2,0},{3,1},{4,2},{5,3},{6,4},{7,5},{8,14},{9,15},{10,... | collective-permute-start | bytes 98312 | tf_op jit(solution)/shard_map/ppermute | solution.py:508
  60.6 4.0 %collective-permute-start.19 = (bf16[128,128]{1,0:T(8,128)(2,1)S(1)}, bf16[128,128]{1,0:T(8,128)(2,1)S(1)}, u32[]{:S(2)}, u32[]{:S(2)}) collective-permute-start(bf16[128,128]{1,0:T(8,128)(2,1)S(1)} %add_convert_fusion.refs_4_), channel_id=1, source_target_pairs={{0,4},{1,5},{2,6},{3,7},{4,0},{5,1},{6,2},{7,3},{8,12},{9,13},{10,... | collective-permute-start | bytes 98312 | tf_op jit(solution)/shard_map/ppermute | solution.py:508
  61.1 4.9 %collective-permute-start.18 = (bf16[128,128]{1,0:T(8,128)(2,1)S(1)}, bf16[128,128]{1,0:T(8,128)(2,1)S(1)}, u32[]{:S(2)}, u32[]{:S(2)}) collective-permute-start(bf16[128,128]{1,0:T(8,128)(2,1)S(1)} %add_convert_fusion.refs_4_), channel_id=1, source_target_pairs={{0,2},{1,3},{2,4},{3,5},{4,6},{5,7},{6,0},{7,1},{8,10},{9,11},{10,... | collective-permute-start | bytes 98312 | tf_op jit(solution)/shard_map/ppermute | solution.py:508
  74.0 1.6 %collective-permute-start.21 = (bf16[4,4,64,128]{3,2,1,0:T(8,128)(2,1)S(1)}, bf16[4,4,64,128]{3,2,1,0:T(8,128)(2,1)S(1)}, u32[]{:S(2)}, u32[]{:S(2)}) collective-permute-start(bf16[4,4,64,128]{3,2,1,0:T(8,128)(2,1)S(1)} %get-tuple-element.48), channel_id=1, source_target_pairs={{0,1},{1,0},{2,3},{3,2},{4,5},{5,4},{6,7},{7,6},{8,9},{9,8},{10,11... | collective-permute-start | bytes 786440 | tf_op jit(solution)/shard_map/ppermute | solution.py:494
  74.0 1.6 %collective-permute-start.22 = (bf16[224,128]{1,0:T(8,128)(2,1)S(1)}, bf16[224,128]{1,0:T(8,128)(2,1)S(1)}, u32[]{:S(2)}, u32[]{:S(2)}) collective-permute-start(bf16[224,128]{1,0:T(8,128)(2,1)S(1)} %get-tuple-element.49.both), channel_id=1, source_target_pairs={{0,1},{1,0},{2,3},{3,2},{4,5},{5,4},{6,7},{7,6},{8,9},{9,8},{10,11... | collective-permute-start | bytes 172040 | tf_op jit(solution)/shard_map/ppermute | solution.py:494
  75.7 4.7 %collective-permute-start.25 = (bf16[224,128]{1,0:T(8,128)(2,1)S(1)}, bf16[224,128]{1,0:T(8,128)(2,1)S(1)}, u32[]{:S(2)}, u32[]{:S(2)}) collective-permute-start(bf16[224,128]{1,0:T(8,128)(2,1)S(1)} %get-tuple-element.50.refs_1_), channel_id=1, source_target_pairs={{0,6},{1,7},{2,0},{3,1},{4,2},{5,3},{6,4},{7,5},{8,14},{9,15},{10,... | collective-permute-start | bytes 172040 | tf_op jit(solution)/shard_map/ppermute | solution.py:508
  75.8 10.9 %collective-permute-start.29 = (bf16[256,128]{1,0:T(8,128)(2,1)S(1)}, bf16[256,128]{1,0:T(8,128)(2,1)S(1)}, u32[]{:S(2)}, u32[]{:S(2)}) collective-permute-start(bf16[256,128]{1,0:T(8,128)(2,1)S(1)} %get-tuple-element.55), channel_id=1, source_target_pairs={{0,2},{1,3},{2,4},{3,5},{4,6},{5,7},{6,0},{7,1},{8,10},{9,11},{10,... | collective-permute-start | bytes 196616 | tf_op jit(solution)/shard_map/ppermute | solution.py:508
  77.8 5.7 %collective-permute-start.24 = (bf16[224,128]{1,0:T(8,128)(2,1)S(1)}, bf16[224,128]{1,0:T(8,128)(2,1)S(1)}, u32[]{:S(2)}, u32[]{:S(2)}) collective-permute-start(bf16[224,128]{1,0:T(8,128)(2,1)S(1)} %get-tuple-element.50.refs_1_), channel_id=1, source_target_pairs={{0,4},{1,5},{2,6},{3,7},{4,0},{5,1},{6,2},{7,3},{8,12},{9,13},{10,... | collective-permute-start | bytes 172040 | tf_op jit(solution)/shard_map/ppermute | solution.py:508
  77.8 5.7 %collective-permute-start.23 = (bf16[224,128]{1,0:T(8,128)(2,1)S(1)}, bf16[224,128]{1,0:T(8,128)(2,1)S(1)}, u32[]{:S(2)}, u32[]{:S(2)}) collective-permute-start(bf16[224,128]{1,0:T(8,128)(2,1)S(1)} %get-tuple-element.50.refs_1_), channel_id=1, source_target_pairs={{0,2},{1,3},{2,4},{3,5},{4,6},{5,7},{6,0},{7,1},{8,10},{9,11},{10,... | collective-permute-start | bytes 172040 | tf_op jit(solution)/shard_map/ppermute | solution.py:508
  79.3 8.2 %collective-permute-start.30 = (bf16[256,128]{1,0:T(8,128)(2,1)S(1)}, bf16[256,128]{1,0:T(8,128)(2,1)S(1)}, u32[]{:S(2)}, u32[]{:S(2)}) collective-permute-start(bf16[256,128]{1,0:T(8,128)(2,1)S(1)} %get-tuple-element.56), channel_id=1, source_target_pairs={{0,4},{1,5},{2,6},{3,7},{4,0},{5,1},{6,2},{7,3},{8,12},{9,13},{10,... | collective-permute-start | bytes 196616 | tf_op jit(solution)/shard_map/ppermute | solution.py:508
  80.4 7.1 %collective-permute-start.31 = (bf16[256,128]{1,0:T(8,128)(2,1)S(1)}, bf16[256,128]{1,0:T(8,128)(2,1)S(1)}, u32[]{:S(2)}, u32[]{:S(2)}) collective-permute-start(bf16[256,128]{1,0:T(8,128)(2,1)S(1)} %get-tuple-element.57), channel_id=1, source_target_pairs={{0,6},{1,7},{2,0},{3,1},{4,2},{5,3},{6,4},{7,5},{8,14},{9,15},{10,... | collective-permute-start | bytes 196616 | tf_op jit(solution)/shard_map/ppermute | solution.py:508
  84.8 3.9 %collective-permute-start.28 = (f32[64,64]{1,0:T(8,128)S(1)}, f32[64,64]{1,0:T(8,128)S(1)}, u32[]{:S(2)}, u32[]{:S(2)}) collective-permute-start(f32[64,64]{1,0:T(8,128)S(1)} %get-tuple-element.53.refs_0_), channel_id=1, source_target_pairs={{0,24},{8,0},{16,8},{24,16},{1,25},{9,1},{17,9},{25,17},{2,26},{10... | collective-permute-start | bytes 49160 | tf_op jit(solution)/shard_map/ppermute | solution.py:499
  86.6 4.8 %collective-permute-start.27 = (f32[64,64]{1,0:T(8,128)S(1)}, f32[64,64]{1,0:T(8,128)S(1)}, u32[]{:S(2)}, u32[]{:S(2)}) collective-permute-start(f32[64,64]{1,0:T(8,128)S(1)} %get-tuple-element.53.refs_0_), channel_id=1, source_target_pairs={{0,16},{8,24},{16,0},{24,8},{1,17},{9,25},{17,1},{25,9},{2,18},{10... | collective-permute-start | bytes 49160 | tf_op jit(solution)/shard_map/ppermute | solution.py:499
  86.6 5.7 %collective-permute-start.26 = (f32[64,64]{1,0:T(8,128)S(1)}, f32[64,64]{1,0:T(8,128)S(1)}, u32[]{:S(2)}, u32[]{:S(2)}) collective-permute-start(f32[64,64]{1,0:T(8,128)S(1)} %get-tuple-element.53.refs_0_), channel_id=1, source_target_pairs={{0,8},{8,16},{16,24},{24,0},{1,9},{9,17},{17,25},{25,1},{2,10},{10... | collective-permute-start | bytes 49160 | tf_op jit(solution)/shard_map/ppermute | solution.py:499
  (2 other events, 77.9 us)
where the time goes:
time: 95.7 us; the launch traced here: 95.6 us
  starting transfers between devices  32.9 us (34%)
  Pallas kernels  32.7 us (34%)
  waiting for transfers between devices  28.5 us (30%)
  between operations  1.42 us (1%)
    pallas_call x9, Pallas kernels, call(): pl.pallas_call(kernel, out_shape=tuple(outs), in_specs=specs, out_specs=t...  32.7 us
    ppermute x15, starting transfers between devices, chip_shift(): lax.ppermute(x, 'col', [(2 * q + p, 2 * ((q + k) % n) + p) for q in range...  16.7 us
    ppermute x9, starting transfers between devices, shift(): return lax.ppermute(x, axis, [(i, (i + k) % n) for i in range(n)])  14.5 us
    ppermute x9, waiting for transfers between devices, shift(): return lax.ppermute(x, axis, [(i, (i + k) % n) for i in range(n)])  14.2 us
    ppermute x15, waiting for transfers between devices, chip_shift(): lax.ppermute(x, 'col', [(2 * q + p, 2 * ((q + k) % n) + p) for q in range...  9.31 us
    ppermute x8, waiting for transfers between devices, swap(): lax.ppermute(x, axis, [(i, i ^ k) for i in range(lax.axis_size(axis))])  4.95 us
  transfers between devices with their start and end apart: 32, of which 20 were waited for; matrix products, arithmetic and copies ran while one was open for 0% of the time, Pallas kernels for 7%

commit v1 on v0

--- a/solution.py
+++ b/solution.py
@@ -45,6 +45,8 @@
     for kind, array in ins:
         if kind == "smem":
             specs.append(SMEM_SPEC)
+        elif kind == "near":
+            specs.append(pl.BlockSpec(memory_space=pl.ANY))
         elif kind == "hbm":
             specs.append(pl.BlockSpec(memory_space=pltpu.HBM))
             array = pltpu.with_memory_space_constraint(array, pltpu.HBM)
@@ -159,22 +161,21 @@
         acc[target] += sums[row : row + 8, lane : lane + BLK]
 
 
-def row_sums(tile, left, acc, row_blocks, spare):
+def row_sums(tile, wide, acc, row_blocks, spare):
     first = tile.group * row_blocks
 
-    def step(*slots):
-        low = [left[0, tile.column(s)] for s in slots[:2]]
-        high = [left[1, tile.column(s)] for s in slots[2:]]
-        sums = jnp.dot(
-            jnp.concatenate(low + high, axis=0),
-            square(tile, slots),
-            preferred_element_type=F32,
-        )
-        firsts = [(0, 0), (PIECES, BLK), (2 * PIECES, 0), (3 * PIECES, BLK)]
-        targets = [jnp.where(s < tile.total, first + tile.row(s), spare) for s in slots]
-        add_rows(acc, sums, firsts, targets)
-
-    slot_loop(step, tile.total, 4, GROUP)
+    def step(s):
+        product = tile.block(s).astype(F32) * wide[tile.column(s)]
+        sums = jnp.sum(product.reshape(BLK // 8, 8, BLK), axis=0)
+        acc[jnp.where(s < tile.total, first + tile.row(s), spare)] += sums
+
+    slot_loop(step, tile.total, 1, GROUP)
+
+
+def spread_lanes(wide, scaling):
+    turned = scaling.T
+    for b in range(scaling.shape[0]):
+        wide[b] = jnp.broadcast_to(turned[:, b : b + 1], (BLK, BLK))
 
 
 def col_sums(tile, left, acc, row_blocks, spare):
@@ -200,7 +201,7 @@
         targets = [jnp.where(s < tile.total, tile.column(s), spare) for s in slots]
         add_rows(acc, sums, firsts, targets)
 
-    slot_loop(step, tile.total, 4, GROUP)
+    slot_loop(step, tile.total, 4, 2 * GROUP if tile.k == 0 else GROUP)
 
 
 def fill_pieces(left, scaling):
@@ -283,18 +284,18 @@
     return jnp.sum(acc[0:col_blocks], axis=1)
 
 
-def row_part(tiles, left, acc, row_blocks, out):
+def row_part(tiles, wide, acc, row_blocks, out):
     blocks = acc.shape[0] - 1
     acc[...] = jnp.zeros_like(acc)
     for tile in tiles:
-        row_sums(tile, left, acc, row_blocks, blocks)
+        row_sums(tile, wide, acc, row_blocks, blocks)
     out[...] = jnp.sum(acc[0:blocks], axis=1)
 
 
 def strip_kernel(pcs, n_row, *refs):
     table, own, col_prof, col_inv, own_sums = refs[:5]
     stacks = refs[5 : 5 + 2 * n_row - 2]
-    others, out, row_prof, row_inv, left, row_acc, col_acc = refs[-7:]
+    others, out, row_prof, row_inv, wide, row_acc, col_acc = refs[-7:]
     row_blocks = row_prof.shape[0] // (n_row - 1)
     tiles = [Tile(table, n_row, k, own, others) for k in range(n_row)]
     for k in range(1, n_row):
@@ -304,8 +305,8 @@
         first = (k - 1) * row_blocks
         build(tiles[k], first, row_prof, row_inv, col_prof, col_inv)
     totals = column_totals(tiles[1:], None, col_acc, row_blocks) + own_sums[...]
-    fill_pieces(left, SCALE / totals)
-    row_part(tiles, left, row_acc, row_blocks, out)
+    spread_lanes(wide, SCALE / totals)
+    row_part(tiles, wide, row_acc, row_blocks, out)
 
 
 def row_scalings(stage, parts):
@@ -317,13 +318,13 @@
 def sweep_kernel(n_row, n_chip, *refs):
     table, own, others = refs[:3]
     parts = refs[3 : 3 + n_chip]
-    out, stage, row_left, left, row_acc, col_acc = refs[-6:]
+    out, stage, row_left, wide, row_acc, col_acc = refs[-6:]
     row_blocks = out.shape[0] // n_row
     tiles = [Tile(table, n_row, k, own, others) for k in range(n_row)]
     fill_pieces(row_left, row_scalings(stage, parts))
     totals = column_totals(tiles, row_left, col_acc, row_blocks)
-    fill_pieces(left, SCALE / totals)
-    row_part(tiles, left, row_acc, row_blocks, out)
+    spread_lanes(wide, SCALE / totals)
+    row_part(tiles, wide, row_acc, row_blocks, out)
 
 
 def pieces_of(value):
@@ -558,7 +559,6 @@
     table = ("smem", table.reshape(n_row * 8, BLK))
     marks = ("smem", landmarks)
     far = [chip_shift(stack, k) for k in range(1, n_chip)]
-    bases = shifts(basis, "row")
     own, col_prof, col_inv, sums = call(
         functools.partial(own_kernel, pcs),
         [
@@ -574,6 +574,8 @@
             pltpu.VMEM((col_blocks + 1, 8, BLK), F32),
         ],
     )
+    basis, sums = lax.optimization_barrier((basis, sums))
+    bases = shifts(basis, "row")
     far, sums, bases = lax.optimization_barrier((far, sums, bases))
     stacks = [x for pack in far for x in (pack, sibling(pack))]
     far_slots = (n_row - 1) * slots
@@ -585,7 +587,7 @@
         [
             pltpu.VMEM((all_rows - row_blocks, FEAT, BLK), BF16),
             pltpu.VMEM((all_rows - row_blocks, 8, BLK), F32),
-            pltpu.VMEM((2, col_blocks, PIECES, 2 * BLK), BF16),
+            pltpu.VMEM((col_blocks, BLK, BLK), F32),
             pltpu.VMEM((all_rows + 1, 8, BLK), F32),
             pltpu.VMEM((col_blocks + 1, 8, BLK), F32),
         ],
@@ -603,7 +605,7 @@
             [
                 pltpu.VMEM((n_chip, all_rows, BLK), F32),
                 pltpu.VMEM((2, all_rows, PIECES, 2 * BLK), BF16),
-                pltpu.VMEM((2, col_blocks, PIECES, 2 * BLK), BF16),
+                pltpu.VMEM((col_blocks, BLK, BLK), F32),
                 pltpu.VMEM((all_rows + 1, 8, BLK), F32),
                 pltpu.VMEM((col_blocks + 1, 8, BLK), F32),
             ],
@@ -875,7 +877,7 @@
         ],
     )
     for number in range(SWEEPS - 1):
-        early = [("hbm", b) for b in bases[1:]] if number == 0 else []
+        early = [("near", b) for b in bases[1:]] if number == 0 else []
         (part,) = call(
             functools.partial(tile_pass_kernel, True, n_row),
             [shape(row_blocks, BLK)],

time: 95.7 us -> 94.6 us (0.989)
    ppermute x9, waiting for transfers between devices: 14.2 us -> 10.6 us  [shift(): return lax.ppermute(x, axis, [(i, (i + k) % n) for i in range(n)])]
    ppermute x15, waiting for transfers between devices: 9.31 us -> 12.6 us  [chip_shift(): lax.ppermute(x, 'col', [(2 * q + p, 2 * ((q + k) % n) + p) for q in range...]
where the time goes in v1:
time: 94.6 us; the launch traced here: 94.3 us
  starting transfers between devices  33 us (35%)
  Pallas kernels  31.8 us (34%)
  waiting for transfers between devices  28.2 us (30%)
  between operations  1.38 us (1%)
    pallas_call x9, Pallas kernels, call(): pl.pallas_call(kernel, out_shape=tuple(outs), in_specs=specs, out_specs=t...  31.8 us
    ppermute x15, starting transfers between devices, chip_shift(): lax.ppermute(x, 'col', [(2 * q + p, 2 * ((q + k) % n) + p) for q in range...  16.5 us
    ppermute x9, starting transfers between devices, shift(): return lax.ppermute(x, axis, [(i, (i + k) % n) for i in range(n)])  14.8 us
    ppermute x15, waiting for transfers between devices, chip_shift(): lax.ppermute(x, 'col', [(2 * q + p, 2 * ((q + k) % n) + p) for q in range...  12.6 us
    ppermute x9, waiting for transfers between devices, shift(): return lax.ppermute(x, axis, [(i, (i + k) % n) for i in range(n)])  10.6 us
    ppermute x8, waiting for transfers between devices, swap(): lax.ppermute(x, axis, [(i, i ^ k) for i in range(lax.axis_size(axis))])  5.03 us
  transfers between devices with their start and end apart: 32, of which 20 were waited for; matrix products, arithmetic and copies ran while one was open for 0% of the time, Pallas kernels for 7%

profile of v1, /device:TPU:0, one launch (start us, length us, event | category | flops | bytes accessed | tf_op | source)
XLA Modules:
  0.0 94.3 jit_solution(4478907755085849727)
XLA Ops:
  2.2 5.1 %collective-permute-start.2 = (bf16[64,512]{1,0:T(8,128)(2,1)S(1)}, bf16[64,512]{1,0:T(8,128)(2,1)S(1)}, u32[]{:S(2)}, u32[]{:S(2)}) collective-permute-start(bf16[64,512]{1,0:T(8,128)(2,1)S(1)} %shard_map.85.refs_0_), channel_id=1, source_target_pairs={{0,24},{8,0},{16,8},{24,16},{1,25},{9,1},{17,9},{25,17},{2,26},{10... | collective-permute-start | bytes 196616 | tf_op jit(solution)/shard_map/ppermute | solution.py:500
  7.3 1.0 %collective-permute-start = (bf16[64,512]{1,0:T(8,128)(2,1)S(1)}, bf16[64,512]{1,0:T(8,128)(2,1)S(1)}, u32[]{:S(2)}, u32[]{:S(2)}) collective-permute-start(bf16[64,512]{1,0:T(8,128)(2,1)S(1)} %shard_map.85.refs_0_), channel_id=1, source_target_pairs={{0,8},{8,16},{16,24},{24,0},{1,9},{9,17},{17,25},{25,1},{2,10},{10... | collective-permute-start | bytes 196616 | tf_op jit(solution)/shard_map/ppermute | solution.py:500
  8.3 1.5 %collective-permute-done.2.refs_3_ = bf16[64,512]{1,0:T(8,128)(2,1)S(1)} collective-permute-done((bf16[64,512]{1,0:T(8,128)(2,1)S(1)}, bf16[64,512]{1,0:T(8,128)(2,1)S(1)}, u32[]{:S(2)}, u32[]{:S(2)}) %collective-permute-start.2) | collective-permute-done | bytes 65568 | tf_op jit(solution)/shard_map/ppermute | solution.py:500
  9.8 4.0 %collective-permute-done.1.refs_2_ = bf16[64,512]{1,0:T(8,128)(2,1)S(1)} collective-permute-done((bf16[64,512]{1,0:T(8,128)(2,1)S(1)}, bf16[64,512]{1,0:T(8,128)(2,1)S(1)}, u32[]{:S(2)}, u32[]{:S(2)}) %collective-permute-start.1) | collective-permute-done | bytes 65568 | tf_op jit(solution)/shard_map/ppermute | solution.py:500
  13.9 2.5 %collective-permute-start.6 = (bf16[4,64,512]{2,1,0:T(8,128)(2,1)S(1)}, bf16[4,64,512]{2,1,0:T(8,128)(2,1)S(1)}, u32[]{:S(2)}, u32[]{:S(2)}) collective-permute-start(bf16[4,64,512]{2,1,0:T(8,128)(2,1)S(1)} %get-tuple-element.34.stack), channel_id=1, source_target_pairs={{0,6},{1,7},{2,0},{3,1},{4,2},{5,3},{6,4},{7,5},{8,14},{9,15},{10,... | collective-permute-start | bytes 786440 | tf_op jit(solution)/shard_map/ppermute | solution.py:509
  17.5 5.5 %shard_map.87 = (bf16[128,128,128]{2,1,0:T(8,128)(2,1)S(1)}, bf16[16,128,64]{2,1,0:T(8,128)(2,1)S(1)}, f32[16,128,128]{2,1,0:T(8,128)S(1)}, f32[16,128]{1,0:T(8,128)S(1)}) custom-call(s32[32,128]{1,0:T(8,128)S(1)} %bitcast.3, bf16[4,64,512]{2,1,0:T(8,128)(2,1)S(1)} %get-tuple-element.34.stack, bf16[4,64,512]{2,1,0:T(8,128)(2,1)S(1)} %collective-permute-done.3.other), custom_call_target="tpu_custom_call" | custom-call | flops 16777216 | bytes 1048576 | tf_op jit(solution)/shard_map/pallas_call | solution.py:58
  23.0 1.9 %collective-permute-start.9 = (bf16[64,512]{1,0:T(8,128)(2,1)}, bf16[64,512]{1,0:T(8,128)(2,1)S(1)}, u32[]{:S(2)}, u32[]{:S(2)}) collective-permute-start(bf16[64,512]{1,0:T(8,128)(2,1)} %refs_8_), channel_id=1, source_target_pairs={{0,24},{8,0},{16,8},{24,16},{1,25},{9,1},{17,9},{25,17},{2,26},{10... | collective-permute-start | bytes 196616 | tf_op jit(solution)/shard_map/ppermute | solution.py:500
  24.9 1.9 %collective-permute-start.7 = (bf16[64,512]{1,0:T(8,128)(2,1)}, bf16[64,512]{1,0:T(8,128)(2,1)S(1)}, u32[]{:S(2)}, u32[]{:S(2)}) collective-permute-start(bf16[64,512]{1,0:T(8,128)(2,1)} %refs_8_), channel_id=1, source_target_pairs={{0,8},{8,16},{16,24},{24,0},{1,9},{9,17},{17,25},{25,1},{2,10},{10... | collective-permute-start | bytes 196616 | tf_op jit(solution)/shard_map/ppermute | solution.py:500
  26.8 3.5 %collective-permute-done.5.refs_7_ = bf16[4,64,512]{2,1,0:T(8,128)(2,1)S(1)} collective-permute-done((bf16[4,64,512]{2,1,0:T(8,128)(2,1)S(1)}, bf16[4,64,512]{2,1,0:T(8,128)(2,1)S(1)}, u32[]{:S(2)}, u32[]{:S(2)}) %collective-permute-start.5) | collective-permute-done | bytes 262176 | tf_op jit(solution)/shard_map/ppermute | solution.py:509
  30.4 1.4 %collective-permute-done.8.refs_10_ = bf16[64,512]{1,0:T(8,128)(2,1)S(1)} collective-permute-done((bf16[64,512]{1,0:T(8,128)(2,1)}, bf16[64,512]{1,0:T(8,128)(2,1)S(1)}, u32[]{:S(2)}, u32[]{:S(2)}) %collective-permute-start.8) | collective-permute-done | bytes 65568 | tf_op jit(solution)/shard_map/ppermute | solution.py:500
  32.2 1.0 %collective-permute-done.10.refs_6_ = bf16[4,64,512]{2,1,0:T(8,128)(2,1)S(1)} collective-permute-done((bf16[4,64,512]{2,1,0:T(8,128)(2,1)S(1)}, bf16[4,64,512]{2,1,0:T(8,128)(2,1)S(1)}, u32[]{:S(2)}, u32[]{:S(2)}) %collective-permute-start.10) | collective-permute-done | bytes 262176 | tf_op jit(solution)/shard_map/ppermute | solution.py:495
  34.0 6.5 %shard_map.88 = (bf16[384,128,128]{2,1,0:T(8,128)(2,1)S(1)}, f32[128,128]{1,0:T(8,128)S(1)}) custom-call(s32[32,128]{1,0:T(8,128)S(1)} %bitcast.4, bf16[128,128,128]{2,1,0:T(8,128)(2,1)S(1)} %get-tuple-element.35.refs_1_.refs_2_, bf16[16,128,64]{2,1,0:T(8,128)(2,1)S(1)} %get-tuple-element.36.refs_2_, f32[16,128,128]{2,1,0:T(8,128)S(1)} %get-tuple-element.37.refs_3_, ...), custom_call_target="tpu_custom_call" | custom-call | flops 16777216 | bytes 1048576 | tf_op jit(solution)/shard_map/pallas_call | solution.py:58
  41.9 2.4 %collective-permute-start.16 = (bf16[128,128]{1,0:T(8,128)(2,1)S(1)}, bf16[128,128]{1,0:T(8,128)(2,1)S(1)}, u32[]{:S(2)}, u32[]{:S(2)}) collective-permute-start(bf16[128,128]{1,0:T(8,128)(2,1)S(1)} %add_convert_fusion.1.refs_3_), channel_id=1, source_target_pairs={{0,6},{1,7},{2,0},{3,1},{4,2},{5,3},{6,4},{7,5},{8,14},{9,15},{10,... | collective-permute-start | bytes 98312 | tf_op jit(solution)/shard_map/ppermute | solution.py:509
  44.3 1.2 %collective-permute-start.15 = (bf16[128,128]{1,0:T(8,128)(2,1)S(1)}, bf16[128,128]{1,0:T(8,128)(2,1)S(1)}, u32[]{:S(2)}, u32[]{:S(2)}) collective-permute-start(bf16[128,128]{1,0:T(8,128)(2,1)S(1)} %add_convert_fusion.1.refs_3_), channel_id=1, source_target_pairs={{0,4},{1,5},{2,6},{3,7},{4,0},{5,1},{6,2},{7,3},{8,12},{9,13},{10,... | collective-permute-start | bytes 98312 | tf_op jit(solution)/shard_map/ppermute | solution.py:509
  46.0 2.2 %collective-permute-done.15.refs_5_ = bf16[128,128]{1,0:T(8,128)(2,1)S(1)} collective-permute-done((bf16[128,128]{1,0:T(8,128)(2,1)S(1)}, bf16[128,128]{1,0:T(8,128)(2,1)S(1)}, u32[]{:S(2)}, u32[]{:S(2)}) %collective-permute-start.15) | collective-permute-done | bytes 32800 | tf_op jit(solution)/shard_map/ppermute | solution.py:509
  48.2 2.1 %collective-permute-done.14.refs_4_ = bf16[128,128]{1,0:T(8,128)(2,1)S(1)} collective-permute-done((bf16[128,128]{1,0:T(8,128)(2,1)S(1)}, bf16[128,128]{1,0:T(8,128)(2,1)S(1)}, u32[]{:S(2)}, u32[]{:S(2)}) %collective-permute-start.14) | collective-permute-done | bytes 32800 | tf_op jit(solution)/shard_map/ppermute | solution.py:509
  50.4 6.5 %shard_map.89 = f32[128,128]{1,0:T(8,128)S(1)} custom-call(s32[32,128]{1,0:T(8,128)S(1)} %bitcast.5, bf16[128,128,128]{2,1,0:T(8,128)(2,1)S(1)} %get-tuple-element.35.refs_1_.refs_2_, bf16[384,128,128]{2,1,0:T(8,128)(2,1)S(1)} %get-tuple-element.45.refs_2_.refs_3_, bf16[128,128]{1,0:T(8,128)(2,1)S(1)} %add_convert_fusion.1.refs_3_, ...), custom_call_target="tpu_custom_call" | custom-call | flops 16777216 | bytes 1048576 | tf_op jit(solution)/shard_map/pallas_call | solution.py:58
  56.9 1.2 %collective-permute-done.17 = f32[128,128]{1,0:T(8,128)S(1)} collective-permute-done((f32[128,128]{1,0:T(8,128)S(1)}, f32[128,128]{1,0:T(8,128)S(1)}, u32[]{:S(2)}, u32[]{:S(2)}) %collective-permute-start.17) | collective-permute-done | bytes 65568 | tf_op jit(solution)/shard_map/ppermute | solution.py:495
  59.1 1.9 %collective-permute-start.18 = (bf16[128,128]{1,0:T(8,128)(2,1)S(1)}, bf16[128,128]{1,0:T(8,128)(2,1)S(1)}, u32[]{:S(2)}, u32[]{:S(2)}) collective-permute-start(bf16[128,128]{1,0:T(8,128)(2,1)S(1)} %add_convert_fusion.refs_4_), channel_id=1, source_target_pairs={{0,2},{1,3},{2,4},{3,5},{4,6},{5,7},{6,0},{7,1},{8,10},{9,11},{10,... | collective-permute-start | bytes 98312 | tf_op jit(solution)/shard_map/ppermute | solution.py:509
  61.0 1.1 %collective-permute-done.20.refs_7_ = bf16[128,128]{1,0:T(8,128)(2,1)S(1)} collective-permute-done((bf16[128,128]{1,0:T(8,128)(2,1)S(1)}, bf16[128,128]{1,0:T(8,128)(2,1)S(1)}, u32[]{:S(2)}, u32[]{:S(2)}) %collective-permute-start.20) | collective-permute-done | bytes 32800 | tf_op jit(solution)/shard_map/ppermute | solution.py:509
  62.2 1.7 %collective-permute-done.18.refs_5_ = bf16[128,128]{1,0:T(8,128)(2,1)S(1)} collective-permute-done((bf16[128,128]{1,0:T(8,128)(2,1)S(1)}, bf16[128,128]{1,0:T(8,128)(2,1)S(1)}, u32[]{:S(2)}, u32[]{:S(2)}) %collective-permute-start.18) | collective-permute-done | bytes 32800 | tf_op jit(solution)/shard_map/ppermute | solution.py:509
  63.9 7.8 %shard_map.90 = (f32[4,4,64,128]{3,2,1,0:T(8,128)S(1)}, bf16[4,4,64,128]{3,2,1,0:T(8,128)(2,1)S(1)}, bf16[224,128]{1,0:T(8,128)(2,1)S(1)}, f32[16,128]{1,0:T(8,128)}) custom-call(s32[32,128]{1,0:T(8,128)S(1)} %bitcast.6, s32[8]{0:T(128)S(1)} %copy-done.1, bf16[128,128,128]{2,1,0:T(8,128)(2,1)S(1)} %get-tuple-element.35.refs_1_.refs_2_, ...), custom_call_target="tpu_custom_call" | custom-call | flops 16777216 | bytes 1048576 | tf_op jit(solution)/shard_map/pallas_call | solution.py:58
  72.2 1.1 %collective-permute-done.22.both_in = bf16[224,128]{1,0:T(8,128)(2,1)S(1)} collective-permute-done((bf16[224,128]{1,0:T(8,128)(2,1)S(1)}, bf16[224,128]{1,0:T(8,128)(2,1)S(1)}, u32[]{:S(2)}, u32[]{:S(2)}) %collective-permute-start.22) | collective-permute-done | bytes 57376 | tf_op jit(solution)/shard_map/ppermute | solution.py:495
  73.5 2.0 %collective-permute-start.29 = (bf16[256,128]{1,0:T(8,128)(2,1)S(1)}, bf16[256,128]{1,0:T(8,128)(2,1)S(1)}, u32[]{:S(2)}, u32[]{:S(2)}) collective-permute-start(bf16[256,128]{1,0:T(8,128)(2,1)S(1)} %get-tuple-element.59), channel_id=1, source_target_pairs={{0,2},{1,3},{2,4},{3,5},{4,6},{5,7},{6,0},{7,1},{8,10},{9,11},{10,... | collective-permute-start | bytes 196616 | tf_op jit(solution)/shard_map/ppermute | solution.py:509
  75.5 1.5 %collective-permute-start.23 = (bf16[224,128]{1,0:T(8,128)(2,1)S(1)}, bf16[224,128]{1,0:T(8,128)(2,1)S(1)}, u32[]{:S(2)}, u32[]{:S(2)}) collective-permute-start(bf16[224,128]{1,0:T(8,128)(2,1)S(1)} %get-tuple-element.54.refs_1_), channel_id=1, source_target_pairs={{0,2},{1,3},{2,4},{3,5},{4,6},{5,7},{6,0},{7,1},{8,10},{9,11},{10,... | collective-permute-start | bytes 172040 | tf_op jit(solution)/shard_map/ppermute | solution.py:509
  78.1 2.3 %collective-permute-start.31 = (bf16[256,128]{1,0:T(8,128)(2,1)S(1)}, bf16[256,128]{1,0:T(8,128)(2,1)S(1)}, u32[]{:S(2)}, u32[]{:S(2)}) collective-permute-start(bf16[256,128]{1,0:T(8,128)(2,1)S(1)} %get-tuple-element.61), channel_id=1, source_target_pairs={{0,6},{1,7},{2,0},{3,1},{4,2},{5,3},{6,4},{7,5},{8,14},{9,15},{10,... | collective-permute-start | bytes 196616 | tf_op jit(solution)/shard_map/ppermute | solution.py:509
  81.2 1.3 %shard_map.92 = (f32[64,64]{1,0:T(8,128)S(1)}, f32[32,128]{1,0:T(8,128)}, f32[4,128]{1,0:T(4,128)S(1)}) custom-call(s32[8]{0:T(128)S(1)} %copy-done.1, bf16[224,128]{1,0:T(8,128)(2,1)S(1)} %get-tuple-element.54.refs_1_, bf16[224,128]{1,0:T(8,128)(2,1)S(1)} %collective-permute-done.23.refs_2_, bf16[224,128]{1,0:T(8,128)(2,1)S(1)} %collective-permute-done.24.refs_3_, ...), custom_call_target="tpu_custom_call" | custom-call | flops 16777216 | bytes 1048576 | tf_op jit(solution)/shard_map/pallas_call | solution.py:58
  82.5 2.9 %collective-permute-start.28 = (f32[64,64]{1,0:T(8,128)S(1)}, f32[64,64]{1,0:T(8,128)S(1)}, u32[]{:S(2)}, u32[]{:S(2)}) collective-permute-start(f32[64,64]{1,0:T(8,128)S(1)} %get-tuple-element.57.refs_0_), channel_id=1, source_target_pairs={{0,24},{8,0},{16,8},{24,16},{1,25},{9,1},{17,9},{25,17},{2,26},{10... | collective-permute-start | bytes 49160 | tf_op jit(solution)/shard_map/ppermute | solution.py:500
  85.4 2.0 %collective-permute-start.26 = (f32[64,64]{1,0:T(8,128)S(1)}, f32[64,64]{1,0:T(8,128)S(1)}, u32[]{:S(2)}, u32[]{:S(2)}) collective-permute-start(f32[64,64]{1,0:T(8,128)S(1)} %get-tuple-element.57.refs_0_), channel_id=1, source_target_pairs={{0,8},{8,16},{16,24},{24,0},{1,9},{9,17},{17,25},{25,1},{2,10},{10... | collective-permute-start | bytes 49160 | tf_op jit(solution)/shard_map/ppermute | solution.py:500
  87.3 2.8 %collective-permute-done.27.refs_2_ = f32[64,64]{1,0:T(8,128)S(1)} collective-permute-done((f32[64,64]{1,0:T(8,128)S(1)}, f32[64,64]{1,0:T(8,128)S(1)}, u32[]{:S(2)}, u32[]{:S(2)}) %collective-permute-start.27) | collective-permute-done | bytes 16416 | tf_op jit(solution)/shard_map/ppermute | solution.py:500
  90.2 0.9 collective-permute-done.26.refs_1_
  91.1 3.2 %shard_map.93 = f32[64,512]{1,0:T(8,128)} custom-call(f32[64,64]{1,0:T(8,128)S(1)} %get-tuple-element.57.refs_0_, f32[64,64]{1,0:T(8,128)S(1)} %collective-permute-done.26.refs_1_, f32[64,64]{1,0:T(8,128)S(1)} %collective-permute-done.27.refs_2_, f32[64,64]{1,0:T(8,128)S(1)} %collective-permute-done.28.refs_3_, ...), custom_call_target="tpu_custom_call" | custom-call | flops 16777216 | bytes 1048576 | tf_op jit(solution)/shard_map/pallas_call | solution.py:58
  (47 shorter events, 8.8 us)
Async XLA Ops:
  2.2 7.6 %collective-permute-start.2 = (bf16[64,512]{1,0:T(8,128)(2,1)S(1)}, bf16[64,512]{1,0:T(8,128)(2,1)S(1)}, u32[]{:S(2)}, u32[]{:S(2)}) collective-permute-start(bf16[64,512]{1,0:T(8,128)(2,1)S(1)} %shard_map.85.refs_0_), channel_id=1, source_target_pairs={{0,24},{8,0},{16,8},{24,16},{1,25},{9,1},{17,9},{25,17},{2,26},{10... | collective-permute-start | bytes 196616 | tf_op jit(solution)/shard_map/ppermute | solution.py:500
  7.3 6.5 %collective-permute-start.1 = (bf16[64,512]{1,0:T(8,128)(2,1)S(1)}, bf16[64,512]{1,0:T(8,128)(2,1)S(1)}, u32[]{:S(2)}, u32[]{:S(2)}) collective-permute-start(bf16[64,512]{1,0:T(8,128)(2,1)S(1)} %shard_map.85.refs_0_), channel_id=1, source_target_pairs={{0,16},{8,24},{16,0},{24,8},{1,17},{9,25},{17,1},{25,9},{2,18},{10... | collective-permute-start | bytes 196616 | tf_op jit(solution)/shard_map/ppermute | solution.py:500
  7.3 6.5 %collective-permute-start = (bf16[64,512]{1,0:T(8,128)(2,1)S(1)}, bf16[64,512]{1,0:T(8,128)(2,1)S(1)}, u32[]{:S(2)}, u32[]{:S(2)}) collective-permute-start(bf16[64,512]{1,0:T(8,128)(2,1)S(1)} %shard_map.85.refs_0_), channel_id=1, source_target_pairs={{0,8},{8,16},{16,24},{24,0},{1,9},{9,17},{17,25},{25,1},{2,10},{10... | collective-permute-start | bytes 196616 | tf_op jit(solution)/shard_map/ppermute | solution.py:500
  13.8 3.7 %collective-permute-start.3 = (bf16[4,64,512]{2,1,0:T(8,128)(2,1)S(1)}, bf16[4,64,512]{2,1,0:T(8,128)(2,1)S(1)}, u32[]{:S(2)}, u32[]{:S(2)}) collective-permute-start(bf16[4,64,512]{2,1,0:T(8,128)(2,1)S(1)} %get-tuple-element.34.stack), channel_id=1, source_target_pairs={{0,1},{1,0},{2,3},{3,2},{4,5},{5,4},{6,7},{7,6},{8,9},{9,8},{10,11... | collective-permute-start | bytes 786440 | tf_op jit(solution)/shard_map/ppermute | solution.py:495
  13.9 11.1 %collective-permute-start.6 = (bf16[4,64,512]{2,1,0:T(8,128)(2,1)S(1)}, bf16[4,64,512]{2,1,0:T(8,128)(2,1)S(1)}, u32[]{:S(2)}, u32[]{:S(2)}) collective-permute-start(bf16[4,64,512]{2,1,0:T(8,128)(2,1)S(1)} %get-tuple-element.34.stack), channel_id=1, source_target_pairs={{0,6},{1,7},{2,0},{3,1},{4,2},{5,3},{6,4},{7,5},{8,14},{9,15},{10,... | collective-permute-start | bytes 786440 | tf_op jit(solution)/shard_map/ppermute | solution.py:509
  16.4 14.0 %collective-permute-start.5 = (bf16[4,64,512]{2,1,0:T(8,128)(2,1)S(1)}, bf16[4,64,512]{2,1,0:T(8,128)(2,1)S(1)}, u32[]{:S(2)}, u32[]{:S(2)}) collective-permute-start(bf16[4,64,512]{2,1,0:T(8,128)(2,1)S(1)} %get-tuple-element.34.stack), channel_id=1, source_target_pairs={{0,4},{1,5},{2,6},{3,7},{4,0},{5,1},{6,2},{7,3},{8,12},{9,13},{10,... | collective-permute-start | bytes 786440 | tf_op jit(solution)/shard_map/ppermute | solution.py:509
  16.9 13.5 %collective-permute-start.4 = (bf16[4,64,512]{2,1,0:T(8,128)(2,1)S(1)}, bf16[4,64,512]{2,1,0:T(8,128)(2,1)S(1)}, u32[]{:S(2)}, u32[]{:S(2)}) collective-permute-start(bf16[4,64,512]{2,1,0:T(8,128)(2,1)S(1)} %get-tuple-element.34.stack), channel_id=1, source_target_pairs={{0,2},{1,3},{2,4},{3,5},{4,6},{5,7},{6,0},{7,1},{8,10},{9,11},{10,... | collective-permute-start | bytes 786440 | tf_op jit(solution)/shard_map/ppermute | solution.py:509
  23.0 7.4 %collective-permute-start.9 = (bf16[64,512]{1,0:T(8,128)(2,1)}, bf16[64,512]{1,0:T(8,128)(2,1)S(1)}, u32[]{:S(2)}, u32[]{:S(2)}) collective-permute-start(bf16[64,512]{1,0:T(8,128)(2,1)} %refs_8_), channel_id=1, source_target_pairs={{0,24},{8,0},{16,8},{24,16},{1,25},{9,1},{17,9},{25,17},{2,26},{10... | collective-permute-start | bytes 196616 | tf_op jit(solution)/shard_map/ppermute | solution.py:500
  24.9 6.8 %collective-permute-start.8 = (bf16[64,512]{1,0:T(8,128)(2,1)}, bf16[64,512]{1,0:T(8,128)(2,1)S(1)}, u32[]{:S(2)}, u32[]{:S(2)}) collective-permute-start(bf16[64,512]{1,0:T(8,128)(2,1)} %refs_8_), channel_id=1, source_target_pairs={{0,16},{8,24},{16,0},{24,8},{1,17},{9,25},{17,1},{25,9},{2,18},{10... | collective-permute-start | bytes 196616 | tf_op jit(solution)/shard_map/ppermute | solution.py:500
  24.9 6.8 %collective-permute-start.7 = (bf16[64,512]{1,0:T(8,128)(2,1)}, bf16[64,512]{1,0:T(8,128)(2,1)S(1)}, u32[]{:S(2)}, u32[]{:S(2)}) collective-permute-start(bf16[64,512]{1,0:T(8,128)(2,1)} %refs_8_), channel_id=1, source_target_pairs={{0,8},{8,16},{16,24},{24,0},{1,9},{9,17},{17,25},{25,1},{2,10},{10... | collective-permute-start | bytes 196616 | tf_op jit(solution)/shard_map/ppermute | solution.py:500
  31.7 1.5 %collective-permute-start.10 = (bf16[4,64,512]{2,1,0:T(8,128)(2,1)S(1)}, bf16[4,64,512]{2,1,0:T(8,128)(2,1)S(1)}, u32[]{:S(2)}, u32[]{:S(2)}) collective-permute-start(bf16[4,64,512]{2,1,0:T(8,128)(2,1)S(1)} %collective-permute-done.4.refs_5_), channel_id=1, source_target_pairs={{0,1},{1,0},{2,3},{3,2},{4,5},{5,4},{6,7},{7,6},{8,9},{9,8},{10,11... | collective-permute-start | bytes 786440 | tf_op jit(solution)/shard_map/ppermute | solution.py:495
  31.7 1.9 %collective-permute-start.11 = (bf16[4,64,512]{2,1,0:T(8,128)(2,1)S(1)}, bf16[4,64,512]{2,1,0:T(8,128)(2,1)S(1)}, u32[]{:S(2)}, u32[]{:S(2)}) collective-permute-start(bf16[4,64,512]{2,1,0:T(8,128)(2,1)S(1)} %collective-permute-done.5.refs_7_), channel_id=1, source_target_pairs={{0,1},{1,0},{2,3},{3,2},{4,5},{5,4},{6,7},{7,6},{8,9},{9,8},{10,11... | collective-permute-start | bytes 786440 | tf_op jit(solution)/shard_map/ppermute | solution.py:495
  32.2 1.8 %collective-permute-start.12 = (bf16[4,64,512]{2,1,0:T(8,128)(2,1)S(1)}, bf16[4,64,512]{2,1,0:T(8,128)(2,1)S(1)}, u32[]{:S(2)}, u32[]{:S(2)}) collective-permute-start(bf16[4,64,512]{2,1,0:T(8,128)(2,1)S(1)} %collective-permute-done.6.refs_9_), channel_id=1, source_target_pairs={{0,1},{1,0},{2,3},{3,2},{4,5},{5,4},{6,7},{7,6},{8,9},{9,8},{10,11... | collective-permute-start | bytes 786440 | tf_op jit(solution)/shard_map/ppermute | solution.py:495
  40.5 1.4 %collective-permute-start.13 = (f32[128,128]{1,0:T(8,128)S(1)}, f32[128,128]{1,0:T(8,128)S(1)}, u32[]{:S(2)}, u32[]{:S(2)}) collective-permute-start(f32[128,128]{1,0:T(8,128)S(1)} %get-tuple-element.46), channel_id=1, source_target_pairs={{0,1},{1,0},{2,3},{3,2},{4,5},{5,4},{6,7},{7,6},{8,9},{9,8},{10,11... | collective-permute-start | bytes 196616 | tf_op jit(solution)/shard_map/ppermute | solution.py:495
  41.9 4.1 %collective-permute-start.16 = (bf16[128,128]{1,0:T(8,128)(2,1)S(1)}, bf16[128,128]{1,0:T(8,128)(2,1)S(1)}, u32[]{:S(2)}, u32[]{:S(2)}) collective-permute-start(bf16[128,128]{1,0:T(8,128)(2,1)S(1)} %add_convert_fusion.1.refs_3_), channel_id=1, source_target_pairs={{0,6},{1,7},{2,0},{3,1},{4,2},{5,3},{6,4},{7,5},{8,14},{9,15},{10,... | collective-permute-start | bytes 98312 | tf_op jit(solution)/shard_map/ppermute | solution.py:509
  44.3 3.9 %collective-permute-start.15 = (bf16[128,128]{1,0:T(8,128)(2,1)S(1)}, bf16[128,128]{1,0:T(8,128)(2,1)S(1)}, u32[]{:S(2)}, u32[]{:S(2)}) collective-permute-start(bf16[128,128]{1,0:T(8,128)(2,1)S(1)} %add_convert_fusion.1.refs_3_), channel_id=1, source_target_pairs={{0,4},{1,5},{2,6},{3,7},{4,0},{5,1},{6,2},{7,3},{8,12},{9,13},{10,... | collective-permute-start | bytes 98312 | tf_op jit(solution)/shard_map/ppermute | solution.py:509
  45.5 4.8 %collective-permute-start.14 = (bf16[128,128]{1,0:T(8,128)(2,1)S(1)}, bf16[128,128]{1,0:T(8,128)(2,1)S(1)}, u32[]{:S(2)}, u32[]{:S(2)}) collective-permute-start(bf16[128,128]{1,0:T(8,128)(2,1)S(1)} %add_convert_fusion.1.refs_3_), channel_id=1, source_target_pairs={{0,2},{1,3},{2,4},{3,5},{4,6},{5,7},{6,0},{7,1},{8,10},{9,11},{10,... | collective-permute-start | bytes 98312 | tf_op jit(solution)/shard_map/ppermute | solution.py:509
  56.8 1.3 %collective-permute-start.17 = (f32[128,128]{1,0:T(8,128)S(1)}, f32[128,128]{1,0:T(8,128)S(1)}, u32[]{:S(2)}, u32[]{:S(2)}) collective-permute-start(f32[128,128]{1,0:T(8,128)S(1)} %shard_map.89), channel_id=1, source_target_pairs={{0,1},{1,0},{2,3},{3,2},{4,5},{5,4},{6,7},{7,6},{8,9},{9,8},{10,11... | collective-permute-start | bytes 196616 | tf_op jit(solution)/shard_map/ppermute | solution.py:495
  58.1 4.0 %collective-permute-start.20 = (bf16[128,128]{1,0:T(8,128)(2,1)S(1)}, bf16[128,128]{1,0:T(8,128)(2,1)S(1)}, u32[]{:S(2)}, u32[]{:S(2)}) collective-permute-start(bf16[128,128]{1,0:T(8,128)(2,1)S(1)} %add_convert_fusion.refs_4_), channel_id=1, source_target_pairs={{0,6},{1,7},{2,0},{3,1},{4,2},{5,3},{6,4},{7,5},{8,14},{9,15},{10,... | collective-permute-start | bytes 98312 | tf_op jit(solution)/shard_map/ppermute | solution.py:509
  58.2 4.0 %collective-permute-start.19 = (bf16[128,128]{1,0:T(8,128)(2,1)S(1)}, bf16[128,128]{1,0:T(8,128)(2,1)S(1)}, u32[]{:S(2)}, u32[]{:S(2)}) collective-permute-start(bf16[128,128]{1,0:T(8,128)(2,1)S(1)} %add_convert_fusion.refs_4_), channel_id=1, source_target_pairs={{0,4},{1,5},{2,6},{3,7},{4,0},{5,1},{6,2},{7,3},{8,12},{9,13},{10,... | collective-permute-start | bytes 98312 | tf_op jit(solution)/shard_map/ppermute | solution.py:509
  59.1 4.8 %collective-permute-start.18 = (bf16[128,128]{1,0:T(8,128)(2,1)S(1)}, bf16[128,128]{1,0:T(8,128)(2,1)S(1)}, u32[]{:S(2)}, u32[]{:S(2)}) collective-permute-start(bf16[128,128]{1,0:T(8,128)(2,1)S(1)} %add_convert_fusion.refs_4_), channel_id=1, source_target_pairs={{0,2},{1,3},{2,4},{3,5},{4,6},{5,7},{6,0},{7,1},{8,10},{9,11},{10,... | collective-permute-start | bytes 98312 | tf_op jit(solution)/shard_map/ppermute | solution.py:509
  71.7 1.6 %collective-permute-start.21 = (bf16[4,4,64,128]{3,2,1,0:T(8,128)(2,1)S(1)}, bf16[4,4,64,128]{3,2,1,0:T(8,128)(2,1)S(1)}, u32[]{:S(2)}, u32[]{:S(2)}) collective-permute-start(bf16[4,4,64,128]{3,2,1,0:T(8,128)(2,1)S(1)} %get-tuple-element.52), channel_id=1, source_target_pairs={{0,1},{1,0},{2,3},{3,2},{4,5},{5,4},{6,7},{7,6},{8,9},{9,8},{10,11... | collective-permute-start | bytes 786440 | tf_op jit(solution)/shard_map/ppermute | solution.py:495
  71.7 1.6 %collective-permute-start.22 = (bf16[224,128]{1,0:T(8,128)(2,1)S(1)}, bf16[224,128]{1,0:T(8,128)(2,1)S(1)}, u32[]{:S(2)}, u32[]{:S(2)}) collective-permute-start(bf16[224,128]{1,0:T(8,128)(2,1)S(1)} %get-tuple-element.53.both), channel_id=1, source_target_pairs={{0,1},{1,0},{2,3},{3,2},{4,5},{5,4},{6,7},{7,6},{8,9},{9,8},{10,11... | collective-permute-start | bytes 172040 | tf_op jit(solution)/shard_map/ppermute | solution.py:495
  73.4 4.7 %collective-permute-start.25 = (bf16[224,128]{1,0:T(8,128)(2,1)S(1)}, bf16[224,128]{1,0:T(8,128)(2,1)S(1)}, u32[]{:S(2)}, u32[]{:S(2)}) collective-permute-start(bf16[224,128]{1,0:T(8,128)(2,1)S(1)} %get-tuple-element.54.refs_1_), channel_id=1, source_target_pairs={{0,6},{1,7},{2,0},{3,1},{4,2},{5,3},{6,4},{7,5},{8,14},{9,15},{10,... | collective-permute-start | bytes 172040 | tf_op jit(solution)/shard_map/ppermute | solution.py:509
  73.5 11.9 %collective-permute-start.29 = (bf16[256,128]{1,0:T(8,128)(2,1)S(1)}, bf16[256,128]{1,0:T(8,128)(2,1)S(1)}, u32[]{:S(2)}, u32[]{:S(2)}) collective-permute-start(bf16[256,128]{1,0:T(8,128)(2,1)S(1)} %get-tuple-element.59), channel_id=1, source_target_pairs={{0,2},{1,3},{2,4},{3,5},{4,6},{5,7},{6,0},{7,1},{8,10},{9,11},{10,... | collective-permute-start | bytes 196616 | tf_op jit(solution)/shard_map/ppermute | solution.py:509
  75.5 5.7 %collective-permute-start.24 = (bf16[224,128]{1,0:T(8,128)(2,1)S(1)}, bf16[224,128]{1,0:T(8,128)(2,1)S(1)}, u32[]{:S(2)}, u32[]{:S(2)}) collective-permute-start(bf16[224,128]{1,0:T(8,128)(2,1)S(1)} %get-tuple-element.54.refs_1_), channel_id=1, source_target_pairs={{0,4},{1,5},{2,6},{3,7},{4,0},{5,1},{6,2},{7,3},{8,12},{9,13},{10,... | collective-permute-start | bytes 172040 | tf_op jit(solution)/shard_map/ppermute | solution.py:509
  75.5 5.7 %collective-permute-start.23 = (bf16[224,128]{1,0:T(8,128)(2,1)S(1)}, bf16[224,128]{1,0:T(8,128)(2,1)S(1)}, u32[]{:S(2)}, u32[]{:S(2)}) collective-permute-start(bf16[224,128]{1,0:T(8,128)(2,1)S(1)} %get-tuple-element.54.refs_1_), channel_id=1, source_target_pairs={{0,2},{1,3},{2,4},{3,5},{4,6},{5,7},{6,0},{7,1},{8,10},{9,11},{10,... | collective-permute-start | bytes 172040 | tf_op jit(solution)/shard_map/ppermute | solution.py:509
  77.0 10.3 %collective-permute-start.30 = (bf16[256,128]{1,0:T(8,128)(2,1)S(1)}, bf16[256,128]{1,0:T(8,128)(2,1)S(1)}, u32[]{:S(2)}, u32[]{:S(2)}) collective-permute-start(bf16[256,128]{1,0:T(8,128)(2,1)S(1)} %get-tuple-element.60), channel_id=1, source_target_pairs={{0,4},{1,5},{2,6},{3,7},{4,0},{5,1},{6,2},{7,3},{8,12},{9,13},{10,... | collective-permute-start | bytes 196616 | tf_op jit(solution)/shard_map/ppermute | solution.py:509
  78.1 9.2 %collective-permute-start.31 = (bf16[256,128]{1,0:T(8,128)(2,1)S(1)}, bf16[256,128]{1,0:T(8,128)(2,1)S(1)}, u32[]{:S(2)}, u32[]{:S(2)}) collective-permute-start(bf16[256,128]{1,0:T(8,128)(2,1)S(1)} %get-tuple-element.61), channel_id=1, source_target_pairs={{0,6},{1,7},{2,0},{3,1},{4,2},{5,3},{6,4},{7,5},{8,14},{9,15},{10,... | collective-permute-start | bytes 196616 | tf_op jit(solution)/shard_map/ppermute | solution.py:509
  82.5 4.9 %collective-permute-start.28 = (f32[64,64]{1,0:T(8,128)S(1)}, f32[64,64]{1,0:T(8,128)S(1)}, u32[]{:S(2)}, u32[]{:S(2)}) collective-permute-start(f32[64,64]{1,0:T(8,128)S(1)} %get-tuple-element.57.refs_0_), channel_id=1, source_target_pairs={{0,24},{8,0},{16,8},{24,16},{1,25},{9,1},{17,9},{25,17},{2,26},{10... | collective-permute-start | bytes 49160 | tf_op jit(solution)/shard_map/ppermute | solution.py:500
  85.4 4.8 %collective-permute-start.27 = (f32[64,64]{1,0:T(8,128)S(1)}, f32[64,64]{1,0:T(8,128)S(1)}, u32[]{:S(2)}, u32[]{:S(2)}) collective-permute-start(f32[64,64]{1,0:T(8,128)S(1)} %get-tuple-element.57.refs_0_), channel_id=1, source_target_pairs={{0,16},{8,24},{16,0},{24,8},{1,17},{9,25},{17,1},{25,9},{2,18},{10... | collective-permute-start | bytes 49160 | tf_op jit(solution)/shard_map/ppermute | solution.py:500
  85.4 5.7 %collective-permute-start.26 = (f32[64,64]{1,0:T(8,128)S(1)}, f32[64,64]{1,0:T(8,128)S(1)}, u32[]{:S(2)}, u32[]{:S(2)}) collective-permute-start(f32[64,64]{1,0:T(8,128)S(1)} %get-tuple-element.57.refs_0_), channel_id=1, source_target_pairs={{0,8},{8,16},{16,24},{24,0},{1,9},{9,17},{17,25},{25,1},{2,10},{10... | collective-permute-start | bytes 49160 | tf_op jit(solution)/shard_map/ppermute | solution.py:500
  (2 other events, 92.9 us)

commit v2 on v1

--- a/solution.py
+++ b/solution.py
@@ -98,13 +98,13 @@
     return lax.axis_index("row"), lax.axis_index("col")
 
 
-def stack_kernel(pcs, *refs):
-    packs, (stack, table) = refs[:-2], refs[-2:]
-    n = len(packs)
+def stack_kernel(pcs, n, *refs):
+    packs, (rest, table) = refs[:n], refs[-2:]
     me_row, _ = places()
     first = FEAT - 16
     for k, pack in enumerate(packs):
-        stack[k] = pack[...]
+        if k:
+            rest[k - 1] = pack[...]
         rows = pack[first:, 0:BLK].astype(F32)
         rows = pltpu.roll(rows, 16 - (pcs + 8 - first), 0)
         table[shifted(me_row, k, n)] = rows[0:8].astype(jnp.int32)
@@ -233,33 +233,37 @@
     slot_loop(step, tile.total, 1, BUILD_GROUP)
 
 
-def fill_rows(pcs, stacks, row_prof, row_inv, offset):
+def piece_block(pieces, k, j):
+    lanes = slice(j * BLK, (j + 1) * BLK)
+    return pieces[0][:, lanes] if k == 0 else pieces[1][k - 1, :, lanes]
+
+
+def fill_rows(pcs, sources, row_prof, row_inv, offset):
     me_row, me_col = places()
-    n_row = stacks[0].shape[0]
-    per = stacks[0].shape[2] // BLK
-    for i, stack in enumerate(stacks):
+    n_row = sources[0][1].shape[0] + 1
+    per = sources[0][0].shape[1] // BLK
+    for i, pieces in enumerate(sources):
         core = lax.rem(me_col + i, 2)
         for k in range(n_row):
             piece = core * n_row + shifted(me_row, k, n_row)
             for j in range(per):
-                block = stack[k, :, j * BLK : (j + 1) * BLK]
+                block = piece_block(pieces, k, j)
                 row_prof[offset + piece * per + j] = block
                 width = block.astype(F32)[pcs + 6 : pcs + 7, :]
                 row_inv[offset + piece * per + j] = jnp.broadcast_to(1.0 / width, (8, BLK))
 
 
-def own_kernel(
-    pcs, table, stack, other, tile, col_prof, col_inv, sums, row_prof, row_inv, acc
-):
-    n_row = stack.shape[0]
-    per = stack.shape[2] // BLK
+def own_kernel(pcs, table, pack, rest, pack_in, rest_in, *refs):
+    tile, col_prof, col_inv, sums, row_prof, row_inv, acc = refs
+    n_row = rest.shape[0] + 1
+    per = pack.shape[1] // BLK
     me_row, _ = places()
-    fill_rows(pcs, [stack, other], row_prof, row_inv, 0)
+    fill_rows(pcs, [(pack, rest), (pack_in, rest_in)], row_prof, row_inv, 0)
     rows = lax.broadcasted_iota(jnp.int32, (FEAT, BLK), 0)
     for k in range(n_row):
         piece = shifted(me_row, k, n_row)
         for j in range(per):
-            block = stack[k, :, j * BLK : (j + 1) * BLK].astype(F32)
+            block = piece_block((pack, rest), k, j).astype(F32)
             turned = jnp.where(rows < pcs, -2.0 * block, 0.0)
             turned = jnp.where((rows >= pcs) & (rows < pcs + 3), 1.0, turned)
             turned = jnp.where(
@@ -294,13 +298,13 @@
 
 def strip_kernel(pcs, n_row, *refs):
     table, own, col_prof, col_inv, own_sums = refs[:5]
-    stacks = refs[5 : 5 + 2 * n_row - 2]
+    sources = [refs[i : i + 2] for i in range(5, 5 + 4 * (n_row - 1), 2)]
     others, out, row_prof, row_inv, wide, row_acc, col_acc = refs[-7:]
     row_blocks = row_prof.shape[0] // (n_row - 1)
     tiles = [Tile(table, n_row, k, own, others) for k in range(n_row)]
     for k in range(1, n_row):
         first = (k - 1) * row_blocks
-        fill_rows(pcs, stacks[2 * k - 2 : 2 * k], row_prof, row_inv, first)
+        fill_rows(pcs, sources[2 * k - 2 : 2 * k], row_prof, row_inv, first)
     for k in range(1, n_row):
         first = (k - 1) * row_blocks
         build(tiles[k], first, row_prof, row_inv, col_prof, col_inv)
@@ -333,10 +337,10 @@
 
 def last_kernel(n_row, n_chip, n_land, *refs):
     table, marks, own, others = refs[:4]
-    parts, bases = refs[4 : 4 + n_chip], refs[4 + n_chip : 4 + n_chip + n_row]
+    parts, bases = refs[4 : 4 + n_chip], refs[4 + n_chip]
     keep, away, both, scaling_out, stage, row_left, col_acc, scaled, acc = refs[-9:]
-    cols = bases[0].shape[0]
-    per = bases[0].shape[1] // BLK
+    cols = bases.shape[1]
+    per = bases.shape[2] // BLK
     blocks = 2 * n_chip * per
     me_row, me_col = places()
     tiles = [Tile(table, n_row, k, own, others) for k in range(n_row)]
@@ -344,9 +348,9 @@
     scaling = SCALE / column_totals(tiles, row_left, col_acc, blocks)
     scaling_out[...] = scaling
     for k in range(n_row):
-        piece = shifted(me_row, k, n_row)
+        piece = lax.bitwise_xor(me_row, k)
         for j in range(per):
-            block = bases[k][:, j * BLK : (j + 1) * BLK].astype(F32)
+            block = bases[k, :, j * BLK : (j + 1) * BLK].astype(F32)
             b = piece * per + j
             scaled[b, 0:cols] = (block * scaling_out[pl.ds(b, 1), :]).astype(BF16)
     high, mid, low = split3(scaling)
@@ -551,14 +555,16 @@
             pltpu.SemaphoreType.DMA((3,)),
         ],
     )
-    stack, table = call(
-        functools.partial(stack_kernel, pcs),
-        [shape(n_row, FEAT, share, dtype=BF16), shape(n_row, 8, BLK, dtype=jnp.int32)],
-        vec(*shifts(packed, "row")),
+    near = [chip_shift(packed, k) for k in range(1, n_chip)]
+    rest, table = call(
+        functools.partial(stack_kernel, pcs, n_row),
+        [shape(n_row - 1, FEAT, share, dtype=BF16), shape(n_row, 8, BLK, dtype=jnp.int32)],
+        vec(*shifts(packed, "row")) + [("near", pack) for pack in near],
     )
     table = ("smem", table.reshape(n_row * 8, BLK))
     marks = ("smem", landmarks)
-    far = [chip_shift(stack, k) for k in range(1, n_chip)]
+    far = [chip_shift(rest, k) for k in range(1, n_chip)]
+    bases = swap(basis, "row", 1)
     own, col_prof, col_inv, sums = call(
         functools.partial(own_kernel, pcs),
         [
@@ -567,17 +573,22 @@
             pltpu.VMEM((col_blocks, BLK, BLK), F32),
             shape(col_blocks, BLK),
         ],
-        [table] + vec(stack, sibling(stack)),
+        [table] + vec(packed, rest, sibling(packed), sibling(rest)),
         [
             pltpu.VMEM((row_blocks, FEAT, BLK), BF16),
             pltpu.VMEM((row_blocks, 8, BLK), F32),
             pltpu.VMEM((col_blocks + 1, 8, BLK), F32),
         ],
     )
-    basis, sums = lax.optimization_barrier((basis, sums))
-    bases = shifts(basis, "row")
     far, sums, bases = lax.optimization_barrier((far, sums, bases))
-    stacks = [x for pack in far for x in (pack, sibling(pack))]
+    bases = jnp.stack([basis, bases])
+    span = 2
+    while span < n_row:
+        bases = jnp.concatenate([bases, swap(bases, "row", span)])
+        span *= 2
+    stacks = []
+    for pack, group in zip(near, far):
+        stacks += [pack, group, sibling(pack), sibling(group)]
     far_slots = (n_row - 1) * slots
     others, part = call(
         functools.partial(strip_kernel, pcs, n_row),
@@ -601,7 +612,7 @@
         (part,) = call(
             functools.partial(sweep_kernel, n_row, n_chip),
             [shape(all_rows, BLK)],
-            [table] + tiles + vec(*chip_parts(part)),
+            [table] + tiles + vec(*chip_parts(part)) + [("near", bases)],
             [
                 pltpu.VMEM((n_chip, all_rows, BLK), F32),
                 pltpu.VMEM((2, all_rows, PIECES, 2 * BLK), BF16),
@@ -619,7 +630,7 @@
             shape(both_rows, BLK, dtype=BF16),
             shape(col_blocks, BLK),
         ],
-        [table, marks] + tiles + vec(*chip_parts(part), *bases),
+        [table, marks] + tiles + vec(*chip_parts(part), bases),
         [
             pltpu.VMEM((n_chip, all_rows, BLK), F32),
             pltpu.VMEM((2, all_rows, PIECES, 2 * BLK), BF16),

time: 94.6 us -> 93.3 us (0.986)
  waiting for transfers between devices: 28.2 us -> 22.6 us
  starting transfers between devices: 33 us -> 35.6 us
  other arithmetic: 0.02 us -> 1.74 us
    ppermute x15 -> x18, waiting for transfers between devices: 12.6 us -> 6.1 us  [chip_shift(): lax.ppermute(x, 'col', [(2 * q + p, 2 * ((q + k) % n) + p) for q in range...]
    ppermute x15 -> x18, starting transfers between devices: 16.5 us -> 22.7 us  [chip_shift(): lax.ppermute(x, 'col', [(2 * q + p, 2 * ((q + k) % n) + p) for q in range...]
    ppermute x8 -> x14, waiting for transfers between devices: 5.03 us -> 10.7 us  [swap(): lax.ppermute(x, axis, [(i, i ^ k) for i in range(lax.axis_size(axis))])]
    ppermute x9 -> x6, starting transfers between devices: 14.8 us -> 9.34 us  [shift(): return lax.ppermute(x, axis, [(i, (i + k) % n) for i in range(n)])]
    ppermute x9 -> x6, waiting for transfers between devices: 10.6 us -> 5.71 us  [shift(): return lax.ppermute(x, axis, [(i, (i + k) % n) for i in range(n)])]
    ppermute x8 -> x14, starting transfers between devices: 1.64 us -> 3.51 us  [swap(): lax.ppermute(x, axis, [(i, i ^ k) for i in range(lax.axis_size(axis))])]
  transfers between devices with their start and end apart: 32 -> 38, of which waited for: 20 -> 17; matrix products, arithmetic and copies ran while one was open for 0% -> 2% of each run, Pallas kernels for 7% -> 7%
where the time goes in v2:
time: 93.3 us; the launch traced here: 93 us
  starting transfers between devices  35.6 us (38%)
  Pallas kernels  31.7 us (34%)
  waiting for transfers between devices  22.6 us (24%)
  other arithmetic  1.74 us (2%)
  between operations  1.44 us (2%)
    pallas_call x9, Pallas kernels, call(): pl.pallas_call(kernel, out_shape=tuple(outs), in_specs=specs, out_specs=t...  31.7 us
    ppermute x18, starting transfers between devices, chip_shift(): lax.ppermute(x, 'col', [(2 * q + p, 2 * ((q + k) % n) + p) for q in range...  22.7 us
    ppermute x14, waiting for transfers between devices, swap(): lax.ppermute(x, axis, [(i, i ^ k) for i in range(lax.axis_size(axis))])  10.7 us
    ppermute x6, starting transfers between devices, shift(): return lax.ppermute(x, axis, [(i, (i + k) % n) for i in range(n)])  9.34 us
    ppermute x18, waiting for transfers between devices, chip_shift(): lax.ppermute(x, 'col', [(2 * q + p, 2 * ((q + k) % n) + p) for q in range...  6.1 us
    ppermute x6, waiting for transfers between devices, shift(): return lax.ppermute(x, axis, [(i, (i + k) % n) for i in range(n)])  5.71 us
    ppermute x14, starting transfers between devices, swap(): lax.ppermute(x, axis, [(i, i ^ k) for i in range(lax.axis_size(axis))])  3.51 us
  transfers between devices with their start and end apart: 38, of which 17 were waited for; matrix products, arithmetic and copies ran while one was open for 2% of the time, Pallas kernels for 7%

profile of v2, /device:TPU:0, one launch (start us, length us, event | category | flops | bytes accessed | tf_op | source)
XLA Modules:
  0.0 93.0 jit_solution(12168806819052103306)
XLA Ops:
  2.2 3.0 %collective-permute-start.3 = (bf16[64,512]{1,0:T(8,128)(2,1)S(1)}, bf16[64,512]{1,0:T(8,128)(2,1)S(1)}, u32[]{:S(2)}, u32[]{:S(2)}) collective-permute-start(bf16[64,512]{1,0:T(8,128)(2,1)S(1)} %shard_map.85.refs_0_.pack), channel_id=1, source_target_pairs={{0,2},{1,3},{2,4},{3,5},{4,6},{5,7},{6,0},{7,1},{8,10},{9,11},{10,... | collective-permute-start | bytes 196616 | tf_op jit(solution)/shard_map/ppermute | solution.py:513
  5.2 1.5 %collective-permute-start.4 = (bf16[64,512]{1,0:T(8,128)(2,1)S(1)}, bf16[64,512]{1,0:T(8,128)(2,1)S(1)}, u32[]{:S(2)}, u32[]{:S(2)}) collective-permute-start(bf16[64,512]{1,0:T(8,128)(2,1)S(1)} %shard_map.85.refs_0_.pack), channel_id=1, source_target_pairs={{0,4},{1,5},{2,6},{3,7},{4,0},{5,1},{6,2},{7,3},{8,12},{9,13},{10,... | collective-permute-start | bytes 196616 | tf_op jit(solution)/shard_map/ppermute | solution.py:513
  6.7 1.4 %collective-permute-start.5 = (bf16[64,512]{1,0:T(8,128)(2,1)S(1)}, bf16[64,512]{1,0:T(8,128)(2,1)S(1)}, u32[]{:S(2)}, u32[]{:S(2)}) collective-permute-start(bf16[64,512]{1,0:T(8,128)(2,1)S(1)} %shard_map.85.refs_0_.pack), channel_id=1, source_target_pairs={{0,6},{1,7},{2,0},{3,1},{4,2},{5,3},{6,4},{7,5},{8,14},{9,15},{10,... | collective-permute-start | bytes 196616 | tf_op jit(solution)/shard_map/ppermute | solution.py:513
  8.1 1.6 %collective-permute-start = (bf16[64,512]{1,0:T(8,128)(2,1)S(1)}, bf16[64,512]{1,0:T(8,128)(2,1)S(1)}, u32[]{:S(2)}, u32[]{:S(2)}) collective-permute-start(bf16[64,512]{1,0:T(8,128)(2,1)S(1)} %shard_map.85.refs_0_.pack), channel_id=1, source_target_pairs={{0,8},{8,16},{16,24},{24,0},{1,9},{9,17},{17,25},{25,1},{2,10},{10... | collective-permute-start | bytes 196616 | tf_op jit(solution)/shard_map/ppermute | solution.py:504
  9.7 2.6 %collective-permute-start.1 = (bf16[64,512]{1,0:T(8,128)(2,1)S(1)}, bf16[64,512]{1,0:T(8,128)(2,1)S(1)}, u32[]{:S(2)}, u32[]{:S(2)}) collective-permute-start(bf16[64,512]{1,0:T(8,128)(2,1)S(1)} %shard_map.85.refs_0_.pack), channel_id=1, source_target_pairs={{0,16},{8,24},{16,0},{24,8},{1,17},{9,25},{17,1},{25,9},{2,18},{10... | collective-permute-start | bytes 196616 | tf_op jit(solution)/shard_map/ppermute | solution.py:504
  12.3 1.3 %collective-permute-start.2 = (bf16[64,512]{1,0:T(8,128)(2,1)S(1)}, bf16[64,512]{1,0:T(8,128)(2,1)S(1)}, u32[]{:S(2)}, u32[]{:S(2)}) collective-permute-start(bf16[64,512]{1,0:T(8,128)(2,1)S(1)} %shard_map.85.refs_0_.pack), channel_id=1, source_target_pairs={{0,24},{8,0},{16,8},{24,16},{1,25},{9,1},{17,9},{25,17},{2,26},{10... | collective-permute-start | bytes 196616 | tf_op jit(solution)/shard_map/ppermute | solution.py:504
  13.6 1.2 %collective-permute-done.refs_1_ = bf16[64,512]{1,0:T(8,128)(2,1)S(1)} collective-permute-done((bf16[64,512]{1,0:T(8,128)(2,1)S(1)}, bf16[64,512]{1,0:T(8,128)(2,1)S(1)}, u32[]{:S(2)}, u32[]{:S(2)}) %collective-permute-start) | collective-permute-done | bytes 65568 | tf_op jit(solution)/shard_map/ppermute | solution.py:504
  14.8 1.8 %collective-permute-done.1.refs_2_ = bf16[64,512]{1,0:T(8,128)(2,1)S(1)} collective-permute-done((bf16[64,512]{1,0:T(8,128)(2,1)S(1)}, bf16[64,512]{1,0:T(8,128)(2,1)S(1)}, u32[]{:S(2)}, u32[]{:S(2)}) %collective-permute-start.1) | collective-permute-done | bytes 65568 | tf_op jit(solution)/shard_map/ppermute | solution.py:504
  17.6 1.5 %collective-permute-start.8 = (bf16[3,64,512]{2,1,0:T(8,128)(2,1)S(1)}, bf16[3,64,512]{2,1,0:T(8,128)(2,1)S(1)}, u32[]{:S(2)}, u32[]{:S(2)}) collective-permute-start(bf16[3,64,512]{2,1,0:T(8,128)(2,1)S(1)} %get-tuple-element.29.rest), channel_id=1, source_target_pairs={{0,2},{1,3},{2,4},{3,5},{4,6},{5,7},{6,0},{7,1},{8,10},{9,11},{10,... | collective-permute-start | bytes 589832 | tf_op jit(solution)/shard_map/ppermute | solution.py:513
  19.5 1.3 %collective-permute-done.6.pack_in = bf16[64,512]{1,0:T(8,128)(2,1)S(1)} collective-permute-done((bf16[64,512]{1,0:T(8,128)(2,1)S(1)}, bf16[64,512]{1,0:T(8,128)(2,1)S(1)}, u32[]{:S(2)}, u32[]{:S(2)}) %collective-permute-start.6) | collective-permute-done | bytes 65568 | tf_op jit(solution)/shard_map/ppermute | solution.py:499
  21.7 5.5 %shard_map.87 = (bf16[128,128,128]{2,1,0:T(8,128)(2,1)S(1)}, bf16[16,128,64]{2,1,0:T(8,128)(2,1)S(1)}, f32[16,128,128]{2,1,0:T(8,128)S(1)}, f32[16,128]{1,0:T(8,128)S(1)}) custom-call(s32[32,128]{1,0:T(8,128)S(1)} %bitcast.5, bf16[64,512]{1,0:T(8,128)(2,1)S(1)} %shard_map.85.refs_0_.pack, bf16[3,64,512]{2,1,0:T(8,128)(2,1)S(1)} %get-tuple-element.29.rest, ...), custom_call_target="tpu_custom_call" | custom-call | flops 16777216 | bytes 1048576 | tf_op jit(solution)/shard_map/pallas_call | solution.py:58
  27.2 1.3 %collective-permute-done.8.refs_6_ = bf16[3,64,512]{2,1,0:T(8,128)(2,1)S(1)} collective-permute-done((bf16[3,64,512]{2,1,0:T(8,128)(2,1)S(1)}, bf16[3,64,512]{2,1,0:T(8,128)(2,1)S(1)}, u32[]{:S(2)}, u32[]{:S(2)}) %collective-permute-start.8) | collective-permute-done | bytes 196640 | tf_op jit(solution)/shard_map/ppermute | solution.py:513
  28.5 1.5 %collective-permute-done.9.refs_10_ = bf16[3,64,512]{2,1,0:T(8,128)(2,1)S(1)} collective-permute-done((bf16[3,64,512]{2,1,0:T(8,128)(2,1)S(1)}, bf16[3,64,512]{2,1,0:T(8,128)(2,1)S(1)}, u32[]{:S(2)}, u32[]{:S(2)}) %collective-permute-start.9) | collective-permute-done | bytes 196640 | tf_op jit(solution)/shard_map/ppermute | solution.py:513
  31.0 1.1 %collective-permute-done.12.refs_7_ = bf16[64,512]{1,0:T(8,128)(2,1)S(1)} collective-permute-done((bf16[64,512]{1,0:T(8,128)(2,1)S(1)}, bf16[64,512]{1,0:T(8,128)(2,1)S(1)}, u32[]{:S(2)}, u32[]{:S(2)}) %collective-permute-start.12) | collective-permute-done | bytes 65568 | tf_op jit(solution)/shard_map/ppermute | solution.py:499
  33.4 6.5 %shard_map.88 = (bf16[384,128,128]{2,1,0:T(8,128)(2,1)S(1)}, f32[128,128]{1,0:T(8,128)S(1)}) custom-call(s32[32,128]{1,0:T(8,128)S(1)} %bitcast.6, bf16[128,128,128]{2,1,0:T(8,128)(2,1)S(1)} %get-tuple-element.30.refs_1_.refs_2_, bf16[16,128,64]{2,1,0:T(8,128)(2,1)S(1)} %get-tuple-element.31.refs_2_, f32[16,128,128]{2,1,0:T(8,128)S(1)} %get-tuple-element.32.refs_3_, ...), custom_call_target="tpu_custom_call" | custom-call | flops 16777216 | bytes 1048576 | tf_op jit(solution)/shard_map/pallas_call | solution.py:58
  41.4 1.3 %collective-permute-start.19 = (bf16[128,128]{1,0:T(8,128)(2,1)S(1)}, bf16[128,128]{1,0:T(8,128)(2,1)S(1)}, u32[]{:S(2)}, u32[]{:S(2)}) collective-permute-start(bf16[128,128]{1,0:T(8,128)(2,1)S(1)} %add_convert_fusion.1.refs_3_), channel_id=1, source_target_pairs={{0,2},{1,3},{2,4},{3,5},{4,6},{5,7},{6,0},{7,1},{8,10},{9,11},{10,... | collective-permute-start | bytes 98312 | tf_op jit(solution)/shard_map/ppermute | solution.py:513
  42.8 1.5 %collective-permute-start.20 = (bf16[128,128]{1,0:T(8,128)(2,1)S(1)}, bf16[128,128]{1,0:T(8,128)(2,1)S(1)}, u32[]{:S(2)}, u32[]{:S(2)}) collective-permute-start(bf16[128,128]{1,0:T(8,128)(2,1)S(1)} %add_convert_fusion.1.refs_3_), channel_id=1, source_target_pairs={{0,4},{1,5},{2,6},{3,7},{4,0},{5,1},{6,2},{7,3},{8,12},{9,13},{10,... | collective-permute-start | bytes 98312 | tf_op jit(solution)/shard_map/ppermute | solution.py:513
  44.3 1.1 %collective-permute-start.21 = (bf16[128,128]{1,0:T(8,128)(2,1)S(1)}, bf16[128,128]{1,0:T(8,128)(2,1)S(1)}, u32[]{:S(2)}, u32[]{:S(2)}) collective-permute-start(bf16[128,128]{1,0:T(8,128)(2,1)S(1)} %add_convert_fusion.1.refs_3_), channel_id=1, source_target_pairs={{0,6},{1,7},{2,0},{3,1},{4,2},{5,3},{6,4},{7,5},{8,14},{9,15},{10,... | collective-permute-start | bytes 98312 | tf_op jit(solution)/shard_map/ppermute | solution.py:513
  45.4 5.0 %collective-permute-done.22 = bf16[2,64,512]{2,1,0:T(8,128)(2,1)S(1)} collective-permute-done((bf16[2,64,512]{2,1,0:T(8,128)(2,1)S(1)}, bf16[2,64,512]{2,1,0:T(8,128)(2,1)S(1)}, u32[]{:S(2)}, u32[]{:S(2)}) %collective-permute-start.22) | collective-permute-done | bytes 131104 | tf_op jit(solution)/shard_map/ppermute | solution.py:499
  51.4 6.4 %shard_map.89 = f32[128,128]{1,0:T(8,128)S(1)} custom-call(s32[32,128]{1,0:T(8,128)S(1)} %bitcast.7, bf16[128,128,128]{2,1,0:T(8,128)(2,1)S(1)} %get-tuple-element.30.refs_1_.refs_2_, bf16[384,128,128]{2,1,0:T(8,128)(2,1)S(1)} %get-tuple-element.38.refs_2_.refs_3_, bf16[128,128]{1,0:T(8,128)(2,1)S(1)} %add_convert_fusion.1.refs_3_, ...), custom_call_target="tpu_custom_call" | custom-call | flops 16777216 | bytes 1048576 | tf_op jit(solution)/shard_map/pallas_call | solution.py:58
  57.9 1.2 %collective-permute-done.23 = f32[128,128]{1,0:T(8,128)S(1)} collective-permute-done((f32[128,128]{1,0:T(8,128)S(1)}, f32[128,128]{1,0:T(8,128)S(1)}, u32[]{:S(2)}, u32[]{:S(2)}) %collective-permute-start.23) | collective-permute-done | bytes 65568 | tf_op jit(solution)/shard_map/ppermute | solution.py:499
  60.2 2.2 %collective-permute-start.26 = (bf16[128,128]{1,0:T(8,128)(2,1)S(1)}, bf16[128,128]{1,0:T(8,128)(2,1)S(1)}, u32[]{:S(2)}, u32[]{:S(2)}) collective-permute-start(bf16[128,128]{1,0:T(8,128)(2,1)S(1)} %add_convert_fusion.refs_4_), channel_id=1, source_target_pairs={{0,6},{1,7},{2,0},{3,1},{4,2},{5,3},{6,4},{7,5},{8,14},{9,15},{10,... | collective-permute-start | bytes 98312 | tf_op jit(solution)/shard_map/ppermute | solution.py:513
  62.4 1.6 %collective-permute-done.24.refs_5_ = bf16[128,128]{1,0:T(8,128)(2,1)S(1)} collective-permute-done((bf16[128,128]{1,0:T(8,128)(2,1)S(1)}, bf16[128,128]{1,0:T(8,128)(2,1)S(1)}, u32[]{:S(2)}, u32[]{:S(2)}) %collective-permute-start.24) | collective-permute-done | bytes 32800 | tf_op jit(solution)/shard_map/ppermute | solution.py:513
  64.6 7.8 %shard_map.90 = (f32[4,4,64,128]{3,2,1,0:T(8,128)S(1)}, bf16[4,4,64,128]{3,2,1,0:T(8,128)(2,1)S(1)}, bf16[224,128]{1,0:T(8,128)(2,1)S(1)}, f32[16,128]{1,0:T(8,128)}) custom-call(s32[32,128]{1,0:T(8,128)S(1)} %bitcast.8, s32[8]{0:T(128)S(1)} %copy-done, bf16[128,128,128]{2,1,0:T(8,128)(2,1)S(1)} %get-tuple-element.30.refs_1_.refs_2_, ...), custom_call_target="tpu_custom_call" | custom-call | flops 16777216 | bytes 1048576 | tf_op jit(solution)/shard_map/pallas_call | solution.py:58
  72.8 1.1 %collective-permute-done.28.both_in = bf16[224,128]{1,0:T(8,128)(2,1)S(1)} collective-permute-done((bf16[224,128]{1,0:T(8,128)(2,1)S(1)}, bf16[224,128]{1,0:T(8,128)(2,1)S(1)}, u32[]{:S(2)}, u32[]{:S(2)}) %collective-permute-start.28) | collective-permute-done | bytes 57376 | tf_op jit(solution)/shard_map/ppermute | solution.py:499
  75.1 2.5 %collective-permute-start.30 = (bf16[224,128]{1,0:T(8,128)(2,1)S(1)}, bf16[224,128]{1,0:T(8,128)(2,1)S(1)}, u32[]{:S(2)}, u32[]{:S(2)}) collective-permute-start(bf16[224,128]{1,0:T(8,128)(2,1)S(1)} %get-tuple-element.44.refs_1_), channel_id=1, source_target_pairs={{0,4},{1,5},{2,6},{3,7},{4,0},{5,1},{6,2},{7,3},{8,12},{9,13},{10,... | collective-permute-start | bytes 172040 | tf_op jit(solution)/shard_map/ppermute | solution.py:513
  78.2 1.8 %collective-permute-start.36 = (bf16[256,128]{1,0:T(8,128)(2,1)S(1)}, bf16[256,128]{1,0:T(8,128)(2,1)S(1)}, u32[]{:S(2)}, u32[]{:S(2)}) collective-permute-start(bf16[256,128]{1,0:T(8,128)(2,1)S(1)} %get-tuple-element.50), channel_id=1, source_target_pairs={{0,4},{1,5},{2,6},{3,7},{4,0},{5,1},{6,2},{7,3},{8,12},{9,13},{10,... | collective-permute-start | bytes 196616 | tf_op jit(solution)/shard_map/ppermute | solution.py:513
  82.2 1.3 %shard_map.92 = (f32[64,64]{1,0:T(8,128)S(1)}, f32[32,128]{1,0:T(8,128)}, f32[4,128]{1,0:T(4,128)S(1)}) custom-call(s32[8]{0:T(128)S(1)} %copy-done, bf16[224,128]{1,0:T(8,128)(2,1)S(1)} %get-tuple-element.44.refs_1_, bf16[224,128]{1,0:T(8,128)(2,1)S(1)} %collective-permute-done.29.refs_2_, bf16[224,128]{1,0:T(8,128)(2,1)S(1)} %collective-permute-done.30.refs_3_, ...), custom_call_target="tpu_custom_call" | custom-call | flops 16777216 | bytes 1048576 | tf_op jit(solution)/shard_map/pallas_call | solution.py:58
  83.5 2.3 %collective-permute-start.33 = (f32[64,64]{1,0:T(8,128)S(1)}, f32[64,64]{1,0:T(8,128)S(1)}, u32[]{:S(2)}, u32[]{:S(2)}) collective-permute-start(f32[64,64]{1,0:T(8,128)S(1)} %get-tuple-element.47.refs_0_), channel_id=1, source_target_pairs={{0,16},{8,24},{16,0},{24,8},{1,17},{9,25},{17,1},{25,9},{2,18},{10... | collective-permute-start | bytes 49160 | tf_op jit(solution)/shard_map/ppermute | solution.py:504
  85.8 1.5 %collective-permute-start.34 = (f32[64,64]{1,0:T(8,128)S(1)}, f32[64,64]{1,0:T(8,128)S(1)}, u32[]{:S(2)}, u32[]{:S(2)}) collective-permute-start(f32[64,64]{1,0:T(8,128)S(1)} %get-tuple-element.47.refs_0_), channel_id=1, source_target_pairs={{0,24},{8,0},{16,8},{24,16},{1,25},{9,1},{17,9},{25,17},{2,26},{10... | collective-permute-start | bytes 49160 | tf_op jit(solution)/shard_map/ppermute | solution.py:504
  87.3 2.0 %collective-permute-done.32.refs_1_ = f32[64,64]{1,0:T(8,128)S(1)} collective-permute-done((f32[64,64]{1,0:T(8,128)S(1)}, f32[64,64]{1,0:T(8,128)S(1)}, u32[]{:S(2)}, u32[]{:S(2)}) %collective-permute-start.32) | collective-permute-done | bytes 16416 | tf_op jit(solution)/shard_map/ppermute | solution.py:504
  89.8 3.2 %shard_map.93 = f32[64,512]{1,0:T(8,128)} custom-call(f32[64,64]{1,0:T(8,128)S(1)} %get-tuple-element.47.refs_0_, f32[64,64]{1,0:T(8,128)S(1)} %collective-permute-done.32.refs_1_, f32[64,64]{1,0:T(8,128)S(1)} %collective-permute-done.33.refs_2_, f32[64,64]{1,0:T(8,128)S(1)} %collective-permute-done.34.refs_3_, ...), custom_call_target="tpu_custom_call" | custom-call | flops 16777216 | bytes 1048576 | tf_op jit(solution)/shard_map/pallas_call | solution.py:58
  (59 shorter events, 14.6 us)
Async XLA Ops:
  2.2 10.1 %collective-permute-start.3 = (bf16[64,512]{1,0:T(8,128)(2,1)S(1)}, bf16[64,512]{1,0:T(8,128)(2,1)S(1)}, u32[]{:S(2)}, u32[]{:S(2)}) collective-permute-start(bf16[64,512]{1,0:T(8,128)(2,1)S(1)} %shard_map.85.refs_0_.pack), channel_id=1, source_target_pairs={{0,2},{1,3},{2,4},{3,5},{4,6},{5,7},{6,0},{7,1},{8,10},{9,11},{10,... | collective-permute-start | bytes 196616 | tf_op jit(solution)/shard_map/ppermute | solution.py:513
  5.2 8.5 %collective-permute-start.4 = (bf16[64,512]{1,0:T(8,128)(2,1)S(1)}, bf16[64,512]{1,0:T(8,128)(2,1)S(1)}, u32[]{:S(2)}, u32[]{:S(2)}) collective-permute-start(bf16[64,512]{1,0:T(8,128)(2,1)S(1)} %shard_map.85.refs_0_.pack), channel_id=1, source_target_pairs={{0,4},{1,5},{2,6},{3,7},{4,0},{5,1},{6,2},{7,3},{8,12},{9,13},{10,... | collective-permute-start | bytes 196616 | tf_op jit(solution)/shard_map/ppermute | solution.py:513
  6.7 7.0 %collective-permute-start.5 = (bf16[64,512]{1,0:T(8,128)(2,1)S(1)}, bf16[64,512]{1,0:T(8,128)(2,1)S(1)}, u32[]{:S(2)}, u32[]{:S(2)}) collective-permute-start(bf16[64,512]{1,0:T(8,128)(2,1)S(1)} %shard_map.85.refs_0_.pack), channel_id=1, source_target_pairs={{0,6},{1,7},{2,0},{3,1},{4,2},{5,3},{6,4},{7,5},{8,14},{9,15},{10,... | collective-permute-start | bytes 196616 | tf_op jit(solution)/shard_map/ppermute | solution.py:513
  8.1 6.7 %collective-permute-start = (bf16[64,512]{1,0:T(8,128)(2,1)S(1)}, bf16[64,512]{1,0:T(8,128)(2,1)S(1)}, u32[]{:S(2)}, u32[]{:S(2)}) collective-permute-start(bf16[64,512]{1,0:T(8,128)(2,1)S(1)} %shard_map.85.refs_0_.pack), channel_id=1, source_target_pairs={{0,8},{8,16},{16,24},{24,0},{1,9},{9,17},{17,25},{25,1},{2,10},{10... | collective-permute-start | bytes 196616 | tf_op jit(solution)/shard_map/ppermute | solution.py:504
  9.7 6.9 %collective-permute-start.1 = (bf16[64,512]{1,0:T(8,128)(2,1)S(1)}, bf16[64,512]{1,0:T(8,128)(2,1)S(1)}, u32[]{:S(2)}, u32[]{:S(2)}) collective-permute-start(bf16[64,512]{1,0:T(8,128)(2,1)S(1)} %shard_map.85.refs_0_.pack), channel_id=1, source_target_pairs={{0,16},{8,24},{16,0},{24,8},{1,17},{9,25},{17,1},{25,9},{2,18},{10... | collective-permute-start | bytes 196616 | tf_op jit(solution)/shard_map/ppermute | solution.py:504
  12.3 4.6 %collective-permute-start.2 = (bf16[64,512]{1,0:T(8,128)(2,1)S(1)}, bf16[64,512]{1,0:T(8,128)(2,1)S(1)}, u32[]{:S(2)}, u32[]{:S(2)}) collective-permute-start(bf16[64,512]{1,0:T(8,128)(2,1)S(1)} %shard_map.85.refs_0_.pack), channel_id=1, source_target_pairs={{0,24},{8,0},{16,8},{24,16},{1,25},{9,1},{17,9},{25,17},{2,26},{10... | collective-permute-start | bytes 196616 | tf_op jit(solution)/shard_map/ppermute | solution.py:504
  16.9 4.8 %collective-permute-start.7 = (bf16[3,64,512]{2,1,0:T(8,128)(2,1)S(1)}, bf16[3,64,512]{2,1,0:T(8,128)(2,1)S(1)}, u32[]{:S(2)}, u32[]{:S(2)}) collective-permute-start(bf16[3,64,512]{2,1,0:T(8,128)(2,1)S(1)} %get-tuple-element.29.rest), channel_id=1, source_target_pairs={{0,1},{1,0},{2,3},{3,2},{4,5},{5,4},{6,7},{7,6},{8,9},{9,8},{10,11... | collective-permute-start | bytes 589832 | tf_op jit(solution)/shard_map/ppermute | solution.py:499
  17.0 10.2 %collective-permute-start.10 = (bf16[3,64,512]{2,1,0:T(8,128)(2,1)S(1)}, bf16[3,64,512]{2,1,0:T(8,128)(2,1)S(1)}, u32[]{:S(2)}, u32[]{:S(2)}) collective-permute-start(bf16[3,64,512]{2,1,0:T(8,128)(2,1)S(1)} %get-tuple-element.29.rest), channel_id=1, source_target_pairs={{0,6},{1,7},{2,0},{3,1},{4,2},{5,3},{6,4},{7,5},{8,14},{9,15},{10,... | collective-permute-start | bytes 589832 | tf_op jit(solution)/shard_map/ppermute | solution.py:513
  17.6 10.9 %collective-permute-start.8 = (bf16[3,64,512]{2,1,0:T(8,128)(2,1)S(1)}, bf16[3,64,512]{2,1,0:T(8,128)(2,1)S(1)}, u32[]{:S(2)}, u32[]{:S(2)}) collective-permute-start(bf16[3,64,512]{2,1,0:T(8,128)(2,1)S(1)} %get-tuple-element.29.rest), channel_id=1, source_target_pairs={{0,2},{1,3},{2,4},{3,5},{4,6},{5,7},{6,0},{7,1},{8,10},{9,11},{10,... | collective-permute-start | bytes 589832 | tf_op jit(solution)/shard_map/ppermute | solution.py:513
  19.1 10.9 %collective-permute-start.9 = (bf16[3,64,512]{2,1,0:T(8,128)(2,1)S(1)}, bf16[3,64,512]{2,1,0:T(8,128)(2,1)S(1)}, u32[]{:S(2)}, u32[]{:S(2)}) collective-permute-start(bf16[3,64,512]{2,1,0:T(8,128)(2,1)S(1)} %get-tuple-element.29.rest), channel_id=1, source_target_pairs={{0,4},{1,5},{2,6},{3,7},{4,0},{5,1},{6,2},{7,3},{8,12},{9,13},{10,... | collective-permute-start | bytes 589832 | tf_op jit(solution)/shard_map/ppermute | solution.py:513
  20.8 6.4 %collective-permute-start.11 = (bf16[64,512]{1,0:T(8,128)(2,1)}, bf16[64,512]{1,0:T(8,128)(2,1)S(1)}, u32[]{:S(2)}, u32[]{:S(2)}) collective-permute-start(bf16[64,512]{1,0:T(8,128)(2,1)} %param.8), channel_id=1, source_target_pairs={{0,8},{8,0},{16,24},{24,16},{1,9},{9,1},{17,25},{25,17},{2,10},{10... | collective-permute-start | bytes 196616 | tf_op jit(solution)/shard_map/ppermute | solution.py:499
  30.0 3.4 %collective-permute-start.13 = (bf16[3,64,512]{2,1,0:T(8,128)(2,1)S(1)}, bf16[3,64,512]{2,1,0:T(8,128)(2,1)S(1)}, u32[]{:S(2)}, u32[]{:S(2)}) collective-permute-start(bf16[3,64,512]{2,1,0:T(8,128)(2,1)S(1)} %collective-permute-done.8.refs_6_), channel_id=1, source_target_pairs={{0,1},{1,0},{2,3},{3,2},{4,5},{5,4},{6,7},{7,6},{8,9},{9,8},{10,11... | collective-permute-start | bytes 589832 | tf_op jit(solution)/shard_map/ppermute | solution.py:499
  30.0 3.4 %collective-permute-start.15 = (bf16[3,64,512]{2,1,0:T(8,128)(2,1)S(1)}, bf16[3,64,512]{2,1,0:T(8,128)(2,1)S(1)}, u32[]{:S(2)}, u32[]{:S(2)}) collective-permute-start(bf16[3,64,512]{2,1,0:T(8,128)(2,1)S(1)} %collective-permute-done.9.refs_10_), channel_id=1, source_target_pairs={{0,1},{1,0},{2,3},{3,2},{4,5},{5,4},{6,7},{7,6},{8,9},{9,8},{10,11... | collective-permute-start | bytes 589832 | tf_op jit(solution)/shard_map/ppermute | solution.py:499
  30.5 2.9 %collective-permute-start.17 = (bf16[3,64,512]{2,1,0:T(8,128)(2,1)S(1)}, bf16[3,64,512]{2,1,0:T(8,128)(2,1)S(1)}, u32[]{:S(2)}, u32[]{:S(2)}) collective-permute-start(bf16[3,64,512]{2,1,0:T(8,128)(2,1)S(1)} %collective-permute-done.10.refs_14_), channel_id=1, source_target_pairs={{0,1},{1,0},{2,3},{3,2},{4,5},{5,4},{6,7},{7,6},{8,9},{9,8},{10,11... | collective-permute-start | bytes 589832 | tf_op jit(solution)/shard_map/ppermute | solution.py:499
  40.8 9.7 %collective-permute-start.22 = (bf16[2,64,512]{2,1,0:T(8,128)(2,1)S(1)}, bf16[2,64,512]{2,1,0:T(8,128)(2,1)S(1)}, u32[]{:S(2)}, u32[]{:S(2)}) collective-permute-start(bf16[2,64,512]{2,1,0:T(8,128)(2,1)S(1)} %pad_maximum_fusion.1), channel_id=1, source_target_pairs={{0,16},{8,24},{16,0},{24,8},{1,17},{9,25},{17,1},{25,9},{2,18},{10... | collective-permute-start | bytes 393224 | tf_op jit(solution)/shard_map/ppermute | solution.py:499
  41.4 9.9 %collective-permute-start.19 = (bf16[128,128]{1,0:T(8,128)(2,1)S(1)}, bf16[128,128]{1,0:T(8,128)(2,1)S(1)}, u32[]{:S(2)}, u32[]{:S(2)}) collective-permute-start(bf16[128,128]{1,0:T(8,128)(2,1)S(1)} %add_convert_fusion.1.refs_3_), channel_id=1, source_target_pairs={{0,2},{1,3},{2,4},{3,5},{4,6},{5,7},{6,0},{7,1},{8,10},{9,11},{10,... | collective-permute-start | bytes 98312 | tf_op jit(solution)/shard_map/ppermute | solution.py:513
  42.8 8.6 %collective-permute-start.20 = (bf16[128,128]{1,0:T(8,128)(2,1)S(1)}, bf16[128,128]{1,0:T(8,128)(2,1)S(1)}, u32[]{:S(2)}, u32[]{:S(2)}) collective-permute-start(bf16[128,128]{1,0:T(8,128)(2,1)S(1)} %add_convert_fusion.1.refs_3_), channel_id=1, source_target_pairs={{0,4},{1,5},{2,6},{3,7},{4,0},{5,1},{6,2},{7,3},{8,12},{9,13},{10,... | collective-permute-start | bytes 98312 | tf_op jit(solution)/shard_map/ppermute | solution.py:513
  44.3 7.1 %collective-permute-start.21 = (bf16[128,128]{1,0:T(8,128)(2,1)S(1)}, bf16[128,128]{1,0:T(8,128)(2,1)S(1)}, u32[]{:S(2)}, u32[]{:S(2)}) collective-permute-start(bf16[128,128]{1,0:T(8,128)(2,1)S(1)} %add_convert_fusion.1.refs_3_), channel_id=1, source_target_pairs={{0,6},{1,7},{2,0},{3,1},{4,2},{5,3},{6,4},{7,5},{8,14},{9,15},{10,... | collective-permute-start | bytes 98312 | tf_op jit(solution)/shard_map/ppermute | solution.py:513
  59.1 4.9 %collective-permute-start.24 = (bf16[128,128]{1,0:T(8,128)(2,1)S(1)}, bf16[128,128]{1,0:T(8,128)(2,1)S(1)}, u32[]{:S(2)}, u32[]{:S(2)}) collective-permute-start(bf16[128,128]{1,0:T(8,128)(2,1)S(1)} %add_convert_fusion.refs_4_), channel_id=1, source_target_pairs={{0,2},{1,3},{2,4},{3,5},{4,6},{5,7},{6,0},{7,1},{8,10},{9,11},{10,... | collective-permute-start | bytes 98312 | tf_op jit(solution)/shard_map/ppermute | solution.py:513
  59.3 4.7 %collective-permute-start.25 = (bf16[128,128]{1,0:T(8,128)(2,1)S(1)}, bf16[128,128]{1,0:T(8,128)(2,1)S(1)}, u32[]{:S(2)}, u32[]{:S(2)}) collective-permute-start(bf16[128,128]{1,0:T(8,128)(2,1)S(1)} %add_convert_fusion.refs_4_), channel_id=1, source_target_pairs={{0,4},{1,5},{2,6},{3,7},{4,0},{5,1},{6,2},{7,3},{8,12},{9,13},{10,... | collective-permute-start | bytes 98312 | tf_op jit(solution)/shard_map/ppermute | solution.py:513
  60.2 4.4 %collective-permute-start.26 = (bf16[128,128]{1,0:T(8,128)(2,1)S(1)}, bf16[128,128]{1,0:T(8,128)(2,1)S(1)}, u32[]{:S(2)}, u32[]{:S(2)}) collective-permute-start(bf16[128,128]{1,0:T(8,128)(2,1)S(1)} %add_convert_fusion.refs_4_), channel_id=1, source_target_pairs={{0,6},{1,7},{2,0},{3,1},{4,2},{5,3},{6,4},{7,5},{8,14},{9,15},{10,... | collective-permute-start | bytes 98312 | tf_op jit(solution)/shard_map/ppermute | solution.py:513
  72.3 1.6 %collective-permute-start.27 = (bf16[4,4,64,128]{3,2,1,0:T(8,128)(2,1)S(1)}, bf16[4,4,64,128]{3,2,1,0:T(8,128)(2,1)S(1)}, u32[]{:S(2)}, u32[]{:S(2)}) collective-permute-start(bf16[4,4,64,128]{3,2,1,0:T(8,128)(2,1)S(1)} %get-tuple-element.42), channel_id=1, source_target_pairs={{0,1},{1,0},{2,3},{3,2},{4,5},{5,4},{6,7},{7,6},{8,9},{9,8},{10,11... | collective-permute-start | bytes 786440 | tf_op jit(solution)/shard_map/ppermute | solution.py:499
  72.3 1.6 %collective-permute-start.28 = (bf16[224,128]{1,0:T(8,128)(2,1)S(1)}, bf16[224,128]{1,0:T(8,128)(2,1)S(1)}, u32[]{:S(2)}, u32[]{:S(2)}) collective-permute-start(bf16[224,128]{1,0:T(8,128)(2,1)S(1)} %get-tuple-element.43.both), channel_id=1, source_target_pairs={{0,1},{1,0},{2,3},{3,2},{4,5},{5,4},{6,7},{7,6},{8,9},{9,8},{10,11... | collective-permute-start | bytes 172040 | tf_op jit(solution)/shard_map/ppermute | solution.py:499
  74.0 6.0 %collective-permute-start.29 = (bf16[224,128]{1,0:T(8,128)(2,1)S(1)}, bf16[224,128]{1,0:T(8,128)(2,1)S(1)}, u32[]{:S(2)}, u32[]{:S(2)}) collective-permute-start(bf16[224,128]{1,0:T(8,128)(2,1)S(1)} %get-tuple-element.44.refs_1_), channel_id=1, source_target_pairs={{0,2},{1,3},{2,4},{3,5},{4,6},{5,7},{6,0},{7,1},{8,10},{9,11},{10,... | collective-permute-start | bytes 172040 | tf_op jit(solution)/shard_map/ppermute | solution.py:513
  75.0 10.7 %collective-permute-start.35 = (bf16[256,128]{1,0:T(8,128)(2,1)S(1)}, bf16[256,128]{1,0:T(8,128)(2,1)S(1)}, u32[]{:S(2)}, u32[]{:S(2)}) collective-permute-start(bf16[256,128]{1,0:T(8,128)(2,1)S(1)} %get-tuple-element.49), channel_id=1, source_target_pairs={{0,2},{1,3},{2,4},{3,5},{4,6},{5,7},{6,0},{7,1},{8,10},{9,11},{10,... | collective-permute-start | bytes 196616 | tf_op jit(solution)/shard_map/ppermute | solution.py:513
  75.1 6.6 %collective-permute-start.30 = (bf16[224,128]{1,0:T(8,128)(2,1)S(1)}, bf16[224,128]{1,0:T(8,128)(2,1)S(1)}, u32[]{:S(2)}, u32[]{:S(2)}) collective-permute-start(bf16[224,128]{1,0:T(8,128)(2,1)S(1)} %get-tuple-element.44.refs_1_), channel_id=1, source_target_pairs={{0,4},{1,5},{2,6},{3,7},{4,0},{5,1},{6,2},{7,3},{8,12},{9,13},{10,... | collective-permute-start | bytes 172040 | tf_op jit(solution)/shard_map/ppermute | solution.py:513
  77.6 4.6 %collective-permute-start.31 = (bf16[224,128]{1,0:T(8,128)(2,1)S(1)}, bf16[224,128]{1,0:T(8,128)(2,1)S(1)}, u32[]{:S(2)}, u32[]{:S(2)}) collective-permute-start(bf16[224,128]{1,0:T(8,128)(2,1)S(1)} %get-tuple-element.44.refs_1_), channel_id=1, source_target_pairs={{0,6},{1,7},{2,0},{3,1},{4,2},{5,3},{6,4},{7,5},{8,14},{9,15},{10,... | collective-permute-start | bytes 172040 | tf_op jit(solution)/shard_map/ppermute | solution.py:513
  78.2 9.1 %collective-permute-start.36 = (bf16[256,128]{1,0:T(8,128)(2,1)S(1)}, bf16[256,128]{1,0:T(8,128)(2,1)S(1)}, u32[]{:S(2)}, u32[]{:S(2)}) collective-permute-start(bf16[256,128]{1,0:T(8,128)(2,1)S(1)} %get-tuple-element.50), channel_id=1, source_target_pairs={{0,4},{1,5},{2,6},{3,7},{4,0},{5,1},{6,2},{7,3},{8,12},{9,13},{10,... | collective-permute-start | bytes 196616 | tf_op jit(solution)/shard_map/ppermute | solution.py:513
  80.0 7.3 %collective-permute-start.37 = (bf16[256,128]{1,0:T(8,128)(2,1)S(1)}, bf16[256,128]{1,0:T(8,128)(2,1)S(1)}, u32[]{:S(2)}, u32[]{:S(2)}) collective-permute-start(bf16[256,128]{1,0:T(8,128)(2,1)S(1)} %get-tuple-element.51), channel_id=1, source_target_pairs={{0,6},{1,7},{2,0},{3,1},{4,2},{5,3},{6,4},{7,5},{8,14},{9,15},{10,... | collective-permute-start | bytes 196616 | tf_op jit(solution)/shard_map/ppermute | solution.py:513
  83.5 5.8 %collective-permute-start.32 = (f32[64,64]{1,0:T(8,128)S(1)}, f32[64,64]{1,0:T(8,128)S(1)}, u32[]{:S(2)}, u32[]{:S(2)}) collective-permute-start(f32[64,64]{1,0:T(8,128)S(1)} %get-tuple-element.47.refs_0_), channel_id=1, source_target_pairs={{0,8},{8,16},{16,24},{24,0},{1,9},{9,17},{17,25},{25,1},{2,10},{10... | collective-permute-start | bytes 49160 | tf_op jit(solution)/shard_map/ppermute | solution.py:504
  83.5 5.8 %collective-permute-start.33 = (f32[64,64]{1,0:T(8,128)S(1)}, f32[64,64]{1,0:T(8,128)S(1)}, u32[]{:S(2)}, u32[]{:S(2)}) collective-permute-start(f32[64,64]{1,0:T(8,128)S(1)} %get-tuple-element.47.refs_0_), channel_id=1, source_target_pairs={{0,16},{8,24},{16,0},{24,8},{1,17},{9,25},{17,1},{25,9},{2,18},{10... | collective-permute-start | bytes 49160 | tf_op jit(solution)/shard_map/ppermute | solution.py:504
  85.8 4.0 %collective-permute-start.34 = (f32[64,64]{1,0:T(8,128)S(1)}, f32[64,64]{1,0:T(8,128)S(1)}, u32[]{:S(2)}, u32[]{:S(2)}) collective-permute-start(f32[64,64]{1,0:T(8,128)S(1)} %get-tuple-element.47.refs_0_), channel_id=1, source_target_pairs={{0,24},{8,0},{16,8},{24,16},{1,25},{9,1},{17,9},{25,17},{2,26},{10... | collective-permute-start | bytes 49160 | tf_op jit(solution)/shard_map/ppermute | solution.py:504
  (7 other events, 39.5 us)

commit v3 on v2

--- a/solution.py
+++ b/solution.py
@@ -14,6 +14,7 @@
 TILE_GROUP = 16
 ROWS, COLUMNS, COUNT = 0, 1, 2
 FEAT = 64
+PACK = 56
 PIECES = 16
 SCALE = 512.0
 LOG2E = 1.4426950408889634
@@ -87,10 +88,13 @@
     work[pcs : pcs + 1, :] = high
     work[pcs + 1 : pcs + 2, :] = mid
     work[pcs + 2 : pcs + 3, :] = low
-    work[pcs + 3 : pcs + 6, :] = jnp.ones((3, prof.shape[1]), F32)
-    work[pcs + 6 : pcs + 7, :] = width_ref[...].astype(F32).reshape(1, -1)
-    work[pcs + 8 : pcs + 10, 0:BLK] = lists_ref[0, 0].astype(F32)
-    work[pcs + 10 : pcs + 11, 0:BLK] = jnp.full((1, BLK), counts[0, 0], jnp.int32).astype(F32)
+    work[pcs + 3 : pcs + 4, :] = width_ref[...].astype(F32).reshape(1, -1)
+    lists = lists_ref[0, 0].astype(F32)
+    slots = slice(pcs + 4, pcs + 5)
+    work[slots, 0:BLK] = lists[0:1]
+    work[slots, BLK : 2 * BLK] = lists[1:2]
+    count = jnp.full((1, BLK), counts[0, 0], jnp.int32)
+    work[slots, 2 * BLK : 3 * BLK] = count.astype(F32)
     out_ref[...] = work[...].astype(BF16)
 
 
@@ -101,13 +105,13 @@
 def stack_kernel(pcs, n, *refs):
     packs, (rest, table) = refs[:n], refs[-2:]
     me_row, _ = places()
-    first = FEAT - 16
     for k, pack in enumerate(packs):
         if k:
             rest[k - 1] = pack[...]
-        rows = pack[first:, 0:BLK].astype(F32)
-        rows = pltpu.roll(rows, 16 - (pcs + 8 - first), 0)
-        table[shifted(me_row, k, n)] = rows[0:8].astype(jnp.int32)
+        slots = pack[:, 0 : 3 * BLK].astype(F32)[pcs + 4 : pcs + 5]
+        for row in (ROWS, COLUMNS, COUNT):
+            values = slots[:, row * BLK : (row + 1) * BLK].astype(jnp.int32)
+            table[shifted(me_row, k, n), row : row + 1] = values
 
 
 def slot_loop(step, count, size, group):
@@ -242,19 +246,22 @@
     me_row, me_col = places()
     n_row = sources[0][1].shape[0] + 1
     per = sources[0][0].shape[1] // BLK
+    ones = lax.broadcasted_iota(jnp.int32, (FEAT - PACK, BLK), 0) < 3
+    ones = ones.astype(F32)
     for i, pieces in enumerate(sources):
         core = lax.rem(me_col + i, 2)
         for k in range(n_row):
             piece = core * n_row + shifted(me_row, k, n_row)
             for j in range(per):
-                block = piece_block(pieces, k, j)
-                row_prof[offset + piece * per + j] = block
-                width = block.astype(F32)[pcs + 6 : pcs + 7, :]
+                block = piece_block(pieces, k, j).astype(F32)
+                whole = jnp.concatenate([block, ones], axis=0)
+                row_prof[offset + piece * per + j] = whole.astype(BF16)
+                width = block[pcs + 3 : pcs + 4, :]
                 row_inv[offset + piece * per + j] = jnp.broadcast_to(1.0 / width, (8, BLK))
 
 
 def own_kernel(pcs, table, pack, rest, pack_in, rest_in, *refs):
-    tile, col_prof, col_inv, sums, row_prof, row_inv, acc = refs
+    tile, col_prof, col_inv, sums, row_prof, row_inv, acc = refs[-7:]
     n_row = rest.shape[0] + 1
     per = pack.shape[1] // BLK
     me_row, _ = places()
@@ -264,16 +271,17 @@
         piece = shifted(me_row, k, n_row)
         for j in range(per):
             block = piece_block((pack, rest), k, j).astype(F32)
+            block = jnp.concatenate([block, jnp.zeros((FEAT - PACK, BLK), F32)], axis=0)
             turned = jnp.where(rows < pcs, -2.0 * block, 0.0)
             turned = jnp.where((rows >= pcs) & (rows < pcs + 3), 1.0, turned)
+            turned = jnp.where(rows == PACK - 1, pltpu.roll(block, PACK - 4 - pcs, 0), turned)
             turned = jnp.where(
-                (rows >= pcs + 3) & (rows < pcs + 6), pltpu.roll(block, 3, 0), turned
+                (rows >= PACK) & (rows < PACK + 3), pltpu.roll(block, PACK - pcs, 0), turned
             )
-            turned = jnp.where(rows == pcs + 7, pltpu.roll(block, 1, 0), turned)
             turned = turned.T
             col_prof[piece * per + j] = turned.astype(BF16)
             col_inv[piece * per + j] = jnp.broadcast_to(
-                -LOG2E / turned[:, pcs + 7 : pcs + 8], (BLK, BLK)
+                -LOG2E / turned[:, PACK - 1 : PACK], (BLK, BLK)
             )
     own = Tile(table, n_row, 0, tile, None)
     build(own, 0, row_prof, row_inv, col_prof, col_inv)
@@ -337,10 +345,10 @@
 
 def last_kernel(n_row, n_chip, n_land, *refs):
     table, marks, own, others = refs[:4]
-    parts, bases = refs[4 : 4 + n_chip], refs[4 + n_chip]
+    parts, bases = refs[4 : 4 + n_chip], refs[4 + n_chip : 4 + n_chip + n_row]
     keep, away, both, scaling_out, stage, row_left, col_acc, scaled, acc = refs[-9:]
-    cols = bases.shape[1]
-    per = bases.shape[2] // BLK
+    cols = bases[0].shape[0]
+    per = bases[0].shape[1] // BLK
     blocks = 2 * n_chip * per
     me_row, me_col = places()
     tiles = [Tile(table, n_row, k, own, others) for k in range(n_row)]
@@ -348,9 +356,9 @@
     scaling = SCALE / column_totals(tiles, row_left, col_acc, blocks)
     scaling_out[...] = scaling
     for k in range(n_row):
-        piece = lax.bitwise_xor(me_row, k)
+        piece = shifted(me_row, k, n_row)
         for j in range(per):
-            block = bases[k, :, j * BLK : (j + 1) * BLK].astype(F32)
+            block = bases[k][:, j * BLK : (j + 1) * BLK].astype(F32)
             b = piece * per + j
             scaled[b, 0:cols] = (block * scaling_out[pl.ds(b, 1), :]).astype(BF16)
     high, mid, low = split3(scaling)
@@ -545,10 +553,10 @@
 
     (packed,) = call(
         pack_kernel,
-        [shape(FEAT, share, dtype=BF16)],
+        [shape(PACK, share, dtype=BF16)],
         [("hbm", a) for a in (profiles, cell_width, block_lists)] + [("smem", block_counts)],
         [
-            pltpu.VMEM((FEAT, share), F32),
+            pltpu.VMEM((PACK, share), F32),
             pltpu.VMEM(profiles.shape, BF16),
             pltpu.VMEM(cell_width.shape, BF16),
             pltpu.VMEM(block_lists.shape, jnp.int32),
@@ -556,15 +564,15 @@
         ],
     )
     near = [chip_shift(packed, k) for k in range(1, n_chip)]
+    near_in = [sibling(pack) for pack in near]
     rest, table = call(
         functools.partial(stack_kernel, pcs, n_row),
-        [shape(n_row - 1, FEAT, share, dtype=BF16), shape(n_row, 8, BLK, dtype=jnp.int32)],
-        vec(*shifts(packed, "row")) + [("near", pack) for pack in near],
+        [shape(n_row - 1, PACK, share, dtype=BF16), shape(n_row, 8, BLK, dtype=jnp.int32)],
+        vec(*shifts(packed, "row")) + [("near", pack) for pack in near_in],
     )
     table = ("smem", table.reshape(n_row * 8, BLK))
     marks = ("smem", landmarks)
     far = [chip_shift(rest, k) for k in range(1, n_chip)]
-    bases = swap(basis, "row", 1)
     own, col_prof, col_inv, sums = call(
         functools.partial(own_kernel, pcs),
         [
@@ -580,15 +588,13 @@
             pltpu.VMEM((col_blocks + 1, 8, BLK), F32),
         ],
     )
-    far, sums, bases = lax.optimization_barrier((far, sums, bases))
-    bases = jnp.stack([basis, bases])
-    span = 2
-    while span < n_row:
-        bases = jnp.concatenate([bases, swap(bases, "row", span)])
-        span *= 2
+    basis, sums = lax.optimization_barrier((basis, sums))
+    bases = shifts(basis, "row")
+    far, sums = lax.optimization_barrier((far, sums))
+    far[-1], bases = lax.optimization_barrier((far[-1], bases))
     stacks = []
-    for pack, group in zip(near, far):
-        stacks += [pack, group, sibling(pack), sibling(group)]
+    for pack, other, group in zip(near, near_in, far):
+        stacks += [pack, group, other, sibling(group)]
     far_slots = (n_row - 1) * slots
     others, part = call(
         functools.partial(strip_kernel, pcs, n_row),
@@ -612,7 +618,7 @@
         (part,) = call(
             functools.partial(sweep_kernel, n_row, n_chip),
             [shape(all_rows, BLK)],
-            [table] + tiles + vec(*chip_parts(part)) + [("near", bases)],
+            [table] + tiles + vec(*chip_parts(part)),
             [
                 pltpu.VMEM((n_chip, all_rows, BLK), F32),
                 pltpu.VMEM((2, all_rows, PIECES, 2 * BLK), BF16),
@@ -630,7 +636,7 @@
             shape(both_rows, BLK, dtype=BF16),
             shape(col_blocks, BLK),
         ],
-        [table, marks] + tiles + vec(*chip_parts(part), bases),
+        [table, marks] + tiles + vec(*chip_parts(part), *bases),
         [
             pltpu.VMEM((n_chip, all_rows, BLK), F32),
             pltpu.VMEM((2, all_rows, PIECES, 2 * BLK), BF16),

time: 93.3 us -> 98.3 us (1.054)
  waiting for transfers between devices: 22.6 us -> 28.9 us
  other arithmetic: 1.74 us -> 0.02 us
    ppermute x6 -> x9, waiting for transfers between devices: 5.71 us -> 13.8 us  [shift(): return lax.ppermute(x, axis, [(i, (i + k) % n) for i in range(n)])]
    ppermute x14 -> x12, waiting for transfers between devices: 10.7 us -> 6.23 us  [swap(): lax.ppermute(x, axis, [(i, i ^ k) for i in range(lax.axis_size(axis))])]
    ppermute x18, waiting for transfers between devices: 6.1 us -> 8.9 us  [chip_shift(): lax.ppermute(x, 'col', [(2 * q + p, 2 * ((q + k) % n) + p) for q in range...]
    ppermute x6 -> x9, starting transfers between devices: 9.34 us -> 11.5 us  [shift(): return lax.ppermute(x, axis, [(i, (i + k) % n) for i in range(n)])]
    ppermute x14 -> x12, starting transfers between devices: 3.51 us -> 1.75 us  [swap(): lax.ppermute(x, axis, [(i, i ^ k) for i in range(lax.axis_size(axis))])]
  transfers between devices with their start and end apart: 38 -> 39, of which waited for: 17 -> 21; matrix products, arithmetic and copies ran while one was open for 2% -> 0% of each run, Pallas kernels for 7% -> 7%
where the time goes in v3:
time: 98.3 us; the launch traced here: 98 us
  starting transfers between devices  35.7 us (36%)
  Pallas kernels  32 us (33%)
  waiting for transfers between devices  28.9 us (29%)
  between operations  1.43 us (1%)
    pallas_call x9, Pallas kernels, call(): pl.pallas_call(kernel, out_shape=tuple(outs), in_specs=specs, out_specs=t...  32 us
    ppermute x18, starting transfers between devices, chip_shift(): lax.ppermute(x, 'col', [(2 * q + p, 2 * ((q + k) % n) + p) for q in range...  22.4 us
    ppermute x9, waiting for transfers between devices, shift(): return lax.ppermute(x, axis, [(i, (i + k) % n) for i in range(n)])  13.8 us
    ppermute x9, starting transfers between devices, shift(): return lax.ppermute(x, axis, [(i, (i + k) % n) for i in range(n)])  11.5 us
    ppermute x18, waiting for transfers between devices, chip_shift(): lax.ppermute(x, 'col', [(2 * q + p, 2 * ((q + k) % n) + p) for q in range...  8.9 us
    ppermute x12, waiting for transfers between devices, swap(): lax.ppermute(x, axis, [(i, i ^ k) for i in range(lax.axis_size(axis))])  6.23 us
  transfers between devices with their start and end apart: 39, of which 21 were waited for; matrix products, arithmetic and copies ran while one was open for 0% of the time, Pallas kernels for 7%

profile of v3, /device:TPU:0, one launch (start us, length us, event | category | flops | bytes accessed | tf_op | source)
XLA Modules:
  0.0 98.0 jit_solution(6930963113056765581)
XLA Ops:
  2.2 3.9 %collective-permute-start.7 = (bf16[56,512]{1,0:T(8,128)(2,1)S(1)}, bf16[56,512]{1,0:T(8,128)(2,1)S(1)}, u32[]{:S(2)}, u32[]{:S(2)}) collective-permute-start(bf16[56,512]{1,0:T(8,128)(2,1)S(1)} %shard_map.85.refs_0_.pack), channel_id=1, source_target_pairs={{0,6},{1,7},{2,0},{3,1},{4,2},{5,3},{6,4},{7,5},{8,14},{9,15},{10,... | collective-permute-start | bytes 172040 | tf_op jit(solution)/shard_map/ppermute | solution.py:521
  7.2 3.6 %collective-permute-start.2 = (bf16[56,512]{1,0:T(8,128)(2,1)S(1)}, bf16[56,512]{1,0:T(8,128)(2,1)S(1)}, u32[]{:S(2)}, u32[]{:S(2)}) collective-permute-start(bf16[56,512]{1,0:T(8,128)(2,1)S(1)} %shard_map.85.refs_0_.pack), channel_id=1, source_target_pairs={{0,24},{8,0},{16,8},{24,16},{1,25},{9,1},{17,9},{25,17},{2,26},{10... | collective-permute-start | bytes 172040 | tf_op jit(solution)/shard_map/ppermute | solution.py:512
  10.8 1.0 %collective-permute-start = (bf16[56,512]{1,0:T(8,128)(2,1)S(1)}, bf16[56,512]{1,0:T(8,128)(2,1)S(1)}, u32[]{:S(2)}, u32[]{:S(2)}) collective-permute-start(bf16[56,512]{1,0:T(8,128)(2,1)S(1)} %shard_map.85.refs_0_.pack), channel_id=1, source_target_pairs={{0,8},{8,16},{16,24},{24,0},{1,9},{9,17},{17,25},{25,1},{2,10},{10... | collective-permute-start | bytes 172040 | tf_op jit(solution)/shard_map/ppermute | solution.py:512
  12.7 3.2 %collective-permute-done.1.refs_2_ = bf16[56,512]{1,0:T(8,128)(2,1)S(1)} collective-permute-done((bf16[56,512]{1,0:T(8,128)(2,1)S(1)}, bf16[56,512]{1,0:T(8,128)(2,1)S(1)}, u32[]{:S(2)}, u32[]{:S(2)}) %collective-permute-start.1) | collective-permute-done | bytes 57376 | tf_op jit(solution)/shard_map/ppermute | solution.py:512
  17.0 2.4 %collective-permute-start.13 = (bf16[3,56,512]{2,1,0:T(8,128)(2,1)S(1)}, bf16[3,56,512]{2,1,0:T(8,128)(2,1)S(1)}, u32[]{:S(2)}, u32[]{:S(2)}) collective-permute-start(bf16[3,56,512]{2,1,0:T(8,128)(2,1)S(1)} %get-tuple-element.35.rest), channel_id=1, source_target_pairs={{0,6},{1,7},{2,0},{3,1},{4,2},{5,3},{6,4},{7,5},{8,14},{9,15},{10,... | collective-permute-start | bytes 516104 | tf_op jit(solution)/shard_map/ppermute | solution.py:521
  19.3 1.5 %collective-permute-start.12 = (bf16[3,56,512]{2,1,0:T(8,128)(2,1)S(1)}, bf16[3,56,512]{2,1,0:T(8,128)(2,1)S(1)}, u32[]{:S(2)}, u32[]{:S(2)}) collective-permute-start(bf16[3,56,512]{2,1,0:T(8,128)(2,1)S(1)} %get-tuple-element.35.rest), channel_id=1, source_target_pairs={{0,4},{1,5},{2,6},{3,7},{4,0},{5,1},{6,2},{7,3},{8,12},{9,13},{10,... | collective-permute-start | bytes 516104 | tf_op jit(solution)/shard_map/ppermute | solution.py:521
  20.9 1.2 %collective-permute-done.9.pack_in = bf16[56,512]{1,0:T(8,128)(2,1)S(1)} collective-permute-done((bf16[56,512]{1,0:T(8,128)(2,1)S(1)}, bf16[56,512]{1,0:T(8,128)(2,1)S(1)}, u32[]{:S(2)}, u32[]{:S(2)}) %collective-permute-start.9) | collective-permute-done | bytes 57376 | tf_op jit(solution)/shard_map/ppermute | solution.py:507
  22.1 5.5 %shard_map.87 = (bf16[128,128,128]{2,1,0:T(8,128)(2,1)S(1)}, bf16[16,128,64]{2,1,0:T(8,128)(2,1)S(1)}, f32[16,128,128]{2,1,0:T(8,128)S(1)}, f32[16,128]{1,0:T(8,128)S(1)}) custom-call(s32[32,128]{1,0:T(8,128)S(1)} %bitcast.3, bf16[56,512]{1,0:T(8,128)(2,1)S(1)} %shard_map.85.refs_0_.pack, bf16[3,56,512]{2,1,0:T(8,128)(2,1)S(1)} %get-tuple-element.35.rest, ...), custom_call_target="tpu_custom_call" | custom-call | flops 16777216 | bytes 1048576 | tf_op jit(solution)/shard_map/pallas_call | solution.py:59
  27.6 1.5 %collective-permute-start.18 = (bf16[64,512]{1,0:T(8,128)(2,1)}, bf16[64,512]{1,0:T(8,128)(2,1)S(1)}, u32[]{:S(2)}, u32[]{:S(2)}) collective-permute-start(bf16[64,512]{1,0:T(8,128)(2,1)} %refs_8_), channel_id=1, source_target_pairs={{0,24},{8,0},{16,8},{24,16},{1,25},{9,1},{17,9},{25,17},{2,26},{10... | collective-permute-start | bytes 196616 | tf_op jit(solution)/shard_map/ppermute | solution.py:512
  29.1 1.7 %collective-permute-start.16 = (bf16[64,512]{1,0:T(8,128)(2,1)}, bf16[64,512]{1,0:T(8,128)(2,1)S(1)}, u32[]{:S(2)}, u32[]{:S(2)}) collective-permute-start(bf16[64,512]{1,0:T(8,128)(2,1)} %refs_8_), channel_id=1, source_target_pairs={{0,8},{8,16},{16,24},{24,0},{1,9},{9,17},{17,25},{25,1},{2,10},{10... | collective-permute-start | bytes 196616 | tf_op jit(solution)/shard_map/ppermute | solution.py:512
  32.2 4.8 %collective-permute-done.17.refs_10_ = bf16[64,512]{1,0:T(8,128)(2,1)S(1)} collective-permute-done((bf16[64,512]{1,0:T(8,128)(2,1)}, bf16[64,512]{1,0:T(8,128)(2,1)S(1)}, u32[]{:S(2)}, u32[]{:S(2)}) %collective-permute-start.17) | collective-permute-done | bytes 65568 | tf_op jit(solution)/shard_map/ppermute | solution.py:512
  36.9 1.4 %collective-permute-done.19.refs_16_ = bf16[3,56,512]{2,1,0:T(8,128)(2,1)S(1)} collective-permute-done((bf16[3,56,512]{2,1,0:T(8,128)(2,1)S(1)}, bf16[3,56,512]{2,1,0:T(8,128)(2,1)S(1)}, u32[]{:S(2)}, u32[]{:S(2)}) %collective-permute-start.19) | collective-permute-done | bytes 172064 | tf_op jit(solution)/shard_map/ppermute | solution.py:507
  38.3 6.7 %shard_map.88 = (bf16[384,128,128]{2,1,0:T(8,128)(2,1)S(1)}, f32[128,128]{1,0:T(8,128)S(1)}) custom-call(s32[32,128]{1,0:T(8,128)S(1)} %bitcast.4, bf16[128,128,128]{2,1,0:T(8,128)(2,1)S(1)} %get-tuple-element.36.refs_1_.refs_2_, bf16[16,128,64]{2,1,0:T(8,128)(2,1)S(1)} %get-tuple-element.37.refs_2_, f32[16,128,128]{2,1,0:T(8,128)S(1)} %get-tuple-element.38.refs_3_, ...), custom_call_target="tpu_custom_call" | custom-call | flops 16777216 | bytes 1048576 | tf_op jit(solution)/shard_map/pallas_call | solution.py:59
  45.1 1.2 %collective-permute-done.20 = f32[128,128]{1,0:T(8,128)S(1)} collective-permute-done((f32[128,128]{1,0:T(8,128)S(1)}, f32[128,128]{1,0:T(8,128)S(1)}, u32[]{:S(2)}, u32[]{:S(2)}) %collective-permute-start.20) | collective-permute-done | bytes 65568 | tf_op jit(solution)/shard_map/ppermute | solution.py:507
  46.4 2.8 %collective-permute-start.23 = (bf16[128,128]{1,0:T(8,128)(2,1)S(1)}, bf16[128,128]{1,0:T(8,128)(2,1)S(1)}, u32[]{:S(2)}, u32[]{:S(2)}) collective-permute-start(bf16[128,128]{1,0:T(8,128)(2,1)S(1)} %add_convert_fusion.1.refs_3_), channel_id=1, source_target_pairs={{0,6},{1,7},{2,0},{3,1},{4,2},{5,3},{6,4},{7,5},{8,14},{9,15},{10,... | collective-permute-start | bytes 98312 | tf_op jit(solution)/shard_map/ppermute | solution.py:521
  50.8 2.7 %collective-permute-done.22.refs_5_ = bf16[128,128]{1,0:T(8,128)(2,1)S(1)} collective-permute-done((bf16[128,128]{1,0:T(8,128)(2,1)S(1)}, bf16[128,128]{1,0:T(8,128)(2,1)S(1)}, u32[]{:S(2)}, u32[]{:S(2)}) %collective-permute-start.22) | collective-permute-done | bytes 32800 | tf_op jit(solution)/shard_map/ppermute | solution.py:521
  53.4 1.0 %collective-permute-done.21.refs_4_ = bf16[128,128]{1,0:T(8,128)(2,1)S(1)} collective-permute-done((bf16[128,128]{1,0:T(8,128)(2,1)S(1)}, bf16[128,128]{1,0:T(8,128)(2,1)S(1)}, u32[]{:S(2)}, u32[]{:S(2)}) %collective-permute-start.21) | collective-permute-done | bytes 32800 | tf_op jit(solution)/shard_map/ppermute | solution.py:521
  54.5 6.5 %shard_map.89 = f32[128,128]{1,0:T(8,128)S(1)} custom-call(s32[32,128]{1,0:T(8,128)S(1)} %bitcast.5, bf16[128,128,128]{2,1,0:T(8,128)(2,1)S(1)} %get-tuple-element.36.refs_1_.refs_2_, bf16[384,128,128]{2,1,0:T(8,128)(2,1)S(1)} %get-tuple-element.47.refs_2_.refs_3_, bf16[128,128]{1,0:T(8,128)(2,1)S(1)} %add_convert_fusion.1.refs_3_, ...), custom_call_target="tpu_custom_call" | custom-call | flops 16777216 | bytes 1048576 | tf_op jit(solution)/shard_map/pallas_call | solution.py:59
  61.0 1.2 %collective-permute-done.24 = f32[128,128]{1,0:T(8,128)S(1)} collective-permute-done((f32[128,128]{1,0:T(8,128)S(1)}, f32[128,128]{1,0:T(8,128)S(1)}, u32[]{:S(2)}, u32[]{:S(2)}) %collective-permute-start.24) | collective-permute-done | bytes 65568 | tf_op jit(solution)/shard_map/ppermute | solution.py:507
  62.4 1.5 %collective-permute-start.26 = (bf16[128,128]{1,0:T(8,128)(2,1)S(1)}, bf16[128,128]{1,0:T(8,128)(2,1)S(1)}, u32[]{:S(2)}, u32[]{:S(2)}) collective-permute-start(bf16[128,128]{1,0:T(8,128)(2,1)S(1)} %add_convert_fusion.refs_4_), channel_id=1, source_target_pairs={{0,4},{1,5},{2,6},{3,7},{4,0},{5,1},{6,2},{7,3},{8,12},{9,13},{10,... | collective-permute-start | bytes 98312 | tf_op jit(solution)/shard_map/ppermute | solution.py:521
  64.0 1.9 %collective-permute-start.25 = (bf16[128,128]{1,0:T(8,128)(2,1)S(1)}, bf16[128,128]{1,0:T(8,128)(2,1)S(1)}, u32[]{:S(2)}, u32[]{:S(2)}) collective-permute-start(bf16[128,128]{1,0:T(8,128)(2,1)S(1)} %add_convert_fusion.refs_4_), channel_id=1, source_target_pairs={{0,2},{1,3},{2,4},{3,5},{4,6},{5,7},{6,0},{7,1},{8,10},{9,11},{10,... | collective-permute-start | bytes 98312 | tf_op jit(solution)/shard_map/ppermute | solution.py:521
  66.3 2.4 %collective-permute-done.25.refs_5_ = bf16[128,128]{1,0:T(8,128)(2,1)S(1)} collective-permute-done((bf16[128,128]{1,0:T(8,128)(2,1)S(1)}, bf16[128,128]{1,0:T(8,128)(2,1)S(1)}, u32[]{:S(2)}, u32[]{:S(2)}) %collective-permute-start.25) | collective-permute-done | bytes 32800 | tf_op jit(solution)/shard_map/ppermute | solution.py:521
  68.8 7.8 %shard_map.90 = (f32[4,4,64,128]{3,2,1,0:T(8,128)S(1)}, bf16[4,4,64,128]{3,2,1,0:T(8,128)(2,1)S(1)}, bf16[224,128]{1,0:T(8,128)(2,1)S(1)}, f32[16,128]{1,0:T(8,128)}) custom-call(s32[32,128]{1,0:T(8,128)S(1)} %bitcast.6, s32[8]{0:T(128)S(1)} %copy-done.1, bf16[128,128,128]{2,1,0:T(8,128)(2,1)S(1)} %get-tuple-element.36.refs_1_.refs_2_, ...), custom_call_target="tpu_custom_call" | custom-call | flops 16777216 | bytes 1048576 | tf_op jit(solution)/shard_map/pallas_call | solution.py:59
  77.1 1.1 %collective-permute-done.29.both_in = bf16[224,128]{1,0:T(8,128)(2,1)S(1)} collective-permute-done((bf16[224,128]{1,0:T(8,128)(2,1)S(1)}, bf16[224,128]{1,0:T(8,128)(2,1)S(1)}, u32[]{:S(2)}, u32[]{:S(2)}) %collective-permute-start.29) | collective-permute-done | bytes 57376 | tf_op jit(solution)/shard_map/ppermute | solution.py:507
  78.3 2.0 %collective-permute-start.36 = (bf16[256,128]{1,0:T(8,128)(2,1)S(1)}, bf16[256,128]{1,0:T(8,128)(2,1)S(1)}, u32[]{:S(2)}, u32[]{:S(2)}) collective-permute-start(bf16[256,128]{1,0:T(8,128)(2,1)S(1)} %get-tuple-element.61), channel_id=1, source_target_pairs={{0,2},{1,3},{2,4},{3,5},{4,6},{5,7},{6,0},{7,1},{8,10},{9,11},{10,... | collective-permute-start | bytes 196616 | tf_op jit(solution)/shard_map/ppermute | solution.py:521
  80.3 1.5 %collective-permute-start.30 = (bf16[224,128]{1,0:T(8,128)(2,1)S(1)}, bf16[224,128]{1,0:T(8,128)(2,1)S(1)}, u32[]{:S(2)}, u32[]{:S(2)}) collective-permute-start(bf16[224,128]{1,0:T(8,128)(2,1)S(1)} %get-tuple-element.56.refs_1_), channel_id=1, source_target_pairs={{0,2},{1,3},{2,4},{3,5},{4,6},{5,7},{6,0},{7,1},{8,10},{9,11},{10,... | collective-permute-start | bytes 172040 | tf_op jit(solution)/shard_map/ppermute | solution.py:521
  83.0 2.3 %collective-permute-start.38 = (bf16[256,128]{1,0:T(8,128)(2,1)S(1)}, bf16[256,128]{1,0:T(8,128)(2,1)S(1)}, u32[]{:S(2)}, u32[]{:S(2)}) collective-permute-start(bf16[256,128]{1,0:T(8,128)(2,1)S(1)} %get-tuple-element.63), channel_id=1, source_target_pairs={{0,6},{1,7},{2,0},{3,1},{4,2},{5,3},{6,4},{7,5},{8,14},{9,15},{10,... | collective-permute-start | bytes 196616 | tf_op jit(solution)/shard_map/ppermute | solution.py:521
  86.0 1.3 %shard_map.92 = (f32[64,64]{1,0:T(8,128)S(1)}, f32[32,128]{1,0:T(8,128)}, f32[4,128]{1,0:T(4,128)S(1)}) custom-call(s32[8]{0:T(128)S(1)} %copy-done.1, bf16[224,128]{1,0:T(8,128)(2,1)S(1)} %get-tuple-element.56.refs_1_, bf16[224,128]{1,0:T(8,128)(2,1)S(1)} %collective-permute-done.30.refs_2_, bf16[224,128]{1,0:T(8,128)(2,1)S(1)} %collective-permute-done.31.refs_3_, ...), custom_call_target="tpu_custom_call" | custom-call | flops 16777216 | bytes 1048576 | tf_op jit(solution)/shard_map/pallas_call | solution.py:59
  87.4 1.6 %collective-permute-start.35 = (f32[64,64]{1,0:T(8,128)S(1)}, f32[64,64]{1,0:T(8,128)S(1)}, u32[]{:S(2)}, u32[]{:S(2)}) collective-permute-start(f32[64,64]{1,0:T(8,128)S(1)} %get-tuple-element.59.refs_0_), channel_id=1, source_target_pairs={{0,24},{8,0},{16,8},{24,16},{1,25},{9,1},{17,9},{25,17},{2,26},{10... | collective-permute-start | bytes 49160 | tf_op jit(solution)/shard_map/ppermute | solution.py:512
  89.1 1.9 %collective-permute-start.33 = (f32[64,64]{1,0:T(8,128)S(1)}, f32[64,64]{1,0:T(8,128)S(1)}, u32[]{:S(2)}, u32[]{:S(2)}) collective-permute-start(f32[64,64]{1,0:T(8,128)S(1)} %get-tuple-element.59.refs_0_), channel_id=1, source_target_pairs={{0,8},{8,16},{16,24},{24,0},{1,9},{9,17},{17,25},{25,1},{2,10},{10... | collective-permute-start | bytes 49160 | tf_op jit(solution)/shard_map/ppermute | solution.py:512
  91.3 2.7 %collective-permute-done.34.refs_2_ = f32[64,64]{1,0:T(8,128)S(1)} collective-permute-done((f32[64,64]{1,0:T(8,128)S(1)}, f32[64,64]{1,0:T(8,128)S(1)}, u32[]{:S(2)}, u32[]{:S(2)}) %collective-permute-start.34) | collective-permute-done | bytes 16416 | tf_op jit(solution)/shard_map/ppermute | solution.py:512
  94.8 3.2 %shard_map.93 = f32[64,512]{1,0:T(8,128)} custom-call(f32[64,64]{1,0:T(8,128)S(1)} %get-tuple-element.59.refs_0_, f32[64,64]{1,0:T(8,128)S(1)} %collective-permute-done.33.refs_1_, f32[64,64]{1,0:T(8,128)S(1)} %collective-permute-done.34.refs_2_, f32[64,64]{1,0:T(8,128)S(1)} %collective-permute-done.35.refs_3_, ...), custom_call_target="tpu_custom_call" | custom-call | flops 16777216 | bytes 1048576 | tf_op jit(solution)/shard_map/pallas_call | solution.py:59
  (61 shorter events, 11.2 us)
Async XLA Ops:
  2.2 8.7 %collective-permute-start.7 = (bf16[56,512]{1,0:T(8,128)(2,1)S(1)}, bf16[56,512]{1,0:T(8,128)(2,1)S(1)}, u32[]{:S(2)}, u32[]{:S(2)}) collective-permute-start(bf16[56,512]{1,0:T(8,128)(2,1)S(1)} %shard_map.85.refs_0_.pack), channel_id=1, source_target_pairs={{0,6},{1,7},{2,0},{3,1},{4,2},{5,3},{6,4},{7,5},{8,14},{9,15},{10,... | collective-permute-start | bytes 172040 | tf_op jit(solution)/shard_map/ppermute | solution.py:521
  6.1 5.7 %collective-permute-start.5 = (bf16[56,512]{1,0:T(8,128)(2,1)S(1)}, bf16[56,512]{1,0:T(8,128)(2,1)S(1)}, u32[]{:S(2)}, u32[]{:S(2)}) collective-permute-start(bf16[56,512]{1,0:T(8,128)(2,1)S(1)} %shard_map.85.refs_0_.pack), channel_id=1, source_target_pairs={{0,4},{1,5},{2,6},{3,7},{4,0},{5,1},{6,2},{7,3},{8,12},{9,13},{10,... | collective-permute-start | bytes 172040 | tf_op jit(solution)/shard_map/ppermute | solution.py:521
  6.6 5.2 %collective-permute-start.3 = (bf16[56,512]{1,0:T(8,128)(2,1)S(1)}, bf16[56,512]{1,0:T(8,128)(2,1)S(1)}, u32[]{:S(2)}, u32[]{:S(2)}) collective-permute-start(bf16[56,512]{1,0:T(8,128)(2,1)S(1)} %shard_map.85.refs_0_.pack), channel_id=1, source_target_pairs={{0,2},{1,3},{2,4},{3,5},{4,6},{5,7},{6,0},{7,1},{8,10},{9,11},{10,... | collective-permute-start | bytes 172040 | tf_op jit(solution)/shard_map/ppermute | solution.py:521
  7.2 5.4 %collective-permute-start.2 = (bf16[56,512]{1,0:T(8,128)(2,1)S(1)}, bf16[56,512]{1,0:T(8,128)(2,1)S(1)}, u32[]{:S(2)}, u32[]{:S(2)}) collective-permute-start(bf16[56,512]{1,0:T(8,128)(2,1)S(1)} %shard_map.85.refs_0_.pack), channel_id=1, source_target_pairs={{0,24},{8,0},{16,8},{24,16},{1,25},{9,1},{17,9},{25,17},{2,26},{10... | collective-permute-start | bytes 172040 | tf_op jit(solution)/shard_map/ppermute | solution.py:512
  10.8 5.1 %collective-permute-start.1 = (bf16[56,512]{1,0:T(8,128)(2,1)S(1)}, bf16[56,512]{1,0:T(8,128)(2,1)S(1)}, u32[]{:S(2)}, u32[]{:S(2)}) collective-permute-start(bf16[56,512]{1,0:T(8,128)(2,1)S(1)} %shard_map.85.refs_0_.pack), channel_id=1, source_target_pairs={{0,16},{8,24},{16,0},{24,8},{1,17},{9,25},{17,1},{25,9},{2,18},{10... | collective-permute-start | bytes 172040 | tf_op jit(solution)/shard_map/ppermute | solution.py:512
  10.8 6.0 %collective-permute-start = (bf16[56,512]{1,0:T(8,128)(2,1)S(1)}, bf16[56,512]{1,0:T(8,128)(2,1)S(1)}, u32[]{:S(2)}, u32[]{:S(2)}) collective-permute-start(bf16[56,512]{1,0:T(8,128)(2,1)S(1)} %shard_map.85.refs_0_.pack), channel_id=1, source_target_pairs={{0,8},{8,16},{16,24},{24,0},{1,9},{9,17},{17,25},{25,1},{2,10},{10... | collective-permute-start | bytes 172040 | tf_op jit(solution)/shard_map/ppermute | solution.py:512
  11.8 5.0 %collective-permute-start.8 = (bf16[56,512]{1,0:T(8,128)(2,1)S(1)}, bf16[56,512]{1,0:T(8,128)(2,1)S(1)}, u32[]{:S(2)}, u32[]{:S(2)}) collective-permute-start(bf16[56,512]{1,0:T(8,128)(2,1)S(1)} %collective-permute-done.7.refs_13_), channel_id=1, source_target_pairs={{0,1},{1,0},{2,3},{3,2},{4,5},{5,4},{6,7},{7,6},{8,9},{9,8},{10,11... | collective-permute-start | bytes 172040 | tf_op jit(solution)/shard_map/ppermute | solution.py:507
  11.9 5.0 %collective-permute-start.6 = (bf16[56,512]{1,0:T(8,128)(2,1)S(1)}, bf16[56,512]{1,0:T(8,128)(2,1)S(1)}, u32[]{:S(2)}, u32[]{:S(2)}) collective-permute-start(bf16[56,512]{1,0:T(8,128)(2,1)S(1)} %collective-permute-done.5.refs_9_), channel_id=1, source_target_pairs={{0,1},{1,0},{2,3},{3,2},{4,5},{5,4},{6,7},{7,6},{8,9},{9,8},{10,11... | collective-permute-start | bytes 172040 | tf_op jit(solution)/shard_map/ppermute | solution.py:507
  12.7 4.2 %collective-permute-start.4 = (bf16[56,512]{1,0:T(8,128)(2,1)S(1)}, bf16[56,512]{1,0:T(8,128)(2,1)S(1)}, u32[]{:S(2)}, u32[]{:S(2)}) collective-permute-start(bf16[56,512]{1,0:T(8,128)(2,1)S(1)} %collective-permute-done.3.refs_5_), channel_id=1, source_target_pairs={{0,1},{1,0},{2,3},{3,2},{4,5},{5,4},{6,7},{7,6},{8,9},{9,8},{10,11... | collective-permute-start | bytes 172040 | tf_op jit(solution)/shard_map/ppermute | solution.py:507
  16.9 5.2 %collective-permute-start.10 = (bf16[3,56,512]{2,1,0:T(8,128)(2,1)S(1)}, bf16[3,56,512]{2,1,0:T(8,128)(2,1)S(1)}, u32[]{:S(2)}, u32[]{:S(2)}) collective-permute-start(bf16[3,56,512]{2,1,0:T(8,128)(2,1)S(1)} %get-tuple-element.35.rest), channel_id=1, source_target_pairs={{0,1},{1,0},{2,3},{3,2},{4,5},{5,4},{6,7},{7,6},{8,9},{9,8},{10,11... | collective-permute-start | bytes 516104 | tf_op jit(solution)/shard_map/ppermute | solution.py:507
  17.0 12.2 %collective-permute-start.13 = (bf16[3,56,512]{2,1,0:T(8,128)(2,1)S(1)}, bf16[3,56,512]{2,1,0:T(8,128)(2,1)S(1)}, u32[]{:S(2)}, u32[]{:S(2)}) collective-permute-start(bf16[3,56,512]{2,1,0:T(8,128)(2,1)S(1)} %get-tuple-element.35.rest), channel_id=1, source_target_pairs={{0,6},{1,7},{2,0},{3,1},{4,2},{5,3},{6,4},{7,5},{8,14},{9,15},{10,... | collective-permute-start | bytes 516104 | tf_op jit(solution)/shard_map/ppermute | solution.py:521
  19.3 11.5 %collective-permute-start.12 = (bf16[3,56,512]{2,1,0:T(8,128)(2,1)S(1)}, bf16[3,56,512]{2,1,0:T(8,128)(2,1)S(1)}, u32[]{:S(2)}, u32[]{:S(2)}) collective-permute-start(bf16[3,56,512]{2,1,0:T(8,128)(2,1)S(1)} %get-tuple-element.35.rest), channel_id=1, source_target_pairs={{0,4},{1,5},{2,6},{3,7},{4,0},{5,1},{6,2},{7,3},{8,12},{9,13},{10,... | collective-permute-start | bytes 516104 | tf_op jit(solution)/shard_map/ppermute | solution.py:521
  20.9 10.0 %collective-permute-start.11 = (bf16[3,56,512]{2,1,0:T(8,128)(2,1)S(1)}, bf16[3,56,512]{2,1,0:T(8,128)(2,1)S(1)}, u32[]{:S(2)}, u32[]{:S(2)}) collective-permute-start(bf16[3,56,512]{2,1,0:T(8,128)(2,1)S(1)} %get-tuple-element.35.rest), channel_id=1, source_target_pairs={{0,2},{1,3},{2,4},{3,5},{4,6},{5,7},{6,0},{7,1},{8,10},{9,11},{10,... | collective-permute-start | bytes 516104 | tf_op jit(solution)/shard_map/ppermute | solution.py:521
  27.6 4.5 %collective-permute-start.18 = (bf16[64,512]{1,0:T(8,128)(2,1)}, bf16[64,512]{1,0:T(8,128)(2,1)S(1)}, u32[]{:S(2)}, u32[]{:S(2)}) collective-permute-start(bf16[64,512]{1,0:T(8,128)(2,1)} %refs_8_), channel_id=1, source_target_pairs={{0,24},{8,0},{16,8},{24,16},{1,25},{9,1},{17,9},{25,17},{2,26},{10... | collective-permute-start | bytes 196616 | tf_op jit(solution)/shard_map/ppermute | solution.py:512
  29.1 7.8 %collective-permute-start.17 = (bf16[64,512]{1,0:T(8,128)(2,1)}, bf16[64,512]{1,0:T(8,128)(2,1)S(1)}, u32[]{:S(2)}, u32[]{:S(2)}) collective-permute-start(bf16[64,512]{1,0:T(8,128)(2,1)} %refs_8_), channel_id=1, source_target_pairs={{0,16},{8,24},{16,0},{24,8},{1,17},{9,25},{17,1},{25,9},{2,18},{10... | collective-permute-start | bytes 196616 | tf_op jit(solution)/shard_map/ppermute | solution.py:512
  29.1 7.8 %collective-permute-start.16 = (bf16[64,512]{1,0:T(8,128)(2,1)}, bf16[64,512]{1,0:T(8,128)(2,1)S(1)}, u32[]{:S(2)}, u32[]{:S(2)}) collective-permute-start(bf16[64,512]{1,0:T(8,128)(2,1)} %refs_8_), channel_id=1, source_target_pairs={{0,8},{8,16},{16,24},{24,0},{1,9},{9,17},{17,25},{25,1},{2,10},{10... | collective-permute-start | bytes 196616 | tf_op jit(solution)/shard_map/ppermute | solution.py:512
  30.9 6.1 %collective-permute-start.14 = (bf16[3,56,512]{2,1,0:T(8,128)(2,1)S(1)}, bf16[3,56,512]{2,1,0:T(8,128)(2,1)S(1)}, u32[]{:S(2)}, u32[]{:S(2)}) collective-permute-start(bf16[3,56,512]{2,1,0:T(8,128)(2,1)S(1)} %collective-permute-done.11.refs_6_), channel_id=1, source_target_pairs={{0,1},{1,0},{2,3},{3,2},{4,5},{5,4},{6,7},{7,6},{8,9},{9,8},{10,11... | collective-permute-start | bytes 516104 | tf_op jit(solution)/shard_map/ppermute | solution.py:507
  30.9 6.1 %collective-permute-start.15 = (bf16[3,56,512]{2,1,0:T(8,128)(2,1)S(1)}, bf16[3,56,512]{2,1,0:T(8,128)(2,1)S(1)}, u32[]{:S(2)}, u32[]{:S(2)}) collective-permute-start(bf16[3,56,512]{2,1,0:T(8,128)(2,1)S(1)} %collective-permute-done.12.refs_10_), channel_id=1, source_target_pairs={{0,1},{1,0},{2,3},{3,2},{4,5},{5,4},{6,7},{7,6},{8,9},{9,8},{10,11... | collective-permute-start | bytes 516104 | tf_op jit(solution)/shard_map/ppermute | solution.py:507
  46.4 4.4 %collective-permute-start.23 = (bf16[128,128]{1,0:T(8,128)(2,1)S(1)}, bf16[128,128]{1,0:T(8,128)(2,1)S(1)}, u32[]{:S(2)}, u32[]{:S(2)}) collective-permute-start(bf16[128,128]{1,0:T(8,128)(2,1)S(1)} %add_convert_fusion.1.refs_3_), channel_id=1, source_target_pairs={{0,6},{1,7},{2,0},{3,1},{4,2},{5,3},{6,4},{7,5},{8,14},{9,15},{10,... | collective-permute-start | bytes 98312 | tf_op jit(solution)/shard_map/ppermute | solution.py:521
  49.2 4.3 %collective-permute-start.22 = (bf16[128,128]{1,0:T(8,128)(2,1)S(1)}, bf16[128,128]{1,0:T(8,128)(2,1)S(1)}, u32[]{:S(2)}, u32[]{:S(2)}) collective-permute-start(bf16[128,128]{1,0:T(8,128)(2,1)S(1)} %add_convert_fusion.1.refs_3_), channel_id=1, source_target_pairs={{0,4},{1,5},{2,6},{3,7},{4,0},{5,1},{6,2},{7,3},{8,12},{9,13},{10,... | collective-permute-start | bytes 98312 | tf_op jit(solution)/shard_map/ppermute | solution.py:521
  49.7 4.8 %collective-permute-start.21 = (bf16[128,128]{1,0:T(8,128)(2,1)S(1)}, bf16[128,128]{1,0:T(8,128)(2,1)S(1)}, u32[]{:S(2)}, u32[]{:S(2)}) collective-permute-start(bf16[128,128]{1,0:T(8,128)(2,1)S(1)} %add_convert_fusion.1.refs_3_), channel_id=1, source_target_pairs={{0,2},{1,3},{2,4},{3,5},{4,6},{5,7},{6,0},{7,1},{8,10},{9,11},{10,... | collective-permute-start | bytes 98312 | tf_op jit(solution)/shard_map/ppermute | solution.py:521
  62.3 4.0 %collective-permute-start.27 = (bf16[128,128]{1,0:T(8,128)(2,1)S(1)}, bf16[128,128]{1,0:T(8,128)(2,1)S(1)}, u32[]{:S(2)}, u32[]{:S(2)}) collective-permute-start(bf16[128,128]{1,0:T(8,128)(2,1)S(1)} %add_convert_fusion.refs_4_), channel_id=1, source_target_pairs={{0,6},{1,7},{2,0},{3,1},{4,2},{5,3},{6,4},{7,5},{8,14},{9,15},{10,... | collective-permute-start | bytes 98312 | tf_op jit(solution)/shard_map/ppermute | solution.py:521
  62.4 3.9 %collective-permute-start.26 = (bf16[128,128]{1,0:T(8,128)(2,1)S(1)}, bf16[128,128]{1,0:T(8,128)(2,1)S(1)}, u32[]{:S(2)}, u32[]{:S(2)}) collective-permute-start(bf16[128,128]{1,0:T(8,128)(2,1)S(1)} %add_convert_fusion.refs_4_), channel_id=1, source_target_pairs={{0,4},{1,5},{2,6},{3,7},{4,0},{5,1},{6,2},{7,3},{8,12},{9,13},{10,... | collective-permute-start | bytes 98312 | tf_op jit(solution)/shard_map/ppermute | solution.py:521
  64.0 4.8 %collective-permute-start.25 = (bf16[128,128]{1,0:T(8,128)(2,1)S(1)}, bf16[128,128]{1,0:T(8,128)(2,1)S(1)}, u32[]{:S(2)}, u32[]{:S(2)}) collective-permute-start(bf16[128,128]{1,0:T(8,128)(2,1)S(1)} %add_convert_fusion.refs_4_), channel_id=1, source_target_pairs={{0,2},{1,3},{2,4},{3,5},{4,6},{5,7},{6,0},{7,1},{8,10},{9,11},{10,... | collective-permute-start | bytes 98312 | tf_op jit(solution)/shard_map/ppermute | solution.py:521
  78.3 4.7 %collective-permute-start.32 = (bf16[224,128]{1,0:T(8,128)(2,1)S(1)}, bf16[224,128]{1,0:T(8,128)(2,1)S(1)}, u32[]{:S(2)}, u32[]{:S(2)}) collective-permute-start(bf16[224,128]{1,0:T(8,128)(2,1)S(1)} %get-tuple-element.56.refs_1_), channel_id=1, source_target_pairs={{0,6},{1,7},{2,0},{3,1},{4,2},{5,3},{6,4},{7,5},{8,14},{9,15},{10,... | collective-permute-start | bytes 172040 | tf_op jit(solution)/shard_map/ppermute | solution.py:521
  78.3 10.8 %collective-permute-start.36 = (bf16[256,128]{1,0:T(8,128)(2,1)S(1)}, bf16[256,128]{1,0:T(8,128)(2,1)S(1)}, u32[]{:S(2)}, u32[]{:S(2)}) collective-permute-start(bf16[256,128]{1,0:T(8,128)(2,1)S(1)} %get-tuple-element.61), channel_id=1, source_target_pairs={{0,2},{1,3},{2,4},{3,5},{4,6},{5,7},{6,0},{7,1},{8,10},{9,11},{10,... | collective-permute-start | bytes 196616 | tf_op jit(solution)/shard_map/ppermute | solution.py:521
  80.3 5.7 %collective-permute-start.31 = (bf16[224,128]{1,0:T(8,128)(2,1)S(1)}, bf16[224,128]{1,0:T(8,128)(2,1)S(1)}, u32[]{:S(2)}, u32[]{:S(2)}) collective-permute-start(bf16[224,128]{1,0:T(8,128)(2,1)S(1)} %get-tuple-element.56.refs_1_), channel_id=1, source_target_pairs={{0,4},{1,5},{2,6},{3,7},{4,0},{5,1},{6,2},{7,3},{8,12},{9,13},{10,... | collective-permute-start | bytes 172040 | tf_op jit(solution)/shard_map/ppermute | solution.py:521
  80.3 5.7 %collective-permute-start.30 = (bf16[224,128]{1,0:T(8,128)(2,1)S(1)}, bf16[224,128]{1,0:T(8,128)(2,1)S(1)}, u32[]{:S(2)}, u32[]{:S(2)}) collective-permute-start(bf16[224,128]{1,0:T(8,128)(2,1)S(1)} %get-tuple-element.56.refs_1_), channel_id=1, source_target_pairs={{0,2},{1,3},{2,4},{3,5},{4,6},{5,7},{6,0},{7,1},{8,10},{9,11},{10,... | collective-permute-start | bytes 172040 | tf_op jit(solution)/shard_map/ppermute | solution.py:521
  81.9 9.2 %collective-permute-start.37 = (bf16[256,128]{1,0:T(8,128)(2,1)S(1)}, bf16[256,128]{1,0:T(8,128)(2,1)S(1)}, u32[]{:S(2)}, u32[]{:S(2)}) collective-permute-start(bf16[256,128]{1,0:T(8,128)(2,1)S(1)} %get-tuple-element.62), channel_id=1, source_target_pairs={{0,4},{1,5},{2,6},{3,7},{4,0},{5,1},{6,2},{7,3},{8,12},{9,13},{10,... | collective-permute-start | bytes 196616 | tf_op jit(solution)/shard_map/ppermute | solution.py:521
  83.0 8.1 %collective-permute-start.38 = (bf16[256,128]{1,0:T(8,128)(2,1)S(1)}, bf16[256,128]{1,0:T(8,128)(2,1)S(1)}, u32[]{:S(2)}, u32[]{:S(2)}) collective-permute-start(bf16[256,128]{1,0:T(8,128)(2,1)S(1)} %get-tuple-element.63), channel_id=1, source_target_pairs={{0,6},{1,7},{2,0},{3,1},{4,2},{5,3},{6,4},{7,5},{8,14},{9,15},{10,... | collective-permute-start | bytes 196616 | tf_op jit(solution)/shard_map/ppermute | solution.py:521
  89.0 5.0 %collective-permute-start.34 = (f32[64,64]{1,0:T(8,128)S(1)}, f32[64,64]{1,0:T(8,128)S(1)}, u32[]{:S(2)}, u32[]{:S(2)}) collective-permute-start(f32[64,64]{1,0:T(8,128)S(1)} %get-tuple-element.59.refs_0_), channel_id=1, source_target_pairs={{0,16},{8,24},{16,0},{24,8},{1,17},{9,25},{17,1},{25,9},{2,18},{10... | collective-permute-start | bytes 49160 | tf_op jit(solution)/shard_map/ppermute | solution.py:512
  89.1 5.7 %collective-permute-start.33 = (f32[64,64]{1,0:T(8,128)S(1)}, f32[64,64]{1,0:T(8,128)S(1)}, u32[]{:S(2)}, u32[]{:S(2)}) collective-permute-start(f32[64,64]{1,0:T(8,128)S(1)} %get-tuple-element.59.refs_0_), channel_id=1, source_target_pairs={{0,8},{8,16},{16,24},{24,0},{1,9},{9,17},{17,25},{25,1},{2,10},{10... | collective-permute-start | bytes 49160 | tf_op jit(solution)/shard_map/ppermute | solution.py:512
  (9 other events, 116.3 us)

commit v4 on v3

--- a/solution.py
+++ b/solution.py
@@ -10,7 +10,7 @@
 BLK = 128
 SWEEPS = 3
 GROUP = 32
-BUILD_GROUP = 16
+BUILD_GROUP = 32
 TILE_GROUP = 16
 ROWS, COLUMNS, COUNT = 0, 1, 2
 FEAT = 64
@@ -356,7 +356,7 @@
     scaling = SCALE / column_totals(tiles, row_left, col_acc, blocks)
     scaling_out[...] = scaling
     for k in range(n_row):
-        piece = shifted(me_row, k, n_row)
+        piece = lax.bitwise_xor(me_row, k)
         for j in range(per):
             block = bases[k][:, j * BLK : (j + 1) * BLK].astype(F32)
             b = piece * per + j
@@ -588,10 +588,7 @@
             pltpu.VMEM((col_blocks + 1, 8, BLK), F32),
         ],
     )
-    basis, sums = lax.optimization_barrier((basis, sums))
-    bases = shifts(basis, "row")
     far, sums = lax.optimization_barrier((far, sums))
-    far[-1], bases = lax.optimization_barrier((far[-1], bases))
     stacks = []
     for pack, other, group in zip(near, near_in, far):
         stacks += [pack, group, other, sibling(group)]
@@ -614,11 +611,14 @@
     def chip_parts(part):
         return chip_shifts((part + sibling(part)).astype(BF16))
 
+    bases = [basis]
     for _ in range(SWEEPS - 2):
+        part, bases[0] = lax.optimization_barrier((part, bases[0]))
+        bases = bases[:1] + [swap(bases[0], "row", 1)]
         (part,) = call(
             functools.partial(sweep_kernel, n_row, n_chip),
             [shape(all_rows, BLK)],
-            [table] + tiles + vec(*chip_parts(part)),
+            [table] + tiles + vec(*chip_parts(part)) + [("near", bases[1])],
             [
                 pltpu.VMEM((n_chip, all_rows, BLK), F32),
                 pltpu.VMEM((2, all_rows, PIECES, 2 * BLK), BF16),
@@ -628,6 +628,9 @@
             ],
         )
     both_rows = 3 * row_blocks + n_land * cols
+    part, bases = lax.optimization_barrier((part, bases))
+    while len(bases) < n_row:
+        bases = bases + [swap(base, "row", len(bases)) for base in bases]
     keep, away, both, col_scaling = call(
         functools.partial(last_kernel, n_row, n_chip, n_land),
         [

time: 98.3 us -> 91.6 us (0.932)
  waiting for transfers between devices: 28.9 us -> 24.7 us
  Pallas kernels: 32 us -> 30.3 us
    ppermute x9 -> x6, waiting for transfers between devices: 13.8 us -> 9.2 us  [shift(): return lax.ppermute(x, axis, [(i, (i + k) % n) for i in range(n)])]
    ppermute x9 -> x6, starting transfers between devices: 11.5 us -> 7.7 us  [shift(): return lax.ppermute(x, axis, [(i, (i + k) % n) for i in range(n)])]
    ppermute x12 -> x15, starting transfers between devices: 1.75 us -> 4.95 us  [swap(): lax.ppermute(x, axis, [(i, i ^ k) for i in range(lax.axis_size(axis))])]
    pallas_call x9, Pallas kernels: 32 us -> 30.3 us  [call(): pl.pallas_call(kernel, out_shape=tuple(outs), in_specs=specs, out_specs=t...]
    ppermute x12 -> x15, waiting for transfers between devices: 6.23 us -> 7.93 us  [swap(): lax.ppermute(x, axis, [(i, i ^ k) for i in range(lax.axis_size(axis))])]
    ppermute x18, waiting for transfers between devices: 8.9 us -> 7.52 us  [chip_shift(): lax.ppermute(x, 'col', [(2 * q + p, 2 * ((q + k) % n) + p) for q in range...]
where the time goes in v4:
time: 91.6 us; the launch traced here: 91.5 us
  starting transfers between devices  35.1 us (38%)
  Pallas kernels  30.3 us (33%)
  waiting for transfers between devices  24.7 us (27%)
  between operations  1.42 us (2%)
    pallas_call x9, Pallas kernels, call(): pl.pallas_call(kernel, out_shape=tuple(outs), in_specs=specs, out_specs=t...  30.3 us
    ppermute x18, starting transfers between devices, chip_shift(): lax.ppermute(x, 'col', [(2 * q + p, 2 * ((q + k) % n) + p) for q in range...  22.4 us
    ppermute x6, waiting for transfers between devices, shift(): return lax.ppermute(x, axis, [(i, (i + k) % n) for i in range(n)])  9.2 us
    ppermute x15, waiting for transfers between devices, swap(): lax.ppermute(x, axis, [(i, i ^ k) for i in range(lax.axis_size(axis))])  7.93 us
    ppermute x6, starting transfers between devices, shift(): return lax.ppermute(x, axis, [(i, (i + k) % n) for i in range(n)])  7.7 us
    ppermute x18, waiting for transfers between devices, chip_shift(): lax.ppermute(x, 'col', [(2 * q + p, 2 * ((q + k) % n) + p) for q in range...  7.52 us
    ppermute x15, starting transfers between devices, swap(): lax.ppermute(x, axis, [(i, i ^ k) for i in range(lax.axis_size(axis))])  4.95 us
  transfers between devices with their start and end apart: 39, of which 21 were waited for; matrix products, arithmetic and copies ran while one was open for 0% of the time, Pallas kernels for 7%

profile of v4, /device:TPU:0, one launch (start us, length us, event | category | flops | bytes accessed | tf_op | source)
XLA Modules:
  0.0 91.5 jit_solution(14120387826275834333)
XLA Ops:
  2.2 3.9 %collective-permute-start.7 = (bf16[56,512]{1,0:T(8,128)(2,1)S(1)}, bf16[56,512]{1,0:T(8,128)(2,1)S(1)}, u32[]{:S(2)}, u32[]{:S(2)}) collective-permute-start(bf16[56,512]{1,0:T(8,128)(2,1)S(1)} %shard_map.85.refs_0_.pack), channel_id=1, source_target_pairs={{0,6},{1,7},{2,0},{3,1},{4,2},{5,3},{6,4},{7,5},{8,14},{9,15},{10,... | collective-permute-start | bytes 172040 | tf_op jit(solution)/shard_map/ppermute | solution.py:521
  7.2 3.6 %collective-permute-start.2 = (bf16[56,512]{1,0:T(8,128)(2,1)S(1)}, bf16[56,512]{1,0:T(8,128)(2,1)S(1)}, u32[]{:S(2)}, u32[]{:S(2)}) collective-permute-start(bf16[56,512]{1,0:T(8,128)(2,1)S(1)} %shard_map.85.refs_0_.pack), channel_id=1, source_target_pairs={{0,24},{8,0},{16,8},{24,16},{1,25},{9,1},{17,9},{25,17},{2,26},{10... | collective-permute-start | bytes 172040 | tf_op jit(solution)/shard_map/ppermute | solution.py:512
  10.8 1.0 %collective-permute-start = (bf16[56,512]{1,0:T(8,128)(2,1)S(1)}, bf16[56,512]{1,0:T(8,128)(2,1)S(1)}, u32[]{:S(2)}, u32[]{:S(2)}) collective-permute-start(bf16[56,512]{1,0:T(8,128)(2,1)S(1)} %shard_map.85.refs_0_.pack), channel_id=1, source_target_pairs={{0,8},{8,16},{16,24},{24,0},{1,9},{9,17},{17,25},{25,1},{2,10},{10... | collective-permute-start | bytes 172040 | tf_op jit(solution)/shard_map/ppermute | solution.py:512
  12.7 3.2 %collective-permute-done.1.refs_2_ = bf16[56,512]{1,0:T(8,128)(2,1)S(1)} collective-permute-done((bf16[56,512]{1,0:T(8,128)(2,1)S(1)}, bf16[56,512]{1,0:T(8,128)(2,1)S(1)}, u32[]{:S(2)}, u32[]{:S(2)}) %collective-permute-start.1) | collective-permute-done | bytes 57376 | tf_op jit(solution)/shard_map/ppermute | solution.py:512
  17.0 2.4 %collective-permute-start.13 = (bf16[3,56,512]{2,1,0:T(8,128)(2,1)S(1)}, bf16[3,56,512]{2,1,0:T(8,128)(2,1)S(1)}, u32[]{:S(2)}, u32[]{:S(2)}) collective-permute-start(bf16[3,56,512]{2,1,0:T(8,128)(2,1)S(1)} %get-tuple-element.33.rest), channel_id=1, source_target_pairs={{0,6},{1,7},{2,0},{3,1},{4,2},{5,3},{6,4},{7,5},{8,14},{9,15},{10,... | collective-permute-start | bytes 516104 | tf_op jit(solution)/shard_map/ppermute | solution.py:521
  19.3 1.5 %collective-permute-start.12 = (bf16[3,56,512]{2,1,0:T(8,128)(2,1)S(1)}, bf16[3,56,512]{2,1,0:T(8,128)(2,1)S(1)}, u32[]{:S(2)}, u32[]{:S(2)}) collective-permute-start(bf16[3,56,512]{2,1,0:T(8,128)(2,1)S(1)} %get-tuple-element.33.rest), channel_id=1, source_target_pairs={{0,4},{1,5},{2,6},{3,7},{4,0},{5,1},{6,2},{7,3},{8,12},{9,13},{10,... | collective-permute-start | bytes 516104 | tf_op jit(solution)/shard_map/ppermute | solution.py:521
  20.9 1.2 %collective-permute-done.9.pack_in = bf16[56,512]{1,0:T(8,128)(2,1)S(1)} collective-permute-done((bf16[56,512]{1,0:T(8,128)(2,1)S(1)}, bf16[56,512]{1,0:T(8,128)(2,1)S(1)}, u32[]{:S(2)}, u32[]{:S(2)}) %collective-permute-start.9) | collective-permute-done | bytes 57376 | tf_op jit(solution)/shard_map/ppermute | solution.py:507
  22.1 4.8 %shard_map.87 = (bf16[128,128,128]{2,1,0:T(8,128)(2,1)S(1)}, bf16[16,128,64]{2,1,0:T(8,128)(2,1)S(1)}, f32[16,128,128]{2,1,0:T(8,128)S(1)}, f32[16,128]{1,0:T(8,128)S(1)}) custom-call(s32[32,128]{1,0:T(8,128)S(1)} %bitcast.3, bf16[56,512]{1,0:T(8,128)(2,1)S(1)} %shard_map.85.refs_0_.pack, bf16[3,56,512]{2,1,0:T(8,128)(2,1)S(1)} %get-tuple-element.33.rest, ...), custom_call_target="tpu_custom_call" | custom-call | flops 16777216 | bytes 1048576 | tf_op jit(solution)/shard_map/pallas_call | solution.py:59
  27.0 2.5 %collective-permute-done.12.refs_10_ = bf16[3,56,512]{2,1,0:T(8,128)(2,1)S(1)} collective-permute-done((bf16[3,56,512]{2,1,0:T(8,128)(2,1)S(1)}, bf16[3,56,512]{2,1,0:T(8,128)(2,1)S(1)}, u32[]{:S(2)}, u32[]{:S(2)}) %collective-permute-start.12) | collective-permute-done | bytes 172064 | tf_op jit(solution)/shard_map/ppermute | solution.py:521
  31.4 6.3 %shard_map.88 = (bf16[384,128,128]{2,1,0:T(8,128)(2,1)S(1)}, f32[128,128]{1,0:T(8,128)S(1)}) custom-call(s32[32,128]{1,0:T(8,128)S(1)} %bitcast.4, bf16[128,128,128]{2,1,0:T(8,128)(2,1)S(1)} %get-tuple-element.34.refs_1_.refs_2_, bf16[16,128,64]{2,1,0:T(8,128)(2,1)S(1)} %get-tuple-element.35.refs_2_, f32[16,128,128]{2,1,0:T(8,128)S(1)} %get-tuple-element.36.refs_3_, ...), custom_call_target="tpu_custom_call" | custom-call | flops 16777216 | bytes 1048576 | tf_op jit(solution)/shard_map/pallas_call | solution.py:59
  38.0 1.0 %collective-permute-done.17 = f32[128,128]{1,0:T(8,128)S(1)} collective-permute-done((f32[128,128]{1,0:T(8,128)S(1)}, f32[128,128]{1,0:T(8,128)S(1)}, u32[]{:S(2)}, u32[]{:S(2)}) %collective-permute-start.17) | collective-permute-done | bytes 65568 | tf_op jit(solution)/shard_map/ppermute | solution.py:507
  39.0 1.3 %collective-permute-start.20 = (bf16[128,128]{1,0:T(8,128)(2,1)S(1)}, bf16[128,128]{1,0:T(8,128)(2,1)S(1)}, u32[]{:S(2)}, u32[]{:S(2)}) collective-permute-start(bf16[128,128]{1,0:T(8,128)(2,1)S(1)} %add_convert_fusion.1.refs_3_), channel_id=1, source_target_pairs={{0,6},{1,7},{2,0},{3,1},{4,2},{5,3},{6,4},{7,5},{8,14},{9,15},{10,... | collective-permute-start | bytes 98312 | tf_op jit(solution)/shard_map/ppermute | solution.py:521
  40.9 1.7 %collective-permute-start.18 = (bf16[128,128]{1,0:T(8,128)(2,1)S(1)}, bf16[128,128]{1,0:T(8,128)(2,1)S(1)}, u32[]{:S(2)}, u32[]{:S(2)}) collective-permute-start(bf16[128,128]{1,0:T(8,128)(2,1)S(1)} %add_convert_fusion.1.refs_3_), channel_id=1, source_target_pairs={{0,2},{1,3},{2,4},{3,5},{4,6},{5,7},{6,0},{7,1},{8,10},{9,11},{10,... | collective-permute-start | bytes 98312 | tf_op jit(solution)/shard_map/ppermute | solution.py:521
  43.0 1.6 %collective-permute-done.19.refs_5_ = bf16[128,128]{1,0:T(8,128)(2,1)S(1)} collective-permute-done((bf16[128,128]{1,0:T(8,128)(2,1)S(1)}, bf16[128,128]{1,0:T(8,128)(2,1)S(1)}, u32[]{:S(2)}, u32[]{:S(2)}) %collective-permute-start.19) | collective-permute-done | bytes 32800 | tf_op jit(solution)/shard_map/ppermute | solution.py:521
  44.6 1.1 %collective-permute-done.18.refs_4_ = bf16[128,128]{1,0:T(8,128)(2,1)S(1)} collective-permute-done((bf16[128,128]{1,0:T(8,128)(2,1)S(1)}, bf16[128,128]{1,0:T(8,128)(2,1)S(1)}, u32[]{:S(2)}, u32[]{:S(2)}) %collective-permute-start.18) | collective-permute-done | bytes 32800 | tf_op jit(solution)/shard_map/ppermute | solution.py:521
  45.7 6.5 %shard_map.89 = f32[128,128]{1,0:T(8,128)S(1)} custom-call(s32[32,128]{1,0:T(8,128)S(1)} %bitcast.5, bf16[128,128,128]{2,1,0:T(8,128)(2,1)S(1)} %get-tuple-element.34.refs_1_.refs_2_, bf16[384,128,128]{2,1,0:T(8,128)(2,1)S(1)} %get-tuple-element.42.refs_2_.refs_3_, bf16[128,128]{1,0:T(8,128)(2,1)S(1)} %add_convert_fusion.1.refs_3_, ...), custom_call_target="tpu_custom_call" | custom-call | flops 16777216 | bytes 1048576 | tf_op jit(solution)/shard_map/pallas_call | solution.py:59
  52.3 1.2 %collective-permute-start.26 = (bf16[64,512]{1,0:T(8,128)(2,1)S(1)}, bf16[64,512]{1,0:T(8,128)(2,1)S(1)}, u32[]{:S(2)}, u32[]{:S(2)}) collective-permute-start(bf16[64,512]{1,0:T(8,128)(2,1)S(1)} %copy-done), channel_id=1, source_target_pairs={{0,16},{8,24},{16,0},{24,8},{1,17},{9,25},{17,1},{25,9},{2,18},{10... | collective-permute-start | bytes 196616 | tf_op jit(solution)/shard_map/ppermute | solution.py:507
  53.5 1.8 %collective-permute-start.27 = (bf16[64,512]{1,0:T(8,128)(2,1)S(1)}, bf16[64,512]{1,0:T(8,128)(2,1)S(1)}, u32[]{:S(2)}, u32[]{:S(2)}) collective-permute-start(bf16[64,512]{1,0:T(8,128)(2,1)S(1)} %collective-permute-done.21.refs_7_.refs_9_), channel_id=1, source_target_pairs={{0,16},{8,24},{16,0},{24,8},{1,17},{9,25},{17,1},{25,9},{2,18},{10... | collective-permute-start | bytes 196616 | tf_op jit(solution)/shard_map/ppermute | solution.py:507
  56.0 1.6 %collective-permute-start.24 = (bf16[128,128]{1,0:T(8,128)(2,1)S(1)}, bf16[128,128]{1,0:T(8,128)(2,1)S(1)}, u32[]{:S(2)}, u32[]{:S(2)}) collective-permute-start(bf16[128,128]{1,0:T(8,128)(2,1)S(1)} %add_convert_fusion.refs_4_), channel_id=1, source_target_pairs={{0,4},{1,5},{2,6},{3,7},{4,0},{5,1},{6,2},{7,3},{8,12},{9,13},{10,... | collective-permute-start | bytes 98312 | tf_op jit(solution)/shard_map/ppermute | solution.py:521
  57.6 1.1 %collective-permute-start.23 = (bf16[128,128]{1,0:T(8,128)(2,1)S(1)}, bf16[128,128]{1,0:T(8,128)(2,1)S(1)}, u32[]{:S(2)}, u32[]{:S(2)}) collective-permute-start(bf16[128,128]{1,0:T(8,128)(2,1)S(1)} %add_convert_fusion.refs_4_), channel_id=1, source_target_pairs={{0,2},{1,3},{2,4},{3,5},{4,6},{5,7},{6,0},{7,1},{8,10},{9,11},{10,... | collective-permute-start | bytes 98312 | tf_op jit(solution)/shard_map/ppermute | solution.py:521
  58.8 2.2 %collective-permute-done.26.refs_10_ = bf16[64,512]{1,0:T(8,128)(2,1)S(1)} collective-permute-done((bf16[64,512]{1,0:T(8,128)(2,1)S(1)}, bf16[64,512]{1,0:T(8,128)(2,1)S(1)}, u32[]{:S(2)}, u32[]{:S(2)}) %collective-permute-start.26) | collective-permute-done | bytes 65568 | tf_op jit(solution)/shard_map/ppermute | solution.py:507
  60.9 1.0 %collective-permute-done.27.refs_11_ = bf16[64,512]{1,0:T(8,128)(2,1)S(1)} collective-permute-done((bf16[64,512]{1,0:T(8,128)(2,1)S(1)}, bf16[64,512]{1,0:T(8,128)(2,1)S(1)}, u32[]{:S(2)}, u32[]{:S(2)}) %collective-permute-start.27) | collective-permute-done | bytes 65568 | tf_op jit(solution)/shard_map/ppermute | solution.py:507
  62.4 7.2 %shard_map.90 = (f32[4,4,64,128]{3,2,1,0:T(8,128)S(1)}, bf16[4,4,64,128]{3,2,1,0:T(8,128)(2,1)S(1)}, bf16[224,128]{1,0:T(8,128)(2,1)S(1)}, f32[16,128]{1,0:T(8,128)}) custom-call(s32[32,128]{1,0:T(8,128)S(1)} %bitcast.6, s32[8]{0:T(128)S(1)} %copy-done.1, bf16[128,128,128]{2,1,0:T(8,128)(2,1)S(1)} %get-tuple-element.34.refs_1_.refs_2_, ...), custom_call_target="tpu_custom_call" | custom-call | flops 16777216 | bytes 1048576 | tf_op jit(solution)/shard_map/pallas_call | solution.py:59
  70.1 1.1 %collective-permute-done.29.both_in = bf16[224,128]{1,0:T(8,128)(2,1)S(1)} collective-permute-done((bf16[224,128]{1,0:T(8,128)(2,1)S(1)}, bf16[224,128]{1,0:T(8,128)(2,1)S(1)}, u32[]{:S(2)}, u32[]{:S(2)}) %collective-permute-start.29) | collective-permute-done | bytes 57376 | tf_op jit(solution)/shard_map/ppermute | solution.py:507
  71.4 2.0 %collective-permute-start.36 = (bf16[256,128]{1,0:T(8,128)(2,1)S(1)}, bf16[256,128]{1,0:T(8,128)(2,1)S(1)}, u32[]{:S(2)}, u32[]{:S(2)}) collective-permute-start(bf16[256,128]{1,0:T(8,128)(2,1)S(1)} %get-tuple-element.57), channel_id=1, source_target_pairs={{0,2},{1,3},{2,4},{3,5},{4,6},{5,7},{6,0},{7,1},{8,10},{9,11},{10,... | collective-permute-start | bytes 196616 | tf_op jit(solution)/shard_map/ppermute | solution.py:521
  73.4 1.5 %collective-permute-start.30 = (bf16[224,128]{1,0:T(8,128)(2,1)S(1)}, bf16[224,128]{1,0:T(8,128)(2,1)S(1)}, u32[]{:S(2)}, u32[]{:S(2)}) collective-permute-start(bf16[224,128]{1,0:T(8,128)(2,1)S(1)} %get-tuple-element.52.refs_1_), channel_id=1, source_target_pairs={{0,2},{1,3},{2,4},{3,5},{4,6},{5,7},{6,0},{7,1},{8,10},{9,11},{10,... | collective-permute-start | bytes 172040 | tf_op jit(solution)/shard_map/ppermute | solution.py:521
  76.0 2.3 %collective-permute-start.38 = (bf16[256,128]{1,0:T(8,128)(2,1)S(1)}, bf16[256,128]{1,0:T(8,128)(2,1)S(1)}, u32[]{:S(2)}, u32[]{:S(2)}) collective-permute-start(bf16[256,128]{1,0:T(8,128)(2,1)S(1)} %get-tuple-element.59), channel_id=1, source_target_pairs={{0,6},{1,7},{2,0},{3,1},{4,2},{5,3},{6,4},{7,5},{8,14},{9,15},{10,... | collective-permute-start | bytes 196616 | tf_op jit(solution)/shard_map/ppermute | solution.py:521
  79.1 1.3 %shard_map.92 = (f32[64,64]{1,0:T(8,128)S(1)}, f32[32,128]{1,0:T(8,128)}, f32[4,128]{1,0:T(4,128)S(1)}) custom-call(s32[8]{0:T(128)S(1)} %copy-done.1, bf16[224,128]{1,0:T(8,128)(2,1)S(1)} %get-tuple-element.52.refs_1_, bf16[224,128]{1,0:T(8,128)(2,1)S(1)} %collective-permute-done.30.refs_2_, bf16[224,128]{1,0:T(8,128)(2,1)S(1)} %collective-permute-done.31.refs_3_, ...), custom_call_target="tpu_custom_call" | custom-call | flops 16777216 | bytes 1048576 | tf_op jit(solution)/shard_map/pallas_call | solution.py:59
  80.4 1.2 %collective-permute-start.35 = (f32[64,64]{1,0:T(8,128)S(1)}, f32[64,64]{1,0:T(8,128)S(1)}, u32[]{:S(2)}, u32[]{:S(2)}) collective-permute-start(f32[64,64]{1,0:T(8,128)S(1)} %get-tuple-element.55.refs_0_), channel_id=1, source_target_pairs={{0,24},{8,0},{16,8},{24,16},{1,25},{9,1},{17,9},{25,17},{2,26},{10... | collective-permute-start | bytes 49160 | tf_op jit(solution)/shard_map/ppermute | solution.py:512
  84.3 2.1 %collective-permute-done.34.refs_2_ = f32[64,64]{1,0:T(8,128)S(1)} collective-permute-done((f32[64,64]{1,0:T(8,128)S(1)}, f32[64,64]{1,0:T(8,128)S(1)}, u32[]{:S(2)}, u32[]{:S(2)}) %collective-permute-start.34) | collective-permute-done | bytes 16416 | tf_op jit(solution)/shard_map/ppermute | solution.py:512
  86.4 1.8 %collective-permute-done.33.refs_1_ = f32[64,64]{1,0:T(8,128)S(1)} collective-permute-done((f32[64,64]{1,0:T(8,128)S(1)}, f32[64,64]{1,0:T(8,128)S(1)}, u32[]{:S(2)}, u32[]{:S(2)}) %collective-permute-start.33) | collective-permute-done | bytes 16416 | tf_op jit(solution)/shard_map/ppermute | solution.py:512
  88.3 3.2 %shard_map.93 = f32[64,512]{1,0:T(8,128)} custom-call(f32[64,64]{1,0:T(8,128)S(1)} %get-tuple-element.55.refs_0_, f32[64,64]{1,0:T(8,128)S(1)} %collective-permute-done.33.refs_1_, f32[64,64]{1,0:T(8,128)S(1)} %collective-permute-done.34.refs_2_, f32[64,64]{1,0:T(8,128)S(1)} %collective-permute-done.35.refs_3_, ...), custom_call_target="tpu_custom_call" | custom-call | flops 16777216 | bytes 1048576 | tf_op jit(solution)/shard_map/pallas_call | solution.py:59
  (61 shorter events, 13.6 us)
Async XLA Ops:
  2.2 8.7 %collective-permute-start.7 = (bf16[56,512]{1,0:T(8,128)(2,1)S(1)}, bf16[56,512]{1,0:T(8,128)(2,1)S(1)}, u32[]{:S(2)}, u32[]{:S(2)}) collective-permute-start(bf16[56,512]{1,0:T(8,128)(2,1)S(1)} %shard_map.85.refs_0_.pack), channel_id=1, source_target_pairs={{0,6},{1,7},{2,0},{3,1},{4,2},{5,3},{6,4},{7,5},{8,14},{9,15},{10,... | collective-permute-start | bytes 172040 | tf_op jit(solution)/shard_map/ppermute | solution.py:521
  6.1 5.7 %collective-permute-start.5 = (bf16[56,512]{1,0:T(8,128)(2,1)S(1)}, bf16[56,512]{1,0:T(8,128)(2,1)S(1)}, u32[]{:S(2)}, u32[]{:S(2)}) collective-permute-start(bf16[56,512]{1,0:T(8,128)(2,1)S(1)} %shard_map.85.refs_0_.pack), channel_id=1, source_target_pairs={{0,4},{1,5},{2,6},{3,7},{4,0},{5,1},{6,2},{7,3},{8,12},{9,13},{10,... | collective-permute-start | bytes 172040 | tf_op jit(solution)/shard_map/ppermute | solution.py:521
  6.6 5.2 %collective-permute-start.3 = (bf16[56,512]{1,0:T(8,128)(2,1)S(1)}, bf16[56,512]{1,0:T(8,128)(2,1)S(1)}, u32[]{:S(2)}, u32[]{:S(2)}) collective-permute-start(bf16[56,512]{1,0:T(8,128)(2,1)S(1)} %shard_map.85.refs_0_.pack), channel_id=1, source_target_pairs={{0,2},{1,3},{2,4},{3,5},{4,6},{5,7},{6,0},{7,1},{8,10},{9,11},{10,... | collective-permute-start | bytes 172040 | tf_op jit(solution)/shard_map/ppermute | solution.py:521
  7.2 5.4 %collective-permute-start.2 = (bf16[56,512]{1,0:T(8,128)(2,1)S(1)}, bf16[56,512]{1,0:T(8,128)(2,1)S(1)}, u32[]{:S(2)}, u32[]{:S(2)}) collective-permute-start(bf16[56,512]{1,0:T(8,128)(2,1)S(1)} %shard_map.85.refs_0_.pack), channel_id=1, source_target_pairs={{0,24},{8,0},{16,8},{24,16},{1,25},{9,1},{17,9},{25,17},{2,26},{10... | collective-permute-start | bytes 172040 | tf_op jit(solution)/shard_map/ppermute | solution.py:512
  10.8 5.1 %collective-permute-start.1 = (bf16[56,512]{1,0:T(8,128)(2,1)S(1)}, bf16[56,512]{1,0:T(8,128)(2,1)S(1)}, u32[]{:S(2)}, u32[]{:S(2)}) collective-permute-start(bf16[56,512]{1,0:T(8,128)(2,1)S(1)} %shard_map.85.refs_0_.pack), channel_id=1, source_target_pairs={{0,16},{8,24},{16,0},{24,8},{1,17},{9,25},{17,1},{25,9},{2,18},{10... | collective-permute-start | bytes 172040 | tf_op jit(solution)/shard_map/ppermute | solution.py:512
  10.8 6.0 %collective-permute-start = (bf16[56,512]{1,0:T(8,128)(2,1)S(1)}, bf16[56,512]{1,0:T(8,128)(2,1)S(1)}, u32[]{:S(2)}, u32[]{:S(2)}) collective-permute-start(bf16[56,512]{1,0:T(8,128)(2,1)S(1)} %shard_map.85.refs_0_.pack), channel_id=1, source_target_pairs={{0,8},{8,16},{16,24},{24,0},{1,9},{9,17},{17,25},{25,1},{2,10},{10... | collective-permute-start | bytes 172040 | tf_op jit(solution)/shard_map/ppermute | solution.py:512
  11.9 5.0 %collective-permute-start.8 = (bf16[56,512]{1,0:T(8,128)(2,1)S(1)}, bf16[56,512]{1,0:T(8,128)(2,1)S(1)}, u32[]{:S(2)}, u32[]{:S(2)}) collective-permute-start(bf16[56,512]{1,0:T(8,128)(2,1)S(1)} %collective-permute-done.7.refs_13_), channel_id=1, source_target_pairs={{0,1},{1,0},{2,3},{3,2},{4,5},{5,4},{6,7},{7,6},{8,9},{9,8},{10,11... | collective-permute-start | bytes 172040 | tf_op jit(solution)/shard_map/ppermute | solution.py:507
  11.9 5.0 %collective-permute-start.6 = (bf16[56,512]{1,0:T(8,128)(2,1)S(1)}, bf16[56,512]{1,0:T(8,128)(2,1)S(1)}, u32[]{:S(2)}, u32[]{:S(2)}) collective-permute-start(bf16[56,512]{1,0:T(8,128)(2,1)S(1)} %collective-permute-done.5.refs_9_), channel_id=1, source_target_pairs={{0,1},{1,0},{2,3},{3,2},{4,5},{5,4},{6,7},{7,6},{8,9},{9,8},{10,11... | collective-permute-start | bytes 172040 | tf_op jit(solution)/shard_map/ppermute | solution.py:507
  12.7 4.2 %collective-permute-start.4 = (bf16[56,512]{1,0:T(8,128)(2,1)S(1)}, bf16[56,512]{1,0:T(8,128)(2,1)S(1)}, u32[]{:S(2)}, u32[]{:S(2)}) collective-permute-start(bf16[56,512]{1,0:T(8,128)(2,1)S(1)} %collective-permute-done.3.refs_5_), channel_id=1, source_target_pairs={{0,1},{1,0},{2,3},{3,2},{4,5},{5,4},{6,7},{7,6},{8,9},{9,8},{10,11... | collective-permute-start | bytes 172040 | tf_op jit(solution)/shard_map/ppermute | solution.py:507
  16.9 5.2 %collective-permute-start.10 = (bf16[3,56,512]{2,1,0:T(8,128)(2,1)S(1)}, bf16[3,56,512]{2,1,0:T(8,128)(2,1)S(1)}, u32[]{:S(2)}, u32[]{:S(2)}) collective-permute-start(bf16[3,56,512]{2,1,0:T(8,128)(2,1)S(1)} %get-tuple-element.33.rest), channel_id=1, source_target_pairs={{0,1},{1,0},{2,3},{3,2},{4,5},{5,4},{6,7},{7,6},{8,9},{9,8},{10,11... | collective-permute-start | bytes 516104 | tf_op jit(solution)/shard_map/ppermute | solution.py:507
  17.0 10.0 %collective-permute-start.13 = (bf16[3,56,512]{2,1,0:T(8,128)(2,1)S(1)}, bf16[3,56,512]{2,1,0:T(8,128)(2,1)S(1)}, u32[]{:S(2)}, u32[]{:S(2)}) collective-permute-start(bf16[3,56,512]{2,1,0:T(8,128)(2,1)S(1)} %get-tuple-element.33.rest), channel_id=1, source_target_pairs={{0,6},{1,7},{2,0},{3,1},{4,2},{5,3},{6,4},{7,5},{8,14},{9,15},{10,... | collective-permute-start | bytes 516104 | tf_op jit(solution)/shard_map/ppermute | solution.py:521
  19.3 10.1 %collective-permute-start.12 = (bf16[3,56,512]{2,1,0:T(8,128)(2,1)S(1)}, bf16[3,56,512]{2,1,0:T(8,128)(2,1)S(1)}, u32[]{:S(2)}, u32[]{:S(2)}) collective-permute-start(bf16[3,56,512]{2,1,0:T(8,128)(2,1)S(1)} %get-tuple-element.33.rest), channel_id=1, source_target_pairs={{0,4},{1,5},{2,6},{3,7},{4,0},{5,1},{6,2},{7,3},{8,12},{9,13},{10,... | collective-permute-start | bytes 516104 | tf_op jit(solution)/shard_map/ppermute | solution.py:521
  20.9 8.6 %collective-permute-start.11 = (bf16[3,56,512]{2,1,0:T(8,128)(2,1)S(1)}, bf16[3,56,512]{2,1,0:T(8,128)(2,1)S(1)}, u32[]{:S(2)}, u32[]{:S(2)}) collective-permute-start(bf16[3,56,512]{2,1,0:T(8,128)(2,1)S(1)} %get-tuple-element.33.rest), channel_id=1, source_target_pairs={{0,2},{1,3},{2,4},{3,5},{4,6},{5,7},{6,0},{7,1},{8,10},{9,11},{10,... | collective-permute-start | bytes 516104 | tf_op jit(solution)/shard_map/ppermute | solution.py:521
  37.9 4.6 %collective-permute-start.21 = (bf16[64,512]{1,0:T(8,128)(2,1)}, bf16[64,512]{1,0:T(8,128)(2,1)S(1)}, u32[]{:S(2)}, u32[]{:S(2)}) collective-permute-start(bf16[64,512]{1,0:T(8,128)(2,1)} %refs_8_), channel_id=1, source_target_pairs={{0,8},{8,0},{16,24},{24,16},{1,9},{9,1},{17,25},{25,17},{2,10},{10... | collective-permute-start | bytes 196616 | tf_op jit(solution)/shard_map/ppermute | solution.py:507
  39.0 4.0 %collective-permute-start.20 = (bf16[128,128]{1,0:T(8,128)(2,1)S(1)}, bf16[128,128]{1,0:T(8,128)(2,1)S(1)}, u32[]{:S(2)}, u32[]{:S(2)}) collective-permute-start(bf16[128,128]{1,0:T(8,128)(2,1)S(1)} %add_convert_fusion.1.refs_3_), channel_id=1, source_target_pairs={{0,6},{1,7},{2,0},{3,1},{4,2},{5,3},{6,4},{7,5},{8,14},{9,15},{10,... | collective-permute-start | bytes 98312 | tf_op jit(solution)/shard_map/ppermute | solution.py:521
  40.3 4.3 %collective-permute-start.19 = (bf16[128,128]{1,0:T(8,128)(2,1)S(1)}, bf16[128,128]{1,0:T(8,128)(2,1)S(1)}, u32[]{:S(2)}, u32[]{:S(2)}) collective-permute-start(bf16[128,128]{1,0:T(8,128)(2,1)S(1)} %add_convert_fusion.1.refs_3_), channel_id=1, source_target_pairs={{0,4},{1,5},{2,6},{3,7},{4,0},{5,1},{6,2},{7,3},{8,12},{9,13},{10,... | collective-permute-start | bytes 98312 | tf_op jit(solution)/shard_map/ppermute | solution.py:521
  40.9 4.8 %collective-permute-start.18 = (bf16[128,128]{1,0:T(8,128)(2,1)S(1)}, bf16[128,128]{1,0:T(8,128)(2,1)S(1)}, u32[]{:S(2)}, u32[]{:S(2)}) collective-permute-start(bf16[128,128]{1,0:T(8,128)(2,1)S(1)} %add_convert_fusion.1.refs_3_), channel_id=1, source_target_pairs={{0,2},{1,3},{2,4},{3,5},{4,6},{5,7},{6,0},{7,1},{8,10},{9,11},{10,... | collective-permute-start | bytes 98312 | tf_op jit(solution)/shard_map/ppermute | solution.py:521
  52.2 3.1 %collective-permute-start.22 = (f32[128,128]{1,0:T(8,128)S(1)}, f32[128,128]{1,0:T(8,128)S(1)}, u32[]{:S(2)}, u32[]{:S(2)}) collective-permute-start(f32[128,128]{1,0:T(8,128)S(1)} %shard_map.89), channel_id=1, source_target_pairs={{0,1},{1,0},{2,3},{3,2},{4,5},{5,4},{6,7},{7,6},{8,9},{9,8},{10,11... | collective-permute-start | bytes 196616 | tf_op jit(solution)/shard_map/ppermute | solution.py:507
  52.3 8.6 %collective-permute-start.26 = (bf16[64,512]{1,0:T(8,128)(2,1)S(1)}, bf16[64,512]{1,0:T(8,128)(2,1)S(1)}, u32[]{:S(2)}, u32[]{:S(2)}) collective-permute-start(bf16[64,512]{1,0:T(8,128)(2,1)S(1)} %copy-done), channel_id=1, source_target_pairs={{0,16},{8,24},{16,0},{24,8},{1,17},{9,25},{17,1},{25,9},{2,18},{10... | collective-permute-start | bytes 196616 | tf_op jit(solution)/shard_map/ppermute | solution.py:507
  53.5 8.4 %collective-permute-start.27 = (bf16[64,512]{1,0:T(8,128)(2,1)S(1)}, bf16[64,512]{1,0:T(8,128)(2,1)S(1)}, u32[]{:S(2)}, u32[]{:S(2)}) collective-permute-start(bf16[64,512]{1,0:T(8,128)(2,1)S(1)} %collective-permute-done.21.refs_7_.refs_9_), channel_id=1, source_target_pairs={{0,16},{8,24},{16,0},{24,8},{1,17},{9,25},{17,1},{25,9},{2,18},{10... | collective-permute-start | bytes 196616 | tf_op jit(solution)/shard_map/ppermute | solution.py:507
  55.3 6.6 %collective-permute-start.25 = (bf16[128,128]{1,0:T(8,128)(2,1)S(1)}, bf16[128,128]{1,0:T(8,128)(2,1)S(1)}, u32[]{:S(2)}, u32[]{:S(2)}) collective-permute-start(bf16[128,128]{1,0:T(8,128)(2,1)S(1)} %add_convert_fusion.refs_4_), channel_id=1, source_target_pairs={{0,6},{1,7},{2,0},{3,1},{4,2},{5,3},{6,4},{7,5},{8,14},{9,15},{10,... | collective-permute-start | bytes 98312 | tf_op jit(solution)/shard_map/ppermute | solution.py:521
  56.0 5.8 %collective-permute-start.24 = (bf16[128,128]{1,0:T(8,128)(2,1)S(1)}, bf16[128,128]{1,0:T(8,128)(2,1)S(1)}, u32[]{:S(2)}, u32[]{:S(2)}) collective-permute-start(bf16[128,128]{1,0:T(8,128)(2,1)S(1)} %add_convert_fusion.refs_4_), channel_id=1, source_target_pairs={{0,4},{1,5},{2,6},{3,7},{4,0},{5,1},{6,2},{7,3},{8,12},{9,13},{10,... | collective-permute-start | bytes 98312 | tf_op jit(solution)/shard_map/ppermute | solution.py:521
  57.6 4.8 %collective-permute-start.23 = (bf16[128,128]{1,0:T(8,128)(2,1)S(1)}, bf16[128,128]{1,0:T(8,128)(2,1)S(1)}, u32[]{:S(2)}, u32[]{:S(2)}) collective-permute-start(bf16[128,128]{1,0:T(8,128)(2,1)S(1)} %add_convert_fusion.refs_4_), channel_id=1, source_target_pairs={{0,2},{1,3},{2,4},{3,5},{4,6},{5,7},{6,0},{7,1},{8,10},{9,11},{10,... | collective-permute-start | bytes 98312 | tf_op jit(solution)/shard_map/ppermute | solution.py:521
  71.3 4.7 %collective-permute-start.32 = (bf16[224,128]{1,0:T(8,128)(2,1)S(1)}, bf16[224,128]{1,0:T(8,128)(2,1)S(1)}, u32[]{:S(2)}, u32[]{:S(2)}) collective-permute-start(bf16[224,128]{1,0:T(8,128)(2,1)S(1)} %get-tuple-element.52.refs_1_), channel_id=1, source_target_pairs={{0,6},{1,7},{2,0},{3,1},{4,2},{5,3},{6,4},{7,5},{8,14},{9,15},{10,... | collective-permute-start | bytes 172040 | tf_op jit(solution)/shard_map/ppermute | solution.py:521
  71.4 11.2 %collective-permute-start.36 = (bf16[256,128]{1,0:T(8,128)(2,1)S(1)}, bf16[256,128]{1,0:T(8,128)(2,1)S(1)}, u32[]{:S(2)}, u32[]{:S(2)}) collective-permute-start(bf16[256,128]{1,0:T(8,128)(2,1)S(1)} %get-tuple-element.57), channel_id=1, source_target_pairs={{0,2},{1,3},{2,4},{3,5},{4,6},{5,7},{6,0},{7,1},{8,10},{9,11},{10,... | collective-permute-start | bytes 196616 | tf_op jit(solution)/shard_map/ppermute | solution.py:521
  73.4 5.7 %collective-permute-start.31 = (bf16[224,128]{1,0:T(8,128)(2,1)S(1)}, bf16[224,128]{1,0:T(8,128)(2,1)S(1)}, u32[]{:S(2)}, u32[]{:S(2)}) collective-permute-start(bf16[224,128]{1,0:T(8,128)(2,1)S(1)} %get-tuple-element.52.refs_1_), channel_id=1, source_target_pairs={{0,4},{1,5},{2,6},{3,7},{4,0},{5,1},{6,2},{7,3},{8,12},{9,13},{10,... | collective-permute-start | bytes 172040 | tf_op jit(solution)/shard_map/ppermute | solution.py:521
  73.4 5.7 %collective-permute-start.30 = (bf16[224,128]{1,0:T(8,128)(2,1)S(1)}, bf16[224,128]{1,0:T(8,128)(2,1)S(1)}, u32[]{:S(2)}, u32[]{:S(2)}) collective-permute-start(bf16[224,128]{1,0:T(8,128)(2,1)S(1)} %get-tuple-element.52.refs_1_), channel_id=1, source_target_pairs={{0,2},{1,3},{2,4},{3,5},{4,6},{5,7},{6,0},{7,1},{8,10},{9,11},{10,... | collective-permute-start | bytes 172040 | tf_op jit(solution)/shard_map/ppermute | solution.py:521
  74.9 8.6 %collective-permute-start.37 = (bf16[256,128]{1,0:T(8,128)(2,1)S(1)}, bf16[256,128]{1,0:T(8,128)(2,1)S(1)}, u32[]{:S(2)}, u32[]{:S(2)}) collective-permute-start(bf16[256,128]{1,0:T(8,128)(2,1)S(1)} %get-tuple-element.58), channel_id=1, source_target_pairs={{0,4},{1,5},{2,6},{3,7},{4,0},{5,1},{6,2},{7,3},{8,12},{9,13},{10,... | collective-permute-start | bytes 196616 | tf_op jit(solution)/shard_map/ppermute | solution.py:521
  76.0 7.5 %collective-permute-start.38 = (bf16[256,128]{1,0:T(8,128)(2,1)S(1)}, bf16[256,128]{1,0:T(8,128)(2,1)S(1)}, u32[]{:S(2)}, u32[]{:S(2)}) collective-permute-start(bf16[256,128]{1,0:T(8,128)(2,1)S(1)} %get-tuple-element.59), channel_id=1, source_target_pairs={{0,6},{1,7},{2,0},{3,1},{4,2},{5,3},{6,4},{7,5},{8,14},{9,15},{10,... | collective-permute-start | bytes 196616 | tf_op jit(solution)/shard_map/ppermute | solution.py:521
  80.4 3.9 %collective-permute-start.35 = (f32[64,64]{1,0:T(8,128)S(1)}, f32[64,64]{1,0:T(8,128)S(1)}, u32[]{:S(2)}, u32[]{:S(2)}) collective-permute-start(f32[64,64]{1,0:T(8,128)S(1)} %get-tuple-element.55.refs_0_), channel_id=1, source_target_pairs={{0,24},{8,0},{16,8},{24,16},{1,25},{9,1},{17,9},{25,17},{2,26},{10... | collective-permute-start | bytes 49160 | tf_op jit(solution)/shard_map/ppermute | solution.py:512
  81.6 4.8 %collective-permute-start.34 = (f32[64,64]{1,0:T(8,128)S(1)}, f32[64,64]{1,0:T(8,128)S(1)}, u32[]{:S(2)}, u32[]{:S(2)}) collective-permute-start(f32[64,64]{1,0:T(8,128)S(1)} %get-tuple-element.55.refs_0_), channel_id=1, source_target_pairs={{0,16},{8,24},{16,0},{24,8},{1,17},{9,25},{17,1},{25,9},{2,18},{10... | collective-permute-start | bytes 49160 | tf_op jit(solution)/shard_map/ppermute | solution.py:512
  82.5 5.7 %collective-permute-start.33 = (f32[64,64]{1,0:T(8,128)S(1)}, f32[64,64]{1,0:T(8,128)S(1)}, u32[]{:S(2)}, u32[]{:S(2)}) collective-permute-start(f32[64,64]{1,0:T(8,128)S(1)} %get-tuple-element.55.refs_0_), channel_id=1, source_target_pairs={{0,8},{8,16},{16,24},{24,0},{1,9},{9,17},{17,25},{25,1},{2,10},{10... | collective-permute-start | bytes 49160 | tf_op jit(solution)/shard_map/ppermute | solution.py:512
  (9 other events, 105.9 us)

commit v5 on v4

--- a/solution.py
+++ b/solution.py
@@ -10,7 +10,6 @@
 BLK = 128
 SWEEPS = 3
 GROUP = 32
-BUILD_GROUP = 32
 TILE_GROUP = 16
 ROWS, COLUMNS, COUNT = 0, 1, 2
 FEAT = 64
@@ -132,6 +131,9 @@
         self.blocks, self.base = (own, 0) if k == 0 else (others, (k - 1) * slots)
         self.total = table[self.group * 8 + COUNT, 0]
 
+    def group_size(self, times):
+        return times * GROUP if self.k == 0 else GROUP
+
     def row(self, s):
         return self.table[self.group * 8 + ROWS, s]
 
@@ -173,7 +175,7 @@
         sums = jnp.sum(product.reshape(BLK // 8, 8, BLK), axis=0)
         acc[jnp.where(s < tile.total, first + tile.row(s), spare)] += sums
 
-    slot_loop(step, tile.total, 1, GROUP)
+    slot_loop(step, tile.total, 1, tile.group_size(2))
 
 
 def spread_lanes(wide, scaling):
@@ -205,7 +207,7 @@
         targets = [jnp.where(s < tile.total, tile.column(s), spare) for s in slots]
         add_rows(acc, sums, firsts, targets)
 
-    slot_loop(step, tile.total, 4, 2 * GROUP if tile.k == 0 else GROUP)
+    slot_loop(step, tile.total, 4, tile.group_size(4))
 
 
 def fill_pieces(left, scaling):
@@ -234,7 +236,7 @@
         block = jnp.exp2(distance * col_inv[column] * row_inv[row][0:1, :])
         tile.blocks[tile.base + s] = block.astype(BF16)
 
-    slot_loop(step, tile.total, 1, BUILD_GROUP)
+    slot_loop(step, tile.total, 1, tile.group_size(2))
 
 
 def piece_block(pieces, k, j):
@@ -384,7 +386,7 @@
             sums = jnp.dot(scaled[tile.column(s)], tile.block(s), preferred_element_type=F32)
             acc[target] += sums[0 : cols + 8]
 
-        slot_loop(step, jnp.where(tile.group == me_row, tile.total, 0), 1, BUILD_GROUP)
+        slot_loop(step, jnp.where(tile.group == me_row, tile.total, 0), 1, tile.group_size(2))
     core = lax.rem(me_col, 2)
     for q in range(n_chip):
         mine = (2 * q + core) * per
@@ -472,11 +474,12 @@
         change = None
         for i in range(WIDE):
             pivot = first + i
-            unit_top = tops[i] / sides[i][pivot : pivot + 1, :]
+            inverse = 1.0 / sides[i][pivot : pivot + 1, :]
+            unit_top = tops[i] * inverse
             for m in range(i + 1, WIDE):
                 factor = sides[i][first + m : first + m + 1, :]
                 tops[m] = tops[m] - factor * unit_top
-                inner = factor / sides[i][pivot : pivot + 1, :]
+                inner = factor * inverse
                 sides[m] = sides[m] - sides[i] * inner
             term = sides[i] * unit_top
             change = term if change is None else change + term
@@ -565,10 +568,11 @@
     )
     near = [chip_shift(packed, k) for k in range(1, n_chip)]
     near_in = [sibling(pack) for pack in near]
+    pack_in = sibling(packed)
     rest, table = call(
         functools.partial(stack_kernel, pcs, n_row),
         [shape(n_row - 1, PACK, share, dtype=BF16), shape(n_row, 8, BLK, dtype=jnp.int32)],
-        vec(*shifts(packed, "row")) + [("near", pack) for pack in near_in],
+        vec(*shifts(packed, "row")) + [("near", pack) for pack in near_in + [pack_in]],
     )
     table = ("smem", table.reshape(n_row * 8, BLK))
     marks = ("smem", landmarks)
@@ -581,7 +585,7 @@
             pltpu.VMEM((col_blocks, BLK, BLK), F32),
             shape(col_blocks, BLK),
         ],
-        [table] + vec(packed, rest, sibling(packed), sibling(rest)),
+        [table] + vec(packed, rest, pack_in, sibling(rest)),
         [
             pltpu.VMEM((row_blocks, FEAT, BLK), BF16),
             pltpu.VMEM((row_blocks, 8, BLK), F32),

time: 91.6 us -> 91.1 us (level)
  Pallas kernels: 30.3 us -> 29.2 us
    ppermute x18, waiting for transfers between devices: 7.52 us -> 9.12 us  [chip_shift(): lax.ppermute(x, 'col', [(2 * q + p, 2 * ((q + k) % n) + p) for q in range...]
    ppermute x15, waiting for transfers between devices: 7.93 us -> 6.61 us  [swap(): lax.ppermute(x, axis, [(i, i ^ k) for i in range(lax.axis_size(axis))])]
    pallas_call x9, Pallas kernels: 30.3 us -> 29.2 us  [call(): pl.pallas_call(kernel, out_shape=tuple(outs), in_specs=specs, out_specs=t...]
  transfers between devices with their start and end apart: 39 -> 39, of which waited for: 21 -> 20; matrix products, arithmetic and copies ran while one was open for 0% -> 0% of each run, Pallas kernels for 7% -> 6%
where the time goes in v5:
time: 91.1 us; the launch traced here: 90.9 us
  starting transfers between devices  35.6 us (39%)
  Pallas kernels  29.2 us (32%)
  waiting for transfers between devices  24.7 us (27%)
  between operations  1.42 us (2%)
    pallas_call x9, Pallas kernels, call(): pl.pallas_call(kernel, out_shape=tuple(outs), in_specs=specs, out_specs=t...  29.2 us
    ppermute x18, starting transfers between devices, chip_shift(): lax.ppermute(x, 'col', [(2 * q + p, 2 * ((q + k) % n) + p) for q in range...  22 us
    ppermute x18, waiting for transfers between devices, chip_shift(): lax.ppermute(x, 'col', [(2 * q + p, 2 * ((q + k) % n) + p) for q in range...  9.12 us
    ppermute x6, waiting for transfers between devices, shift(): return lax.ppermute(x, axis, [(i, (i + k) % n) for i in range(n)])  8.94 us
    ppermute x6, starting transfers between devices, shift(): return lax.ppermute(x, axis, [(i, (i + k) % n) for i in range(n)])  8.07 us
    ppermute x15, waiting for transfers between devices, swap(): lax.ppermute(x, axis, [(i, i ^ k) for i in range(lax.axis_size(axis))])  6.61 us
    ppermute x15, starting transfers between devices, swap(): lax.ppermute(x, axis, [(i, i ^ k) for i in range(lax.axis_size(axis))])  5.48 us
  transfers between devices with their start and end apart: 39, of which 20 were waited for; matrix products, arithmetic and copies ran while one was open for 0% of the time, Pallas kernels for 6%

profile of v5, /device:TPU:0, one launch (start us, length us, event | category | flops | bytes accessed | tf_op | source)
XLA Modules:
  0.0 90.9 jit_solution(4360975423540322663)
XLA Ops:
  2.7 3.5 %collective-permute-start.7 = (bf16[56,512]{1,0:T(8,128)(2,1)S(1)}, bf16[56,512]{1,0:T(8,128)(2,1)S(1)}, u32[]{:S(2)}, u32[]{:S(2)}) collective-permute-start(bf16[56,512]{1,0:T(8,128)(2,1)S(1)} %shard_map.85.refs_0_.pack), channel_id=1, source_target_pairs={{0,6},{1,7},{2,0},{3,1},{4,2},{5,3},{6,4},{7,5},{8,14},{9,15},{10,... | collective-permute-start | bytes 172040 | tf_op jit(solution)/shard_map/ppermute | solution.py:524
  7.3 3.6 %collective-permute-start.2 = (bf16[56,512]{1,0:T(8,128)(2,1)S(1)}, bf16[56,512]{1,0:T(8,128)(2,1)S(1)}, u32[]{:S(2)}, u32[]{:S(2)}) collective-permute-start(bf16[56,512]{1,0:T(8,128)(2,1)S(1)} %shard_map.85.refs_0_.pack), channel_id=1, source_target_pairs={{0,24},{8,0},{16,8},{24,16},{1,25},{9,1},{17,9},{25,17},{2,26},{10... | collective-permute-start | bytes 172040 | tf_op jit(solution)/shard_map/ppermute | solution.py:515
  10.9 1.0 %collective-permute-start = (bf16[56,512]{1,0:T(8,128)(2,1)S(1)}, bf16[56,512]{1,0:T(8,128)(2,1)S(1)}, u32[]{:S(2)}, u32[]{:S(2)}) collective-permute-start(bf16[56,512]{1,0:T(8,128)(2,1)S(1)} %shard_map.85.refs_0_.pack), channel_id=1, source_target_pairs={{0,8},{8,16},{16,24},{24,0},{1,9},{9,17},{17,25},{25,1},{2,10},{10... | collective-permute-start | bytes 172040 | tf_op jit(solution)/shard_map/ppermute | solution.py:515
  13.1 2.9 %collective-permute-done.1.refs_2_ = bf16[56,512]{1,0:T(8,128)(2,1)S(1)} collective-permute-done((bf16[56,512]{1,0:T(8,128)(2,1)S(1)}, bf16[56,512]{1,0:T(8,128)(2,1)S(1)}, u32[]{:S(2)}, u32[]{:S(2)}) %collective-permute-start.1) | collective-permute-done | bytes 57376 | tf_op jit(solution)/shard_map/ppermute | solution.py:515
  16.0 1.0 %collective-permute-done.refs_1_ = bf16[56,512]{1,0:T(8,128)(2,1)S(1)} collective-permute-done((bf16[56,512]{1,0:T(8,128)(2,1)S(1)}, bf16[56,512]{1,0:T(8,128)(2,1)S(1)}, u32[]{:S(2)}, u32[]{:S(2)}) %collective-permute-start) | collective-permute-done | bytes 57376 | tf_op jit(solution)/shard_map/ppermute | solution.py:515
  17.1 2.4 %collective-permute-start.13 = (bf16[3,56,512]{2,1,0:T(8,128)(2,1)S(1)}, bf16[3,56,512]{2,1,0:T(8,128)(2,1)S(1)}, u32[]{:S(2)}, u32[]{:S(2)}) collective-permute-start(bf16[3,56,512]{2,1,0:T(8,128)(2,1)S(1)} %get-tuple-element.33.rest), channel_id=1, source_target_pairs={{0,6},{1,7},{2,0},{3,1},{4,2},{5,3},{6,4},{7,5},{8,14},{9,15},{10,... | collective-permute-start | bytes 516104 | tf_op jit(solution)/shard_map/ppermute | solution.py:524
  19.5 1.5 %collective-permute-start.12 = (bf16[3,56,512]{2,1,0:T(8,128)(2,1)S(1)}, bf16[3,56,512]{2,1,0:T(8,128)(2,1)S(1)}, u32[]{:S(2)}, u32[]{:S(2)}) collective-permute-start(bf16[3,56,512]{2,1,0:T(8,128)(2,1)S(1)} %get-tuple-element.33.rest), channel_id=1, source_target_pairs={{0,4},{1,5},{2,6},{3,7},{4,0},{5,1},{6,2},{7,3},{8,12},{9,13},{10,... | collective-permute-start | bytes 516104 | tf_op jit(solution)/shard_map/ppermute | solution.py:524
  21.0 4.4 %shard_map.87 = (bf16[128,128,128]{2,1,0:T(8,128)(2,1)S(1)}, bf16[16,128,64]{2,1,0:T(8,128)(2,1)S(1)}, f32[16,128,128]{2,1,0:T(8,128)S(1)}, f32[16,128]{1,0:T(8,128)S(1)}) custom-call(s32[32,128]{1,0:T(8,128)S(1)} %bitcast.3, bf16[56,512]{1,0:T(8,128)(2,1)S(1)} %shard_map.85.refs_0_.pack, bf16[3,56,512]{2,1,0:T(8,128)(2,1)S(1)} %get-tuple-element.33.rest, ...), custom_call_target="tpu_custom_call" | custom-call | flops 16777216 | bytes 1048576 | tf_op jit(solution)/shard_map/pallas_call | solution.py:58
  25.4 4.2 %collective-permute-done.12.refs_10_ = bf16[3,56,512]{2,1,0:T(8,128)(2,1)S(1)} collective-permute-done((bf16[3,56,512]{2,1,0:T(8,128)(2,1)S(1)}, bf16[3,56,512]{2,1,0:T(8,128)(2,1)S(1)}, u32[]{:S(2)}, u32[]{:S(2)}) %collective-permute-start.12) | collective-permute-done | bytes 172064 | tf_op jit(solution)/shard_map/ppermute | solution.py:524
  31.5 6.2 %shard_map.88 = (bf16[384,128,128]{2,1,0:T(8,128)(2,1)S(1)}, f32[128,128]{1,0:T(8,128)S(1)}) custom-call(s32[32,128]{1,0:T(8,128)S(1)} %bitcast.4, bf16[128,128,128]{2,1,0:T(8,128)(2,1)S(1)} %get-tuple-element.34.refs_1_.refs_2_, bf16[16,128,64]{2,1,0:T(8,128)(2,1)S(1)} %get-tuple-element.35.refs_2_, f32[16,128,128]{2,1,0:T(8,128)S(1)} %get-tuple-element.36.refs_3_, ...), custom_call_target="tpu_custom_call" | custom-call | flops 16777216 | bytes 1048576 | tf_op jit(solution)/shard_map/pallas_call | solution.py:58
  38.1 1.0 %collective-permute-done.17 = f32[128,128]{1,0:T(8,128)S(1)} collective-permute-done((f32[128,128]{1,0:T(8,128)S(1)}, f32[128,128]{1,0:T(8,128)S(1)}, u32[]{:S(2)}, u32[]{:S(2)}) %collective-permute-start.17) | collective-permute-done | bytes 65568 | tf_op jit(solution)/shard_map/ppermute | solution.py:510
  39.1 1.3 %collective-permute-start.20 = (bf16[128,128]{1,0:T(8,128)(2,1)S(1)}, bf16[128,128]{1,0:T(8,128)(2,1)S(1)}, u32[]{:S(2)}, u32[]{:S(2)}) collective-permute-start(bf16[128,128]{1,0:T(8,128)(2,1)S(1)} %add_convert_fusion.1.refs_3_), channel_id=1, source_target_pairs={{0,6},{1,7},{2,0},{3,1},{4,2},{5,3},{6,4},{7,5},{8,14},{9,15},{10,... | collective-permute-start | bytes 98312 | tf_op jit(solution)/shard_map/ppermute | solution.py:524
  40.9 1.7 %collective-permute-start.18 = (bf16[128,128]{1,0:T(8,128)(2,1)S(1)}, bf16[128,128]{1,0:T(8,128)(2,1)S(1)}, u32[]{:S(2)}, u32[]{:S(2)}) collective-permute-start(bf16[128,128]{1,0:T(8,128)(2,1)S(1)} %add_convert_fusion.1.refs_3_), channel_id=1, source_target_pairs={{0,2},{1,3},{2,4},{3,5},{4,6},{5,7},{6,0},{7,1},{8,10},{9,11},{10,... | collective-permute-start | bytes 98312 | tf_op jit(solution)/shard_map/ppermute | solution.py:524
  43.1 1.6 %collective-permute-done.19.refs_5_ = bf16[128,128]{1,0:T(8,128)(2,1)S(1)} collective-permute-done((bf16[128,128]{1,0:T(8,128)(2,1)S(1)}, bf16[128,128]{1,0:T(8,128)(2,1)S(1)}, u32[]{:S(2)}, u32[]{:S(2)}) %collective-permute-start.19) | collective-permute-done | bytes 32800 | tf_op jit(solution)/shard_map/ppermute | solution.py:524
  44.7 1.0 %collective-permute-done.18.refs_4_ = bf16[128,128]{1,0:T(8,128)(2,1)S(1)} collective-permute-done((bf16[128,128]{1,0:T(8,128)(2,1)S(1)}, bf16[128,128]{1,0:T(8,128)(2,1)S(1)}, u32[]{:S(2)}, u32[]{:S(2)}) %collective-permute-start.18) | collective-permute-done | bytes 32800 | tf_op jit(solution)/shard_map/ppermute | solution.py:524
  45.7 6.5 %shard_map.89 = f32[128,128]{1,0:T(8,128)S(1)} custom-call(s32[32,128]{1,0:T(8,128)S(1)} %bitcast.5, bf16[128,128,128]{2,1,0:T(8,128)(2,1)S(1)} %get-tuple-element.34.refs_1_.refs_2_, bf16[384,128,128]{2,1,0:T(8,128)(2,1)S(1)} %get-tuple-element.42.refs_2_.refs_3_, bf16[128,128]{1,0:T(8,128)(2,1)S(1)} %add_convert_fusion.1.refs_3_, ...), custom_call_target="tpu_custom_call" | custom-call | flops 16777216 | bytes 1048576 | tf_op jit(solution)/shard_map/pallas_call | solution.py:58
  52.3 1.4 %collective-permute-start.26 = (bf16[64,512]{1,0:T(8,128)(2,1)S(1)}, bf16[64,512]{1,0:T(8,128)(2,1)S(1)}, u32[]{:S(2)}, u32[]{:S(2)}) collective-permute-start(bf16[64,512]{1,0:T(8,128)(2,1)S(1)} %copy-done), channel_id=1, source_target_pairs={{0,16},{8,24},{16,0},{24,8},{1,17},{9,25},{17,1},{25,9},{2,18},{10... | collective-permute-start | bytes 196616 | tf_op jit(solution)/shard_map/ppermute | solution.py:510
  53.8 1.6 %collective-permute-start.27 = (bf16[64,512]{1,0:T(8,128)(2,1)S(1)}, bf16[64,512]{1,0:T(8,128)(2,1)S(1)}, u32[]{:S(2)}, u32[]{:S(2)}) collective-permute-start(bf16[64,512]{1,0:T(8,128)(2,1)S(1)} %collective-permute-done.21.refs_7_.refs_9_), channel_id=1, source_target_pairs={{0,16},{8,24},{16,0},{24,8},{1,17},{9,25},{17,1},{25,9},{2,18},{10... | collective-permute-start | bytes 196616 | tf_op jit(solution)/shard_map/ppermute | solution.py:510
  56.2 1.4 %collective-permute-start.24 = (bf16[128,128]{1,0:T(8,128)(2,1)S(1)}, bf16[128,128]{1,0:T(8,128)(2,1)S(1)}, u32[]{:S(2)}, u32[]{:S(2)}) collective-permute-start(bf16[128,128]{1,0:T(8,128)(2,1)S(1)} %add_convert_fusion.refs_4_), channel_id=1, source_target_pairs={{0,4},{1,5},{2,6},{3,7},{4,0},{5,1},{6,2},{7,3},{8,12},{9,13},{10,... | collective-permute-start | bytes 98312 | tf_op jit(solution)/shard_map/ppermute | solution.py:524
  57.6 1.2 %collective-permute-start.23 = (bf16[128,128]{1,0:T(8,128)(2,1)S(1)}, bf16[128,128]{1,0:T(8,128)(2,1)S(1)}, u32[]{:S(2)}, u32[]{:S(2)}) collective-permute-start(bf16[128,128]{1,0:T(8,128)(2,1)S(1)} %add_convert_fusion.refs_4_), channel_id=1, source_target_pairs={{0,2},{1,3},{2,4},{3,5},{4,6},{5,7},{6,0},{7,1},{8,10},{9,11},{10,... | collective-permute-start | bytes 98312 | tf_op jit(solution)/shard_map/ppermute | solution.py:524
  58.9 2.1 %collective-permute-done.26.refs_10_ = bf16[64,512]{1,0:T(8,128)(2,1)S(1)} collective-permute-done((bf16[64,512]{1,0:T(8,128)(2,1)S(1)}, bf16[64,512]{1,0:T(8,128)(2,1)S(1)}, u32[]{:S(2)}, u32[]{:S(2)}) %collective-permute-start.26) | collective-permute-done | bytes 65568 | tf_op jit(solution)/shard_map/ppermute | solution.py:510
  62.5 6.5 %shard_map.90 = (f32[4,4,64,128]{3,2,1,0:T(8,128)S(1)}, bf16[4,4,64,128]{3,2,1,0:T(8,128)(2,1)S(1)}, bf16[224,128]{1,0:T(8,128)(2,1)S(1)}, f32[16,128]{1,0:T(8,128)}) custom-call(s32[32,128]{1,0:T(8,128)S(1)} %bitcast.6, s32[8]{0:T(128)S(1)} %copy-done.1, bf16[128,128,128]{2,1,0:T(8,128)(2,1)S(1)} %get-tuple-element.34.refs_1_.refs_2_, ...), custom_call_target="tpu_custom_call" | custom-call | flops 16777216 | bytes 1048576 | tf_op jit(solution)/shard_map/pallas_call | solution.py:58
  69.5 1.1 %collective-permute-done.29.both_in = bf16[224,128]{1,0:T(8,128)(2,1)S(1)} collective-permute-done((bf16[224,128]{1,0:T(8,128)(2,1)S(1)}, bf16[224,128]{1,0:T(8,128)(2,1)S(1)}, u32[]{:S(2)}, u32[]{:S(2)}) %collective-permute-start.29) | collective-permute-done | bytes 57376 | tf_op jit(solution)/shard_map/ppermute | solution.py:510
  70.8 2.0 %collective-permute-start.36 = (bf16[256,128]{1,0:T(8,128)(2,1)S(1)}, bf16[256,128]{1,0:T(8,128)(2,1)S(1)}, u32[]{:S(2)}, u32[]{:S(2)}) collective-permute-start(bf16[256,128]{1,0:T(8,128)(2,1)S(1)} %get-tuple-element.57), channel_id=1, source_target_pairs={{0,2},{1,3},{2,4},{3,5},{4,6},{5,7},{6,0},{7,1},{8,10},{9,11},{10,... | collective-permute-start | bytes 196616 | tf_op jit(solution)/shard_map/ppermute | solution.py:524
  72.8 1.5 %collective-permute-start.30 = (bf16[224,128]{1,0:T(8,128)(2,1)S(1)}, bf16[224,128]{1,0:T(8,128)(2,1)S(1)}, u32[]{:S(2)}, u32[]{:S(2)}) collective-permute-start(bf16[224,128]{1,0:T(8,128)(2,1)S(1)} %get-tuple-element.52.refs_1_), channel_id=1, source_target_pairs={{0,2},{1,3},{2,4},{3,5},{4,6},{5,7},{6,0},{7,1},{8,10},{9,11},{10,... | collective-permute-start | bytes 172040 | tf_op jit(solution)/shard_map/ppermute | solution.py:524
  75.4 2.3 %collective-permute-start.38 = (bf16[256,128]{1,0:T(8,128)(2,1)S(1)}, bf16[256,128]{1,0:T(8,128)(2,1)S(1)}, u32[]{:S(2)}, u32[]{:S(2)}) collective-permute-start(bf16[256,128]{1,0:T(8,128)(2,1)S(1)} %get-tuple-element.59), channel_id=1, source_target_pairs={{0,6},{1,7},{2,0},{3,1},{4,2},{5,3},{6,4},{7,5},{8,14},{9,15},{10,... | collective-permute-start | bytes 196616 | tf_op jit(solution)/shard_map/ppermute | solution.py:524
  78.5 1.3 %shard_map.92 = (f32[64,64]{1,0:T(8,128)S(1)}, f32[32,128]{1,0:T(8,128)}, f32[4,128]{1,0:T(4,128)S(1)}) custom-call(s32[8]{0:T(128)S(1)} %copy-done.1, bf16[224,128]{1,0:T(8,128)(2,1)S(1)} %get-tuple-element.52.refs_1_, bf16[224,128]{1,0:T(8,128)(2,1)S(1)} %collective-permute-done.30.refs_2_, bf16[224,128]{1,0:T(8,128)(2,1)S(1)} %collective-permute-done.31.refs_3_, ...), custom_call_target="tpu_custom_call" | custom-call | flops 16777216 | bytes 1048576 | tf_op jit(solution)/shard_map/pallas_call | solution.py:58
  79.8 1.5 %collective-permute-start.35 = (f32[64,64]{1,0:T(8,128)S(1)}, f32[64,64]{1,0:T(8,128)S(1)}, u32[]{:S(2)}, u32[]{:S(2)}) collective-permute-start(f32[64,64]{1,0:T(8,128)S(1)} %get-tuple-element.55.refs_0_), channel_id=1, source_target_pairs={{0,24},{8,0},{16,8},{24,16},{1,25},{9,1},{17,9},{25,17},{2,26},{10... | collective-permute-start | bytes 49160 | tf_op jit(solution)/shard_map/ppermute | solution.py:515
  82.0 1.3 %collective-permute-start.33 = (f32[64,64]{1,0:T(8,128)S(1)}, f32[64,64]{1,0:T(8,128)S(1)}, u32[]{:S(2)}, u32[]{:S(2)}) collective-permute-start(f32[64,64]{1,0:T(8,128)S(1)} %get-tuple-element.55.refs_0_), channel_id=1, source_target_pairs={{0,8},{8,16},{16,24},{24,0},{1,9},{9,17},{17,25},{25,1},{2,10},{10... | collective-permute-start | bytes 49160 | tf_op jit(solution)/shard_map/ppermute | solution.py:515
  83.7 2.7 %collective-permute-done.34.refs_2_ = f32[64,64]{1,0:T(8,128)S(1)} collective-permute-done((f32[64,64]{1,0:T(8,128)S(1)}, f32[64,64]{1,0:T(8,128)S(1)}, u32[]{:S(2)}, u32[]{:S(2)}) %collective-permute-start.34) | collective-permute-done | bytes 16416 | tf_op jit(solution)/shard_map/ppermute | solution.py:515
  86.4 1.3 %collective-permute-done.33.refs_1_ = f32[64,64]{1,0:T(8,128)S(1)} collective-permute-done((f32[64,64]{1,0:T(8,128)S(1)}, f32[64,64]{1,0:T(8,128)S(1)}, u32[]{:S(2)}, u32[]{:S(2)}) %collective-permute-start.33) | collective-permute-done | bytes 16416 | tf_op jit(solution)/shard_map/ppermute | solution.py:515
  87.7 3.2 %shard_map.93 = f32[64,512]{1,0:T(8,128)} custom-call(f32[64,64]{1,0:T(8,128)S(1)} %get-tuple-element.55.refs_0_, f32[64,64]{1,0:T(8,128)S(1)} %collective-permute-done.33.refs_1_, f32[64,64]{1,0:T(8,128)S(1)} %collective-permute-done.34.refs_2_, f32[64,64]{1,0:T(8,128)S(1)} %collective-permute-done.35.refs_3_, ...), custom_call_target="tpu_custom_call" | custom-call | flops 16777216 | bytes 1048576 | tf_op jit(solution)/shard_map/pallas_call | solution.py:58
  (61 shorter events, 13.1 us)
Async XLA Ops:
  2.2 8.7 %collective-permute-start.9 = (bf16[56,512]{1,0:T(8,128)(2,1)S(1)}, bf16[56,512]{1,0:T(8,128)(2,1)S(1)}, u32[]{:S(2)}, u32[]{:S(2)}) collective-permute-start(bf16[56,512]{1,0:T(8,128)(2,1)S(1)} %shard_map.85.refs_0_.pack), channel_id=1, source_target_pairs={{0,1},{1,0},{2,3},{3,2},{4,5},{5,4},{6,7},{7,6},{8,9},{9,8},{10,11... | collective-permute-start | bytes 172040 | tf_op jit(solution)/shard_map/ppermute | solution.py:510
  2.7 8.2 %collective-permute-start.7 = (bf16[56,512]{1,0:T(8,128)(2,1)S(1)}, bf16[56,512]{1,0:T(8,128)(2,1)S(1)}, u32[]{:S(2)}, u32[]{:S(2)}) collective-permute-start(bf16[56,512]{1,0:T(8,128)(2,1)S(1)} %shard_map.85.refs_0_.pack), channel_id=1, source_target_pairs={{0,6},{1,7},{2,0},{3,1},{4,2},{5,3},{6,4},{7,5},{8,14},{9,15},{10,... | collective-permute-start | bytes 172040 | tf_op jit(solution)/shard_map/ppermute | solution.py:524
  6.2 5.7 %collective-permute-start.5 = (bf16[56,512]{1,0:T(8,128)(2,1)S(1)}, bf16[56,512]{1,0:T(8,128)(2,1)S(1)}, u32[]{:S(2)}, u32[]{:S(2)}) collective-permute-start(bf16[56,512]{1,0:T(8,128)(2,1)S(1)} %shard_map.85.refs_0_.pack), channel_id=1, source_target_pairs={{0,4},{1,5},{2,6},{3,7},{4,0},{5,1},{6,2},{7,3},{8,12},{9,13},{10,... | collective-permute-start | bytes 172040 | tf_op jit(solution)/shard_map/ppermute | solution.py:524
  6.7 5.2 %collective-permute-start.3 = (bf16[56,512]{1,0:T(8,128)(2,1)S(1)}, bf16[56,512]{1,0:T(8,128)(2,1)S(1)}, u32[]{:S(2)}, u32[]{:S(2)}) collective-permute-start(bf16[56,512]{1,0:T(8,128)(2,1)S(1)} %shard_map.85.refs_0_.pack), channel_id=1, source_target_pairs={{0,2},{1,3},{2,4},{3,5},{4,6},{5,7},{6,0},{7,1},{8,10},{9,11},{10,... | collective-permute-start | bytes 172040 | tf_op jit(solution)/shard_map/ppermute | solution.py:524
  7.3 5.8 %collective-permute-start.2 = (bf16[56,512]{1,0:T(8,128)(2,1)S(1)}, bf16[56,512]{1,0:T(8,128)(2,1)S(1)}, u32[]{:S(2)}, u32[]{:S(2)}) collective-permute-start(bf16[56,512]{1,0:T(8,128)(2,1)S(1)} %shard_map.85.refs_0_.pack), channel_id=1, source_target_pairs={{0,24},{8,0},{16,8},{24,16},{1,25},{9,1},{17,9},{25,17},{2,26},{10... | collective-permute-start | bytes 172040 | tf_op jit(solution)/shard_map/ppermute | solution.py:515
  10.9 5.1 %collective-permute-start.1 = (bf16[56,512]{1,0:T(8,128)(2,1)S(1)}, bf16[56,512]{1,0:T(8,128)(2,1)S(1)}, u32[]{:S(2)}, u32[]{:S(2)}) collective-permute-start(bf16[56,512]{1,0:T(8,128)(2,1)S(1)} %shard_map.85.refs_0_.pack), channel_id=1, source_target_pairs={{0,16},{8,24},{16,0},{24,8},{1,17},{9,25},{17,1},{25,9},{2,18},{10... | collective-permute-start | bytes 172040 | tf_op jit(solution)/shard_map/ppermute | solution.py:515
  10.9 6.0 %collective-permute-start = (bf16[56,512]{1,0:T(8,128)(2,1)S(1)}, bf16[56,512]{1,0:T(8,128)(2,1)S(1)}, u32[]{:S(2)}, u32[]{:S(2)}) collective-permute-start(bf16[56,512]{1,0:T(8,128)(2,1)S(1)} %shard_map.85.refs_0_.pack), channel_id=1, source_target_pairs={{0,8},{8,16},{16,24},{24,0},{1,9},{9,17},{17,25},{25,1},{2,10},{10... | collective-permute-start | bytes 172040 | tf_op jit(solution)/shard_map/ppermute | solution.py:515
  11.9 5.0 %collective-permute-start.8 = (bf16[56,512]{1,0:T(8,128)(2,1)S(1)}, bf16[56,512]{1,0:T(8,128)(2,1)S(1)}, u32[]{:S(2)}, u32[]{:S(2)}) collective-permute-start(bf16[56,512]{1,0:T(8,128)(2,1)S(1)} %collective-permute-done.7.refs_13_), channel_id=1, source_target_pairs={{0,1},{1,0},{2,3},{3,2},{4,5},{5,4},{6,7},{7,6},{8,9},{9,8},{10,11... | collective-permute-start | bytes 172040 | tf_op jit(solution)/shard_map/ppermute | solution.py:510
  11.9 5.0 %collective-permute-start.6 = (bf16[56,512]{1,0:T(8,128)(2,1)S(1)}, bf16[56,512]{1,0:T(8,128)(2,1)S(1)}, u32[]{:S(2)}, u32[]{:S(2)}) collective-permute-start(bf16[56,512]{1,0:T(8,128)(2,1)S(1)} %collective-permute-done.5.refs_9_), channel_id=1, source_target_pairs={{0,1},{1,0},{2,3},{3,2},{4,5},{5,4},{6,7},{7,6},{8,9},{9,8},{10,11... | collective-permute-start | bytes 172040 | tf_op jit(solution)/shard_map/ppermute | solution.py:510
  13.1 3.9 %collective-permute-start.4 = (bf16[56,512]{1,0:T(8,128)(2,1)S(1)}, bf16[56,512]{1,0:T(8,128)(2,1)S(1)}, u32[]{:S(2)}, u32[]{:S(2)}) collective-permute-start(bf16[56,512]{1,0:T(8,128)(2,1)S(1)} %collective-permute-done.3.refs_5_), channel_id=1, source_target_pairs={{0,1},{1,0},{2,3},{3,2},{4,5},{5,4},{6,7},{7,6},{8,9},{9,8},{10,11... | collective-permute-start | bytes 172040 | tf_op jit(solution)/shard_map/ppermute | solution.py:510
  17.0 4.0 %collective-permute-start.10 = (bf16[3,56,512]{2,1,0:T(8,128)(2,1)S(1)}, bf16[3,56,512]{2,1,0:T(8,128)(2,1)S(1)}, u32[]{:S(2)}, u32[]{:S(2)}) collective-permute-start(bf16[3,56,512]{2,1,0:T(8,128)(2,1)S(1)} %get-tuple-element.33.rest), channel_id=1, source_target_pairs={{0,1},{1,0},{2,3},{3,2},{4,5},{5,4},{6,7},{7,6},{8,9},{9,8},{10,11... | collective-permute-start | bytes 516104 | tf_op jit(solution)/shard_map/ppermute | solution.py:510
  17.1 8.3 %collective-permute-start.13 = (bf16[3,56,512]{2,1,0:T(8,128)(2,1)S(1)}, bf16[3,56,512]{2,1,0:T(8,128)(2,1)S(1)}, u32[]{:S(2)}, u32[]{:S(2)}) collective-permute-start(bf16[3,56,512]{2,1,0:T(8,128)(2,1)S(1)} %get-tuple-element.33.rest), channel_id=1, source_target_pairs={{0,6},{1,7},{2,0},{3,1},{4,2},{5,3},{6,4},{7,5},{8,14},{9,15},{10,... | collective-permute-start | bytes 516104 | tf_op jit(solution)/shard_map/ppermute | solution.py:524
  19.5 10.1 %collective-permute-start.12 = (bf16[3,56,512]{2,1,0:T(8,128)(2,1)S(1)}, bf16[3,56,512]{2,1,0:T(8,128)(2,1)S(1)}, u32[]{:S(2)}, u32[]{:S(2)}) collective-permute-start(bf16[3,56,512]{2,1,0:T(8,128)(2,1)S(1)} %get-tuple-element.33.rest), channel_id=1, source_target_pairs={{0,4},{1,5},{2,6},{3,7},{4,0},{5,1},{6,2},{7,3},{8,12},{9,13},{10,... | collective-permute-start | bytes 516104 | tf_op jit(solution)/shard_map/ppermute | solution.py:524
  21.0 8.6 %collective-permute-start.11 = (bf16[3,56,512]{2,1,0:T(8,128)(2,1)S(1)}, bf16[3,56,512]{2,1,0:T(8,128)(2,1)S(1)}, u32[]{:S(2)}, u32[]{:S(2)}) collective-permute-start(bf16[3,56,512]{2,1,0:T(8,128)(2,1)S(1)} %get-tuple-element.33.rest), channel_id=1, source_target_pairs={{0,2},{1,3},{2,4},{3,5},{4,6},{5,7},{6,0},{7,1},{8,10},{9,11},{10,... | collective-permute-start | bytes 516104 | tf_op jit(solution)/shard_map/ppermute | solution.py:524
  38.1 4.6 %collective-permute-start.21 = (bf16[64,512]{1,0:T(8,128)(2,1)}, bf16[64,512]{1,0:T(8,128)(2,1)S(1)}, u32[]{:S(2)}, u32[]{:S(2)}) collective-permute-start(bf16[64,512]{1,0:T(8,128)(2,1)} %refs_8_), channel_id=1, source_target_pairs={{0,8},{8,0},{16,24},{24,16},{1,9},{9,1},{17,25},{25,17},{2,10},{10... | collective-permute-start | bytes 196616 | tf_op jit(solution)/shard_map/ppermute | solution.py:510
  39.1 4.0 %collective-permute-start.20 = (bf16[128,128]{1,0:T(8,128)(2,1)S(1)}, bf16[128,128]{1,0:T(8,128)(2,1)S(1)}, u32[]{:S(2)}, u32[]{:S(2)}) collective-permute-start(bf16[128,128]{1,0:T(8,128)(2,1)S(1)} %add_convert_fusion.1.refs_3_), channel_id=1, source_target_pairs={{0,6},{1,7},{2,0},{3,1},{4,2},{5,3},{6,4},{7,5},{8,14},{9,15},{10,... | collective-permute-start | bytes 98312 | tf_op jit(solution)/shard_map/ppermute | solution.py:524
  40.4 4.3 %collective-permute-start.19 = (bf16[128,128]{1,0:T(8,128)(2,1)S(1)}, bf16[128,128]{1,0:T(8,128)(2,1)S(1)}, u32[]{:S(2)}, u32[]{:S(2)}) collective-permute-start(bf16[128,128]{1,0:T(8,128)(2,1)S(1)} %add_convert_fusion.1.refs_3_), channel_id=1, source_target_pairs={{0,4},{1,5},{2,6},{3,7},{4,0},{5,1},{6,2},{7,3},{8,12},{9,13},{10,... | collective-permute-start | bytes 98312 | tf_op jit(solution)/shard_map/ppermute | solution.py:524
  40.9 4.8 %collective-permute-start.18 = (bf16[128,128]{1,0:T(8,128)(2,1)S(1)}, bf16[128,128]{1,0:T(8,128)(2,1)S(1)}, u32[]{:S(2)}, u32[]{:S(2)}) collective-permute-start(bf16[128,128]{1,0:T(8,128)(2,1)S(1)} %add_convert_fusion.1.refs_3_), channel_id=1, source_target_pairs={{0,2},{1,3},{2,4},{3,5},{4,6},{5,7},{6,0},{7,1},{8,10},{9,11},{10,... | collective-permute-start | bytes 98312 | tf_op jit(solution)/shard_map/ppermute | solution.py:524
  52.3 8.7 %collective-permute-start.26 = (bf16[64,512]{1,0:T(8,128)(2,1)S(1)}, bf16[64,512]{1,0:T(8,128)(2,1)S(1)}, u32[]{:S(2)}, u32[]{:S(2)}) collective-permute-start(bf16[64,512]{1,0:T(8,128)(2,1)S(1)} %copy-done), channel_id=1, source_target_pairs={{0,16},{8,24},{16,0},{24,8},{1,17},{9,25},{17,1},{25,9},{2,18},{10... | collective-permute-start | bytes 196616 | tf_op jit(solution)/shard_map/ppermute | solution.py:510
  53.8 8.2 %collective-permute-start.27 = (bf16[64,512]{1,0:T(8,128)(2,1)S(1)}, bf16[64,512]{1,0:T(8,128)(2,1)S(1)}, u32[]{:S(2)}, u32[]{:S(2)}) collective-permute-start(bf16[64,512]{1,0:T(8,128)(2,1)S(1)} %collective-permute-done.21.refs_7_.refs_9_), channel_id=1, source_target_pairs={{0,16},{8,24},{16,0},{24,8},{1,17},{9,25},{17,1},{25,9},{2,18},{10... | collective-permute-start | bytes 196616 | tf_op jit(solution)/shard_map/ppermute | solution.py:510
  55.3 6.6 %collective-permute-start.25 = (bf16[128,128]{1,0:T(8,128)(2,1)S(1)}, bf16[128,128]{1,0:T(8,128)(2,1)S(1)}, u32[]{:S(2)}, u32[]{:S(2)}) collective-permute-start(bf16[128,128]{1,0:T(8,128)(2,1)S(1)} %add_convert_fusion.refs_4_), channel_id=1, source_target_pairs={{0,6},{1,7},{2,0},{3,1},{4,2},{5,3},{6,4},{7,5},{8,14},{9,15},{10,... | collective-permute-start | bytes 98312 | tf_op jit(solution)/shard_map/ppermute | solution.py:524
  56.2 5.7 %collective-permute-start.24 = (bf16[128,128]{1,0:T(8,128)(2,1)S(1)}, bf16[128,128]{1,0:T(8,128)(2,1)S(1)}, u32[]{:S(2)}, u32[]{:S(2)}) collective-permute-start(bf16[128,128]{1,0:T(8,128)(2,1)S(1)} %add_convert_fusion.refs_4_), channel_id=1, source_target_pairs={{0,4},{1,5},{2,6},{3,7},{4,0},{5,1},{6,2},{7,3},{8,12},{9,13},{10,... | collective-permute-start | bytes 98312 | tf_op jit(solution)/shard_map/ppermute | solution.py:524
  57.6 4.8 %collective-permute-start.23 = (bf16[128,128]{1,0:T(8,128)(2,1)S(1)}, bf16[128,128]{1,0:T(8,128)(2,1)S(1)}, u32[]{:S(2)}, u32[]{:S(2)}) collective-permute-start(bf16[128,128]{1,0:T(8,128)(2,1)S(1)} %add_convert_fusion.refs_4_), channel_id=1, source_target_pairs={{0,2},{1,3},{2,4},{3,5},{4,6},{5,7},{6,0},{7,1},{8,10},{9,11},{10,... | collective-permute-start | bytes 98312 | tf_op jit(solution)/shard_map/ppermute | solution.py:524
  70.7 4.7 %collective-permute-start.32 = (bf16[224,128]{1,0:T(8,128)(2,1)S(1)}, bf16[224,128]{1,0:T(8,128)(2,1)S(1)}, u32[]{:S(2)}, u32[]{:S(2)}) collective-permute-start(bf16[224,128]{1,0:T(8,128)(2,1)S(1)} %get-tuple-element.52.refs_1_), channel_id=1, source_target_pairs={{0,6},{1,7},{2,0},{3,1},{4,2},{5,3},{6,4},{7,5},{8,14},{9,15},{10,... | collective-permute-start | bytes 172040 | tf_op jit(solution)/shard_map/ppermute | solution.py:524
  70.8 11.2 %collective-permute-start.36 = (bf16[256,128]{1,0:T(8,128)(2,1)S(1)}, bf16[256,128]{1,0:T(8,128)(2,1)S(1)}, u32[]{:S(2)}, u32[]{:S(2)}) collective-permute-start(bf16[256,128]{1,0:T(8,128)(2,1)S(1)} %get-tuple-element.57), channel_id=1, source_target_pairs={{0,2},{1,3},{2,4},{3,5},{4,6},{5,7},{6,0},{7,1},{8,10},{9,11},{10,... | collective-permute-start | bytes 196616 | tf_op jit(solution)/shard_map/ppermute | solution.py:524
  72.8 5.7 %collective-permute-start.31 = (bf16[224,128]{1,0:T(8,128)(2,1)S(1)}, bf16[224,128]{1,0:T(8,128)(2,1)S(1)}, u32[]{:S(2)}, u32[]{:S(2)}) collective-permute-start(bf16[224,128]{1,0:T(8,128)(2,1)S(1)} %get-tuple-element.52.refs_1_), channel_id=1, source_target_pairs={{0,4},{1,5},{2,6},{3,7},{4,0},{5,1},{6,2},{7,3},{8,12},{9,13},{10,... | collective-permute-start | bytes 172040 | tf_op jit(solution)/shard_map/ppermute | solution.py:524
  72.8 5.7 %collective-permute-start.30 = (bf16[224,128]{1,0:T(8,128)(2,1)S(1)}, bf16[224,128]{1,0:T(8,128)(2,1)S(1)}, u32[]{:S(2)}, u32[]{:S(2)}) collective-permute-start(bf16[224,128]{1,0:T(8,128)(2,1)S(1)} %get-tuple-element.52.refs_1_), channel_id=1, source_target_pairs={{0,2},{1,3},{2,4},{3,5},{4,6},{5,7},{6,0},{7,1},{8,10},{9,11},{10,... | collective-permute-start | bytes 172040 | tf_op jit(solution)/shard_map/ppermute | solution.py:524
  74.3 9.0 %collective-permute-start.37 = (bf16[256,128]{1,0:T(8,128)(2,1)S(1)}, bf16[256,128]{1,0:T(8,128)(2,1)S(1)}, u32[]{:S(2)}, u32[]{:S(2)}) collective-permute-start(bf16[256,128]{1,0:T(8,128)(2,1)S(1)} %get-tuple-element.58), channel_id=1, source_target_pairs={{0,4},{1,5},{2,6},{3,7},{4,0},{5,1},{6,2},{7,3},{8,12},{9,13},{10,... | collective-permute-start | bytes 196616 | tf_op jit(solution)/shard_map/ppermute | solution.py:524
  75.4 7.9 %collective-permute-start.38 = (bf16[256,128]{1,0:T(8,128)(2,1)S(1)}, bf16[256,128]{1,0:T(8,128)(2,1)S(1)}, u32[]{:S(2)}, u32[]{:S(2)}) collective-permute-start(bf16[256,128]{1,0:T(8,128)(2,1)S(1)} %get-tuple-element.59), channel_id=1, source_target_pairs={{0,6},{1,7},{2,0},{3,1},{4,2},{5,3},{6,4},{7,5},{8,14},{9,15},{10,... | collective-permute-start | bytes 196616 | tf_op jit(solution)/shard_map/ppermute | solution.py:524
  79.8 3.9 %collective-permute-start.35 = (f32[64,64]{1,0:T(8,128)S(1)}, f32[64,64]{1,0:T(8,128)S(1)}, u32[]{:S(2)}, u32[]{:S(2)}) collective-permute-start(f32[64,64]{1,0:T(8,128)S(1)} %get-tuple-element.55.refs_0_), channel_id=1, source_target_pairs={{0,24},{8,0},{16,8},{24,16},{1,25},{9,1},{17,9},{25,17},{2,26},{10... | collective-permute-start | bytes 49160 | tf_op jit(solution)/shard_map/ppermute | solution.py:515
  81.2 5.2 %collective-permute-start.34 = (f32[64,64]{1,0:T(8,128)S(1)}, f32[64,64]{1,0:T(8,128)S(1)}, u32[]{:S(2)}, u32[]{:S(2)}) collective-permute-start(f32[64,64]{1,0:T(8,128)S(1)} %get-tuple-element.55.refs_0_), channel_id=1, source_target_pairs={{0,16},{8,24},{16,0},{24,8},{1,17},{9,25},{17,1},{25,9},{2,18},{10... | collective-permute-start | bytes 49160 | tf_op jit(solution)/shard_map/ppermute | solution.py:515
  82.0 5.7 %collective-permute-start.33 = (f32[64,64]{1,0:T(8,128)S(1)}, f32[64,64]{1,0:T(8,128)S(1)}, u32[]{:S(2)}, u32[]{:S(2)}) collective-permute-start(f32[64,64]{1,0:T(8,128)S(1)} %get-tuple-element.55.refs_0_), channel_id=1, source_target_pairs={{0,8},{8,16},{16,24},{24,0},{1,9},{9,17},{17,25},{25,1},{2,10},{10... | collective-permute-start | bytes 49160 | tf_op jit(solution)/shard_map/ppermute | solution.py:515
  (9 other events, 107.7 us)
